TPU v7x, 32 devices: a whole 2x2x4 slice. The times are simulated.
32 devices in a mesh: row: 8 (over y, x, core), col: 4 (over z).
Axes of the slice: x: 2, y: 2, z: 4, core: 2. Of those that a mesh axis runs over, the one named last changes fastest.
Arguments:
- rhs: bfloat16 [5, 8, 32, 256], P(None, 'row'), may hold values from -6 to 6
- factor: bfloat16 [10, 8, 8, 256, 256], P(None, 'col', 'row'), may hold values from -0.125 to 0.125
- pattern: int32 [10, 8, 8], P(None, 'col', 'row'), may hold values 0 or 1
- diag_inverse: bfloat16 [5, 8, 256, 256], P(None, 'row'), as said below
Outputs:
- forward: bfloat16 [5, 8, 32, 256], P(None, 'row')
- solution: bfloat16 [5, 8, 32, 256], P(None, 'row')
Inputs may be any that keep to these rules, and one draw needn't show every extreme that they name: Each block of diag_inverse is lower triangular with a positive diagonal.
All inputs are finite; a program needn't handle non-finite values. No bound on the sum of `pattern` on one device may be relied on, other than what follows from the above.
Results may differ from a plain program's by a relative error of at most 0.028.
Values may be sent and summed in bfloat16 or wider, within the bound.
No kernel may reach another device: no remote copies, remote signals or barrier semaphores. Data moves between devices by JAX's collectives and lax.ppermute only.
A program may use at most 64 MiB of HBM per device.

v0:
```python
import jax
import jax.numpy as jnp
from jax import lax
from jax.sharding import PartitionSpec as P


def spread_2(array, axis, root):
    mine = lax.axis_index(axis) == root
    return lax.psum(jnp.where(mine, array, jnp.zeros_like(array)), axis)


def pair_index(later, earlier):
    return later * (later - 1) // 2 + earlier


def lower_term(blocks, mask_blocks, solved):
    prod = jnp.einsum("tsij,srj->tsri", blocks, solved, preferred_element_type=jnp.float32)
    return jnp.sum(prod * mask_blocks.astype(jnp.float32)[:, :, None, None], axis=1)


def upper_term(blocks, mask_blocks, solved_rows):
    prod = jnp.einsum("tri,tsij->tsrj", solved_rows, blocks, preferred_element_type=jnp.float32)
    return jnp.sum(prod * mask_blocks.astype(jnp.float32)[:, :, None, None], axis=0)


def solve_lower(zeta, inverse):
    return jnp.einsum("mrj,mij->mri", zeta, inverse, preferred_element_type=jnp.float32).astype(
        jnp.bfloat16
    )


def solve_upper(zeta, inverse):
    return jnp.einsum("mri,mij->mrj", zeta, inverse, preferred_element_type=jnp.float32).astype(
        jnp.bfloat16
    )


def on_device(rhs, factor, pattern, diag_inverse):
    levels = rhs.shape[0]
    own = rhs.shape[1]
    block_rows = factor.shape[1]
    ratio = lax.axis_size("row") // lax.axis_size("col")
    row_id = lax.axis_index("row")
    col_id = lax.axis_index("col")

    def fterm(later, earlier, solved):
        index = pair_index(later, earlier)
        return lower_term(factor[index], pattern[index], solved)

    forward_list = [solve_lower(rhs[0], diag_inverse[0])]
    for level in range(1, levels):
        partial_value = fterm(level, 0, forward_list[0])
        for earlier in range(1, level):
            partial_value = partial_value + fterm(level, earlier, forward_list[earlier])
        finish_total = lax.psum(partial_value.astype(jnp.bfloat16), "row").astype(jnp.float32)
        offset = row_id % ratio * own
        mine = lax.dynamic_slice_in_dim(finish_total, offset, own, 0)
        arrived = spread_2(mine.astype(jnp.bfloat16), "col", row_id // ratio).astype(mine.dtype)
        finish_zeta = (rhs[level].astype(jnp.float32) - arrived).astype(jnp.bfloat16)
        forward_list.append(solve_lower(finish_zeta, diag_inverse[level]))

    def spread(solved):
        whole = lax.all_gather(solved, "row", axis=0, tiled=True)
        return lax.dynamic_slice_in_dim(whole, col_id * block_rows, block_rows, 0)

    def bterm(later, earlier, spread_rows):
        index = pair_index(later, earlier)
        return upper_term(factor[index], pattern[index], spread_rows)

    back_list = [None] * levels
    spread_list = [None] * levels
    back_list[levels - 1] = solve_upper(forward_list[levels - 1], diag_inverse[levels - 1])
    spread_list[levels - 1] = spread(back_list[levels - 1])
    for level in range(levels - 2, -1, -1):
        partial_value = bterm(levels - 1, level, spread_list[levels - 1])
        for later in range(levels - 2, level, -1):
            partial_value = partial_value + bterm(later, level, spread_list[later])
        total = lax.psum(partial_value.astype(jnp.bfloat16), "col").astype(jnp.float32)
        zeta = (forward_list[level].astype(jnp.float32) - total).astype(jnp.bfloat16)
        back_list[level] = solve_upper(zeta, diag_inverse[level])
        if level > 0:
            spread_list[level] = spread(back_list[level])
    return (jnp.stack(forward_list), jnp.stack(back_list))


def solution(mesh):
    return jax.shard_map(
        on_device,
        mesh=mesh,
        in_specs=(
            P(None, "row", None, None),
            P(None, "col", "row", None, None),
            P(None, "col", "row"),
            P(None, "row", None, None),
        ),
        out_specs=(P(None, "row", None, None), P(None, "row", None, None)),
        check_vma=False,
    )
```

profile of v0, /device:TPU:0, one launch (start us, length us, event | category | flops | bytes accessed | tf_op | source)
XLA Modules:
  0.0 284.5 jit_solution(11243879152641821446)
XLA Ops:
  0.7 1.7 convert_reduce_fusion.3
  2.4 1.7 constant_dynamic-update-slice_fusion.4
  4.2 1.1 fusion.40
  5.3 25.5 %psum.84 = bf16[2,32,256]{2,1,0:T(8,128)(2,1)S(1)} all-reduce(bf16[2,32,256]{2,1,0:T(8,128)(2,1)S(1)} %fusion.40), channel_id=1, replica_groups=mesh['row'=8,'col'=4] {'row'}, use_global_device_ids=true, to_apply=%region_0.0 | all-reduce | flops 16384 | bytes 65536 | tf_op jit(solution)/shard_map/psum | solution.py:55
  30.8 19.0 %psum.85 = bf16[1,32,256]{2,1,0:T(8,128)(2,1)S(1)} all-reduce(bf16[1,32,256]{2,1,0:T(8,128)(2,1)S(1)} %fusion.84), channel_id=1, replica_groups=mesh['row'=8,'col'=4] {'col'}, use_global_device_ids=true, to_apply=%region_1.0 | all-reduce | flops 8192 | bytes 32768 | tf_op jit(solution)/shard_map/psum | solution.py:9
  49.8 1.7 constant_dynamic-update-slice_fusion.3
  51.6 1.1 fusion.12
  52.7 1.1 fusion.17
  53.8 1.1 fusion.41
  55.0 22.4 %psum.86 = bf16[2,32,256]{2,1,0:T(8,128)(2,1)S(1)} all-reduce(bf16[2,32,256]{2,1,0:T(8,128)(2,1)S(1)} %fusion.41), channel_id=1, replica_groups=mesh['row'=8,'col'=4] {'row'}, use_global_device_ids=true, to_apply=%region_2.3 | all-reduce | flops 16384 | bytes 65536 | tf_op jit(solution)/shard_map/psum | solution.py:55
  77.4 15.5 %psum.87 = bf16[1,32,256]{2,1,0:T(8,128)(2,1)S(1)} all-reduce(bf16[1,32,256]{2,1,0:T(8,128)(2,1)S(1)} %fusion.85), channel_id=1, replica_groups=mesh['row'=8,'col'=4] {'col'}, use_global_device_ids=true, to_apply=%region_3.4 | all-reduce | flops 8192 | bytes 32768 | tf_op jit(solution)/shard_map/psum | solution.py:9
  92.9 1.7 constant_dynamic-update-slice_fusion.2
  94.6 1.1 fusion.14
  96.3 22.4 %psum.88 = bf16[2,32,256]{2,1,0:T(8,128)(2,1)S(1)} all-reduce(bf16[2,32,256]{2,1,0:T(8,128)(2,1)S(1)} %fusion.42), channel_id=1, replica_groups=mesh['row'=8,'col'=4] {'row'}, use_global_device_ids=true, to_apply=%region_4.5 | all-reduce | flops 16384 | bytes 65536 | tf_op jit(solution)/shard_map/psum | solution.py:55
  118.7 16.3 %psum.89 = bf16[1,32,256]{2,1,0:T(8,128)(2,1)S(1)} all-reduce(bf16[1,32,256]{2,1,0:T(8,128)(2,1)S(1)} %fusion.86), channel_id=1, replica_groups=mesh['row'=8,'col'=4] {'col'}, use_global_device_ids=true, to_apply=%region_5.6 | all-reduce | flops 8192 | bytes 32768 | tf_op jit(solution)/shard_map/psum | solution.py:9
  135.0 1.5 constant_dynamic-update-slice_fusion.1
  136.6 0.8 fusion.10
  137.6 22.4 %psum.90 = bf16[2,32,256]{2,1,0:T(8,128)(2,1)S(1)} all-reduce(bf16[2,32,256]{2,1,0:T(8,128)(2,1)S(1)} %fusion.43), channel_id=1, replica_groups=mesh['row'=8,'col'=4] {'row'}, use_global_device_ids=true, to_apply=%region_6.7 | all-reduce | flops 16384 | bytes 65536 | tf_op jit(solution)/shard_map/psum | solution.py:55
  160.0 15.5 %psum.91 = bf16[1,32,256]{2,1,0:T(8,128)(2,1)S(1)} all-reduce(bf16[1,32,256]{2,1,0:T(8,128)(2,1)S(1)} %fusion.87), channel_id=1, replica_groups=mesh['row'=8,'col'=4] {'col'}, use_global_device_ids=true, to_apply=%region_7.8 | all-reduce | flops 8192 | bytes 32768 | tf_op jit(solution)/shard_map/psum | solution.py:9
  175.5 1.5 constant_dynamic-update-slice_fusion
  177.1 8.2 %all-gather = bf16[256,256]{1,0:T(8,128)(2,1)S(1)} all-gather(bf16[32,256]{1,0:T(8,128)(2,1)S(1)} %convolution_convert_fusion.4), channel_id=2, replica_groups=mesh['row'=8,'col'=4] {'row'}, dimensions={0}, use_global_device_ids=true | all-gather | bytes 147456 | tf_op jit(solution)/shard_map/all_gather | solution.py:63
  185.4 0.8 fusion.28
  186.2 16.3 %psum.92 = bf16[1,32,256]{2,1,0:T(8,128)(2,1)S(1)} all-reduce(bf16[1,32,256]{2,1,0:T(8,128)(2,1)S(1)} %bitcast.440), channel_id=1, replica_groups=mesh['row'=8,'col'=4] {'col'}, use_global_device_ids=true, to_apply=%region_10.11 | all-reduce | flops 8192 | bytes 32768 | tf_op jit(solution)/shard_map/psum | solution.py:78
  203.7 9.2 %all-gather.1 = bf16[256,256]{1,0:T(8,128)(2,1)S(1)} all-gather(bf16[32,256]{1,0:T(8,128)(2,1)S(1)} %convolution_convert_fusion.3), channel_id=3, replica_groups=mesh['row'=8,'col'=4] {'row'}, dimensions={0}, use_global_device_ids=true | all-gather | bytes 147456 | tf_op jit(solution)/shard_map/all_gather | solution.py:63
  213.1 15.5 %psum.93 = bf16[1,32,256]{2,1,0:T(8,128)(2,1)S(1)} all-reduce(bf16[1,32,256]{2,1,0:T(8,128)(2,1)S(1)} %fusion.88), channel_id=1, replica_groups=mesh['row'=8,'col'=4] {'col'}, use_global_device_ids=true, to_apply=%region_14.15 | all-reduce | flops 8192 | bytes 32768 | tf_op jit(solution)/shard_map/psum | solution.py:78
  228.8 0.8 fusion.34
  229.6 1.4 fusion.29
  231.0 8.2 %all-gather.2 = bf16[256,256]{1,0:T(8,128)(2,1)S(1)} all-gather(bf16[32,256]{1,0:T(8,128)(2,1)S(1)} %convolution_convert_fusion.2), channel_id=4, replica_groups=mesh['row'=8,'col'=4] {'row'}, dimensions={0}, use_global_device_ids=true | all-gather | bytes 147456 | tf_op jit(solution)/shard_map/all_gather | solution.py:63
  239.2 0.8 fusion.35
  240.9 16.3 %psum.94 = bf16[1,32,256]{2,1,0:T(8,128)(2,1)S(1)} all-reduce(bf16[1,32,256]{2,1,0:T(8,128)(2,1)S(1)} %fusion.89), channel_id=1, replica_groups=mesh['row'=8,'col'=4] {'col'}, use_global_device_ids=true, to_apply=%region_19.20 | all-reduce | flops 8192 | bytes 32768 | tf_op jit(solution)/shard_map/psum | solution.py:78
  257.3 9.2 %all-gather.3 = bf16[256,256]{1,0:T(8,128)(2,1)S(1)} all-gather(bf16[32,256]{1,0:T(8,128)(2,1)S(1)} %convolution_convert_fusion.1), channel_id=5, replica_groups=mesh['row'=8,'col'=4] {'row'}, dimensions={0}, use_global_device_ids=true | all-gather | bytes 147456 | tf_op jit(solution)/shard_map/all_gather | solution.py:63
  268.1 15.6 %psum.95 = bf16[1,32,256]{2,1,0:T(8,128)(2,1)S(1)} all-reduce(bf16[1,32,256]{2,1,0:T(8,128)(2,1)S(1)} %fusion.90), channel_id=1, replica_groups=mesh['row'=8,'col'=4] {'col'}, use_global_device_ids=true, to_apply=%region_21.22 | all-reduce | flops 8192 | bytes 32768 | tf_op jit(solution)/shard_map/psum | solution.py:78
  (42 shorter events, 5.7 us)
Async XLA Ops:
  0.6 95.1 %copy-start = (bf16[10,2,1,256,256]{4,3,2,1,0:T(8,128)(2,1)S(1)}, bf16[10,2,1,256,256]{4,3,2,1,0:T(8,128)(2,1)}, u32[]{:S(2)}) copy-start(bf16[10,2,1,256,256]{4,3,2,1,0:T(8,128)(2,1)} %param.5) | copy-start | bytes 7864324
  0.6 134.4 %copy-start.1 = (bf16[5,1,256,256]{3,2,1,0:T(8,128)(2,1)S(1)}, bf16[5,1,256,256]{3,2,1,0:T(8,128)(2,1)}, u32[]{:S(2)}) copy-start(bf16[5,1,256,256]{3,2,1,0:T(8,128)(2,1)} %param.7) | copy-start | bytes 1966084
  2.4 1.7 copy-start.2
  2.4 50.3 %copy-start.4 = (f32[2]{0:T(128)}, f32[2]{0:T(128)S(1)}, u32[]{:S(2)}) copy-start(f32[2]{0:T(128)S(1)} %get-tuple-element.7) | copy-start | bytes 28
  2.4 51.4 %copy-start.3 = (f32[2]{0:T(128)}, f32[2]{0:T(128)S(1)}, u32[]{:S(2)}) copy-start(f32[2]{0:T(128)S(1)} %get-tuple-element.8) | copy-start | bytes 28
  2.4 93.5 %copy-start.5 = (f32[2]{0:T(128)}, f32[2]{0:T(128)S(1)}, u32[]{:S(2)}) copy-start(f32[2]{0:T(128)S(1)} %get-tuple-element.5) | copy-start | bytes 28
  2.4 93.7 %copy-start.6 = (f32[2]{0:T(128)}, f32[2]{0:T(128)S(1)}, u32[]{:S(2)}) copy-start(f32[2]{0:T(128)S(1)} %get-tuple-element.6) | copy-start | bytes 28
  283.8 0.6 copy-start.7
where the time goes:
time: 286 us; the launch traced here: 284 us
  blocking collectives  258 us (90%)
  matrix products  22.6 us (8%)
    psum x4, blocking collectives, on_device(): lax.psum(partial_value.astype(jnp.bfloat16), 'row').astype(jnp.float32)  92.6 us
    psum x4, blocking collectives, spread_2(): return lax.psum(jnp.where(mine, array, jnp.zeros_like(array)), axis)  66.4 us
    psum x4, blocking collectives, on_device(): lax.psum(partial_value.astype(jnp.bfloat16), 'col').astype(jnp.float32)  63.7 us
    all_gather x4, blocking collectives, spread(): whole = lax.all_gather(solved, 'row', axis=0, tiled=True)  34.9 us
    dot_general x5, matrix products, solve_lower(): jnp.einsum('mrj,mij->mri', zeta, inverse, preferred_element_type=jnp.floa...  8.15 us
    dot_general x10, matrix products, lower_term(): jnp.einsum('tsij,srj->tsri', blocks, solved, preferred_element_type=jnp.f...  7.19 us
    dot_general x10, matrix products, upper_term(): jnp.einsum('tri,tsij->tsrj', solved_rows, blocks, preferred_element_type=...  6.54 us

commit v1 on v0

v1 whole, which is shorter than its diff:
```python
import functools

import jax
import jax.numpy as jnp
from jax import lax
from jax.experimental import pallas as pl
from jax.experimental.pallas import tpu as pltpu
from jax.sharding import PartitionSpec as P

BOTH = ("row", "col")
NT = (((1,), (1,)), ((), ()))
NN = (((1,), (0,)), ((), ()))


def pair_index(later, earlier):
    return later * (later - 1) // 2 + earlier


def parity(q):
    return bin(q).count("1") & 1


def turn(q, z):
    return parity(q) ^ (z & 1)


def perm(n, target):
    pairs = []
    for q in range(n):
        for k in range(2):
            for z in range(n):
                to = target(q, k, z)
                if to == (q, k, z):
                    to = (q, k ^ 1, z)
                pairs.append(((2 * q + k) * n + z, (2 * to[0] + to[1]) * n + to[2]))
    return pairs


def plane_perms(n):
    return [perm(n, lambda q, k, z, m=m: (q ^ m, k ^ parity(m), z)) for m in range(1, n)]


def line_perms(n):
    return [perm(n, lambda q, k, z, m=m: (q, k ^ (m & 1), z ^ m)) for m in range(1, n)]


def chip_perm(n, chip):
    def target(q, k, z):
        a, b = chip(q, z)
        return a, k ^ turn(q, z) ^ turn(a, b), b

    return perm(n, target)


def down_perms(n):
    return [chip_perm(n, lambda q, z, j=j: (z, (q + j) % n)) for j in range(n)]


def up_perms(n):
    return [chip_perm(n, lambda q, z, j=j: ((z + j) % n, q)) for j in range(n)]


def turn_perm(n):
    return chip_perm(n, lambda q, z: (z, q))


def core_perm(n):
    return perm(n, lambda q, k, z: (q, k ^ 1, z))


def tree(parts):
    while len(parts) > 1:
        half = len(parts) // 2
        parts = [parts[i] + parts[i + half] for i in range(half)]
    return parts[0]


def f32(x):
    return x.astype(jnp.float32)


def bf16(x):
    return x.astype(jnp.bfloat16)


def dot(a, b, dims):
    return lax.dot_general(a, b, dims, preferred_element_type=jnp.float32)


def total_direct(info, own, got):
    first = jnp.where(info[1] == 1, f32(own[...]), f32(got[0][...]))
    return tree([first] + [f32(g[...]) for g in got[1:]])


def total_swap(own, got):
    return tree([f32(own[...])] + [f32(g[...]) for g in got])


def lower_part(info, pairs, solved, mine, other, mask, mask_other):
    k = info[0]
    outs = []
    for t in range(2):
        acc = None
        for p, y in zip(pairs, solved, strict=True):
            a = dot(y[k], mine[p, t], NT) * f32(mask[p, t])
            b = dot(y[1 - k], other[p, t], NT) * f32(mask_other[p, t])
            acc = a + b if acc is None else acc + (a + b)
        outs.append(acc)
    return outs


def upper_part(info, pairs, solved, mine, other, mask, mask_other):
    outs = []
    for blocks, m in ((mine, mask), (other, mask_other)):
        acc = None
        for p, x in zip(pairs, solved, strict=True):
            for t in range(2):
                a = dot(x[t], blocks[p, t], NN) * f32(m[p, t])
                acc = a if acc is None else acc + a
        outs.append(acc)
    return outs


def start_kernel(pairs, info, mask, mask_other, rhs, rhs_other, inv, inv_other, mine, other, y_ref, msg_ref):
    k = info[0]
    rows = pl.ds(pl.multiple_of(info[2] * 16, 16), 16)
    y_ref[k] = bf16(dot(rhs[0, rows, :], inv[0], NT))
    y_ref[1 - k] = bf16(dot(rhs_other[0, rows, :], inv_other[0], NT))
    for t, part in enumerate(lower_part(info, pairs, [y_ref], mine, other, mask, mask_other)):
        msg_ref[t] = bf16(part)


def down_kernel(level, n, pairs, *refs):
    info, mask, mask_other, rhs, rhs_other, inv, inv_other, mine, other, own = refs[:10]
    got, earlier = refs[10 : 10 + n], refs[10 + n : 10 + n + level]
    y_ref, msg_ref, total_ref = refs[10 + n + level :]
    k = info[0]
    rows = pl.ds(pl.multiple_of(info[2] * 16, 16), 16)
    total_ref[...] = total_direct(info, own, got)
    y_ref[k] = bf16(dot(bf16(f32(rhs[level, rows, :]) - total_ref[k]), inv[level], NT))
    y_ref[1 - k] = bf16(dot(bf16(f32(rhs_other[level, rows, :]) - total_ref[1 - k]), inv_other[level], NT))
    parts = lower_part(info, pairs, list(earlier) + [y_ref], mine, other, mask, mask_other)
    if level == 3:
        total_ref[k] = f32(rhs[level + 1, rows, :])
        total_ref[1 - k] = f32(rhs_other[level + 1, rows, :])
        parts = [jnp.where(info[1] == 1, p - total_ref[t], p) for t, p in enumerate(parts)]
    for t, part in enumerate(parts):
        msg_ref[t] = bf16(part)


def turn_kernel(n, pairs, *refs):
    info, mask, mask_other, inv, inv_other, mine, other, y3, own = refs[:9]
    got = refs[9 : 9 + n - 1]
    y_ref, x_ref, msg_ref = refs[9 + n - 1 :]
    k = info[0]
    zeta = bf16(-total_swap(own, got))
    x_ref[...] = zeta
    zk, zo = x_ref[k], x_ref[1 - k]
    y_ref[k] = bf16(dot(zk, inv[3], NT))
    y_ref[1 - k] = bf16(dot(zo, inv_other[3], NT))
    x_ref[k] = bf16(dot(y_ref[k], inv[3], NN))
    x_ref[1 - k] = bf16(dot(y_ref[1 - k], inv_other[3], NN))
    parts = upper_part(info, pairs, [x_ref], mine, other, mask, mask_other)
    for i, part in enumerate(parts):
        at = k if i == 0 else 1 - k
        msg_ref[at] = bf16(jnp.where(info[1] == 1, part - f32(y3[at]), part))


def up_kernel(level, n, pairs, *refs):
    info, mask, mask_other, inv, inv_other, mine, other, below, own = refs[:9]
    got, later = refs[9 : 9 + n], refs[9 + n : 9 + n + 4 - level]
    x_ref, msg_ref = refs[9 + n + 4 - level :]
    k = info[0]
    x_ref[...] = bf16(-total_direct(info, own, got))
    zk, zo = x_ref[k], x_ref[1 - k]
    x_ref[k] = bf16(dot(zk, inv[level - 1], NN))
    x_ref[1 - k] = bf16(dot(zo, inv_other[level - 1], NN))
    parts = upper_part(info, pairs, list(later) + [x_ref], mine, other, mask, mask_other)
    for i, part in enumerate(parts):
        at = k if i == 0 else 1 - k
        if level > 1:
            part = jnp.where(info[1] == 1, part - f32(below[at]), part)
        msg_ref[at] = bf16(part)


def last_kernel(n, *refs):
    info, inv, inv_other, y0, own = refs[:5]
    got = refs[5 : 5 + n - 1]
    x_ref, total_ref = refs[5 + n - 1 :]
    k = info[0]
    total_ref[...] = f32(y0[...]) - total_swap(own, got)
    x_ref[k] = bf16(dot(bf16(total_ref[k]), inv[0], NN))
    x_ref[1 - k] = bf16(dot(bf16(total_ref[1 - k]), inv_other[0], NN))


def call(body, outs, smem, vmem, scratch=()):
    return pl.pallas_call(
        body,
        out_shape=[jax.ShapeDtypeStruct(s, jnp.bfloat16) for s in outs],
        in_specs=[pl.BlockSpec(memory_space=pltpu.SMEM)] * len(smem)
        + [pl.BlockSpec(memory_space=pltpu.VMEM)] * len(vmem),
        out_specs=[pl.BlockSpec(memory_space=pltpu.VMEM)] * len(outs),
        scratch_shapes=[pltpu.VMEM(s, jnp.float32) for s in scratch],
        compiler_params=pltpu.CompilerParams(vmem_limit_bytes=40 * 1024 * 1024),
    )(*smem, *vmem)


def on_device(rhs, factor, pattern, diag_inverse):
    n = lax.axis_size("col")
    levels, own, count, width = rhs.shape
    assert levels == 5 and own == 1 and factor.shape[1] == 2 and lax.axis_size("row") == 2 * n
    row, z = lax.axis_index("row"), lax.axis_index("col")
    q, k = row // 2, row % 2
    bits = max(1, (n - 1).bit_length())
    odd = functools.reduce(jnp.bitwise_xor, [(q >> i) & 1 for i in range(bits)])
    half = k ^ odd ^ (z & 1)
    info = jnp.stack([k, (q == z).astype(jnp.int32), half]).astype(jnp.int32)

    rhs, inv = rhs[:, 0], diag_inverse[:, 0]
    mine, mask = factor[:, :, 0], pattern[:, :, 0]
    swap = functools.partial(lax.ppermute, axis_name=BOTH, perm=core_perm(n))
    send = lambda x, perms: [lax.ppermute(x, BOTH, p) for p in perms]
    rhs_o, mask_o, inv_o, other = swap(rhs), swap(mask), swap(inv), swap(mine)

    far = perm(n, lambda a, c, b: (b, c ^ 1, a))
    inv_to = lax.ppermute(inv[1:], BOTH, far)
    inv_tk = swap(inv_to)

    vec = (2, count // 2, width)
    masks = (info, mask, mask_o)
    y = [None] * 5
    x = [None] * 5
    y[0], msg = call(
        functools.partial(start_kernel, [pair_index(1, 0)]), [vec, vec], masks, (rhs, rhs_o, inv, inv_o, mine, other)
    )
    for level in range(1, 4):
        got = send(msg, down_perms(n))
        pairs = [pair_index(level + 1, b) for b in range(level + 1)]
        y[level], msg = call(
            functools.partial(down_kernel, level, n, pairs),
            [vec, vec],
            masks,
            (rhs, rhs_o, inv, inv_o, mine, other, msg, *got, *y[:level]),
            [vec],
        )
    got = send(msg, plane_perms(n))
    y[4], x[4], msg = call(
        functools.partial(turn_kernel, n, [pair_index(4, 3)]),
        [vec, vec, vec],
        masks,
        (inv_tk, inv_to, mine, other, y[3], msg, *got),
    )
    for level in (3, 2, 1):
        got = send(msg, up_perms(n))
        pairs = [pair_index(c, level - 1) for c in range(4, level - 1, -1)]
        x[level], msg = call(
            functools.partial(up_kernel, level, n, pairs),
            [vec, vec],
            masks,
            (inv_tk, inv_to, mine, other, y[level - 1], msg, *got, *x[4:level:-1]),
        )
    got = send(msg, line_perms(n))
    (x[0],) = call(functools.partial(last_kernel, n), [vec], (info,), (inv, inv_o, y[0], msg, *got), [vec])

    held = jnp.stack([y[4], x[4], x[3], x[2], x[1]])
    moved = lax.ppermute(held, BOTH, turn_perm(n))
    moved = jnp.where(q == z, held, moved)
    full = jnp.stack([*y[:4], moved[0], x[0], moved[4], moved[3], moved[2], moved[1]])
    keep = jnp.where(k == 0, full[:, 0], full[:, 1])
    give = jnp.where(k == 0, full[:, 1], full[:, 0])
    take = swap(give)
    low = jnp.where(half == 0, keep, take)
    high = jnp.where(half == 0, take, keep)
    out = jnp.concatenate([low, high], axis=1)[:, None]
    return out[:5], out[5:]


def solution(mesh):
    return jax.shard_map(
        on_device,
        mesh=mesh,
        in_specs=(
            P(None, "row", None, None),
            P(None, "col", "row", None, None),
            P(None, "col", "row"),
            P(None, "row", None, None),
        ),
        out_specs=(P(None, "row", None, None), P(None, "row", None, None)),
        check_vma=False,
    )
```

time: 286 us -> 128 us (0.45)
  blocking collectives: 258 us -> 0 us
  starting transfers between devices: 0 us -> 61.7 us
  waiting for transfers between devices: 0 us -> 34.7 us
  matrix products: 22.6 us -> 0 us
  local copies, waits for them, and re-layouts: 0.77 us -> 15 us
  Pallas kernels: 0 us -> 11.8 us
    psum x12 -> x0, blocking collectives: 223 us -> none  [the longest x4 92.6 us: on_device(): lax.psum(partial_value.astype(jnp.bfloat16), 'row').astype(jnp.float32)]
    ppermute x0 -> x38, starting transfers between devices: none -> 61.7 us  [the longest x30 60 us: on_device(): send = lambda x, perms: [lax.ppermute(x, BOTH, p) for p in perms]]
    all_gather x4 -> x0, blocking collectives: 34.9 us -> none  [spread(): whole = lax.all_gather(solved, 'row', axis=0, tiled=True)]
    ppermute x0 -> x38, waiting for transfers between devices: none -> 34.7 us  [the longest x30 30.6 us: on_device(): send = lambda x, perms: [lax.ppermute(x, BOTH, p) for p in perms]]
    dot_general x30 -> x0, matrix products: 22.6 us -> none  [the longest x5 8.15 us: solve_lower(): jnp.einsum('mrj,mij->mri', zeta, inverse, preferred_element_type=jnp.floa...]
    pallas_call x0 -> x9, Pallas kernels: none -> 11.8 us  [call(): pl.pallas_call(body, out_shape=[jax.ShapeDtypeStruct(s, jnp.bfloat16) for...]
    unnamed x19 -> x39, local copies, waits for them, and re-layouts: 0.77 us -> 12.4 us
  transfers between devices with their start and end apart: 0 -> 38, of which waited for: 0 -> 20; matrix products, arithmetic and copies ran while one was open for 0% -> 2% of each run, Pallas kernels for 0% -> 5%
where the time goes in v1:
time: 128 us; the launch traced here: 126 us
  starting transfers between devices  61.7 us (48%)
  waiting for transfers between devices  34.7 us (27%)
  local copies, waits for them, and re-layouts  15 us (12%)
  Pallas kernels  11.8 us (9%)
  other arithmetic  1.72 us (1%)
    ppermute x30, starting transfers between devices, on_device(): send = lambda x, perms: [lax.ppermute(x, BOTH, p) for p in perms]  60 us
    ppermute x30, waiting for transfers between devices, on_device(): send = lambda x, perms: [lax.ppermute(x, BOTH, p) for p in perms]  30.6 us
    unnamed x39, local copies, waits for them, and re-layouts  12.4 us
    pallas_call x9, Pallas kernels, call(): pl.pallas_call(body, out_shape=[jax.ShapeDtypeStruct(s, jnp.bfloat16) for...  11.8 us
    ppermute x4, waiting for transfers between devices, on_device(): rhs_o, mask_o, inv_o, other = (swap(rhs), swap(mask), swap(inv), swap(mine))  2.82 us
  transfers between devices with their start and end apart: 38, of which 20 were waited for; matrix products, arithmetic and copies ran while one was open for 2% of the time, Pallas kernels for 5%

profile of v1, /device:TPU:0, one launch (start us, length us, event | category | flops | bytes accessed | tf_op | source)
XLA Modules:
  0.0 125.7 jit_solution(7852565349546727528)
XLA Ops:
  1.2 1.9 %slice_bitcast_fusion = bf16[4,256,256]{2,1,0:T(8,128)(2,1)} fusion(bf16[5,1,256,256]{3,2,0,1:T(8,128)(2,1)} %bitcast.76), kind=kLoop, calls=%fused_computation | loop fusion | bytes 1048576 | tf_op jit(solution)/shard_map/slice | solution.py:226
  5.7 2.0 %collective-permute-done.1.rhs_other.refs_4_ = bf16[5,32,256]{2,1,0:T(8,128)(2,1)S(1)} collective-permute-done((bf16[5,32,256]{2,1,0:T(8,128)(2,1)}, bf16[5,32,256]{2,1,0:T(8,128)(2,1)S(1)}, u32[]{:S(2)}, u32[]{:S(2)}) %collective-permute-start.1) | collective-permute-done | bytes 81952 | tf_op jit(solution)/shard_map/ppermute | solution.py:223
  8.6 1.5 %copy-done.2 = bf16[10,2,256,256]{3,2,1,0:T(8,128)(2,1)} copy-done((bf16[10,2,256,256]{3,2,1,0:T(8,128)(2,1)}, bf16[10,2,256,256]{3,2,1,0:T(8,128)(2,1)S(1)}, u32[]{:S(2)}) %copy-start.2) | copy-done | bytes 2621464
  10.0 1.7 %copy-done = bf16[10,2,1,256,256]{4,3,2,1,0:T(8,128)(2,1)S(1)} copy-done((bf16[10,2,1,256,256]{4,3,2,1,0:T(8,128)(2,1)S(1)}, bf16[10,2,1,256,256]{4,3,2,1,0:T(8,128)(2,1)}, u32[]{:S(2)}) %copy-start) | copy-done | bytes 2621464
  11.8 1.7 %copy-done.3 = bf16[10,2,256,256]{3,2,1,0:T(8,128)(2,1)S(1)} copy-done((bf16[10,2,256,256]{3,2,1,0:T(8,128)(2,1)S(1)}, bf16[10,2,256,256]{3,2,1,0:T(8,128)(2,1)}, u32[]{:S(2)}) %copy-start.3) | copy-done | bytes 2621464
  17.7 4.7 %collective-permute-start.7 = (bf16[2,16,256]{2,1,0:T(8,128)(2,1)S(1)}, bf16[2,16,256]{2,1,0:T(8,128)(2,1)S(1)}, u32[]{:S(2)}, u32[]{:S(2)}) collective-permute-start(bf16[2,16,256]{2,1,0:T(8,128)(2,1)S(1)} %get-tuple-element.20.refs_9_), channel_id=1, source_target_pairs={{0,7},{1,15},{2,19},{3,27},{4,3},{5,11},{6,23},{7,31},{8,4},{9,12}... | collective-permute-start | bytes 49160 | tf_op jit(solution)/shard_map/ppermute | solution.py:222
  25.6 2.5 %collective-permute-done.5.refs_11_ = bf16[2,16,256]{2,1,0:T(8,128)(2,1)S(1)} collective-permute-done((bf16[2,16,256]{2,1,0:T(8,128)(2,1)S(1)}, bf16[2,16,256]{2,1,0:T(8,128)(2,1)S(1)}, u32[]{:S(2)}, u32[]{:S(2)}) %collective-permute-start.5) | collective-permute-done | bytes 16416 | tf_op jit(solution)/shard_map/ppermute | solution.py:222
  28.2 1.7 %copy-done.4 = bf16[10,2,256,256]{3,2,1,0:T(8,128)(2,1)S(1)} copy-done((bf16[10,2,256,256]{3,2,1,0:T(8,128)(2,1)S(1)}, bf16[10,2,256,256]{3,2,1,0:T(8,128)(2,1)}, u32[]{:S(2)}) %copy-start.4) | copy-done | bytes 2621464
  32.2 4.2 %collective-permute-start.11 = (bf16[2,16,256]{2,1,0:T(8,128)(2,1)S(1)}, bf16[2,16,256]{2,1,0:T(8,128)(2,1)S(1)}, u32[]{:S(2)}, u32[]{:S(2)}) collective-permute-start(bf16[2,16,256]{2,1,0:T(8,128)(2,1)S(1)} %get-tuple-element.22.refs_9_), channel_id=1, source_target_pairs={{0,7},{1,15},{2,19},{3,27},{4,3},{5,11},{6,23},{7,31},{8,4},{9,12}... | collective-permute-start | bytes 49160 | tf_op jit(solution)/shard_map/ppermute | solution.py:222
  36.4 16.3 %collective-permute-start.10 = (bf16[2,16,256]{2,1,0:T(8,128)(2,1)S(1)}, bf16[2,16,256]{2,1,0:T(8,128)(2,1)S(1)}, u32[]{:S(2)}, u32[]{:S(2)}) collective-permute-start(bf16[2,16,256]{2,1,0:T(8,128)(2,1)S(1)} %get-tuple-element.22.refs_9_), channel_id=1, source_target_pairs={{0,2},{1,10},{2,22},{3,30},{4,6},{5,14},{6,18},{7,26},{8,3},{9,11}... | collective-permute-start | bytes 49160 | tf_op jit(solution)/shard_map/ppermute | solution.py:222
  52.8 1.4 %collective-permute-done.10.refs_12_ = bf16[2,16,256]{2,1,0:T(8,128)(2,1)S(1)} collective-permute-done((bf16[2,16,256]{2,1,0:T(8,128)(2,1)S(1)}, bf16[2,16,256]{2,1,0:T(8,128)(2,1)S(1)}, u32[]{:S(2)}, u32[]{:S(2)}) %collective-permute-start.10) | collective-permute-done | bytes 16416 | tf_op jit(solution)/shard_map/ppermute | solution.py:222
  54.2 3.2 %collective-permute-done.9.refs_11_ = bf16[2,16,256]{2,1,0:T(8,128)(2,1)S(1)} collective-permute-done((bf16[2,16,256]{2,1,0:T(8,128)(2,1)S(1)}, bf16[2,16,256]{2,1,0:T(8,128)(2,1)S(1)}, u32[]{:S(2)}, u32[]{:S(2)}) %collective-permute-start.9) | collective-permute-done | bytes 16416 | tf_op jit(solution)/shard_map/ppermute | solution.py:222
  58.8 3.1 %collective-permute-start.15 = (bf16[2,16,256]{2,1,0:T(8,128)(2,1)S(1)}, bf16[2,16,256]{2,1,0:T(8,128)(2,1)S(1)}, u32[]{:S(2)}, u32[]{:S(2)}) collective-permute-start(bf16[2,16,256]{2,1,0:T(8,128)(2,1)S(1)} %get-tuple-element.24.refs_9_), channel_id=1, source_target_pairs={{0,7},{1,15},{2,19},{3,27},{4,3},{5,11},{6,23},{7,31},{8,4},{9,12}... | collective-permute-start | bytes 49160 | tf_op jit(solution)/shard_map/ppermute | solution.py:222
  65.0 1.5 %collective-permute-done.13.refs_11_ = bf16[2,16,256]{2,1,0:T(8,128)(2,1)S(1)} collective-permute-done((bf16[2,16,256]{2,1,0:T(8,128)(2,1)S(1)}, bf16[2,16,256]{2,1,0:T(8,128)(2,1)S(1)}, u32[]{:S(2)}, u32[]{:S(2)}) %collective-permute-start.13) | collective-permute-done | bytes 16416 | tf_op jit(solution)/shard_map/ppermute | solution.py:222
  66.5 1.5 %shard_map.62 = (bf16[2,16,256]{2,1,0:T(8,128)(2,1)S(1)}, bf16[2,16,256]{2,1,0:T(8,128)(2,1)S(1)}) custom-call(s32[3]{0:T(128)S(1)} %pad_add_fusion.info.refs_0_, s32[10,2]{1,0:T(8,128)S(1)} %copy.7.mask.refs_1_, s32[10,2]{1,0:T(8,128)S(1)} %collective-permute-done.mask_other.refs_2_, bf16[5,32,256]{2,1,0:T(8,128)(2,1)S(1)} %bitcast.86, ...), custom_call_target="tpu_custom_call" | custom-call | tf_op jit(solution)/shard_map/pallas_call | solution.py:197
  68.0 5.1 %collective-permute-start.20 = (bf16[2,16,256]{2,1,0:T(8,128)(2,1)S(1)}, bf16[2,16,256]{2,1,0:T(8,128)(2,1)S(1)}, u32[]{:S(2)}, u32[]{:S(2)}) collective-permute-start(bf16[2,16,256]{2,1,0:T(8,128)(2,1)S(1)} %get-tuple-element.26.refs_8_), channel_id=1, source_target_pairs={{0,24},{1,25},{2,26},{3,27},{4,28},{5,29},{6,30},{7,31},{8,16},{9,... | collective-permute-start | bytes 49160 | tf_op jit(solution)/shard_map/ppermute | solution.py:222
  74.9 1.4 %collective-permute-done.19.refs_10_ = bf16[2,16,256]{2,1,0:T(8,128)(2,1)S(1)} collective-permute-done((bf16[2,16,256]{2,1,0:T(8,128)(2,1)S(1)}, bf16[2,16,256]{2,1,0:T(8,128)(2,1)S(1)}, u32[]{:S(2)}, u32[]{:S(2)}) %collective-permute-start.19) | collective-permute-done | bytes 16416 | tf_op jit(solution)/shard_map/ppermute | solution.py:222
  76.3 1.5 %shard_map.63 = (bf16[2,16,256]{2,1,0:T(8,128)(2,1)S(1)}, bf16[2,16,256]{2,1,0:T(8,128)(2,1)S(1)}, bf16[2,16,256]{2,1,0:T(8,128)(2,1)S(1)}) custom-call(s32[3]{0:T(128)S(1)} %pad_add_fusion.info.refs_0_, s32[10,2]{1,0:T(8,128)S(1)} %copy.7.mask.refs_1_, s32[10,2]{1,0:T(8,128)S(1)} %collective-permute-done.mask_other.refs_2_, ...), custom_call_target="tpu_custom_call" | custom-call | tf_op jit(solution)/shard_map/pallas_call | solution.py:197
  77.8 1.7 %collective-permute-start.24 = (bf16[2,16,256]{2,1,0:T(8,128)(2,1)S(1)}, bf16[2,16,256]{2,1,0:T(8,128)(2,1)S(1)}, u32[]{:S(2)}, u32[]{:S(2)}) collective-permute-start(bf16[2,16,256]{2,1,0:T(8,128)(2,1)S(1)} %get-tuple-element.29.refs_8_), channel_id=1, source_target_pairs={{0,24},{1,4},{2,12},{3,16},{4,28},{5,0},{6,8},{7,20},{8,25},{9,5},... | collective-permute-start | bytes 49160 | tf_op jit(solution)/shard_map/ppermute | solution.py:222
  80.4 2.6 %collective-permute-start.22 = (bf16[2,16,256]{2,1,0:T(8,128)(2,1)S(1)}, bf16[2,16,256]{2,1,0:T(8,128)(2,1)S(1)}, u32[]{:S(2)}, u32[]{:S(2)}) collective-permute-start(bf16[2,16,256]{2,1,0:T(8,128)(2,1)S(1)} %get-tuple-element.29.refs_8_), channel_id=1, source_target_pairs={{0,12},{1,16},{2,24},{3,4},{4,8},{5,20},{6,28},{7,0},{8,13},{9,17}... | collective-permute-start | bytes 49160 | tf_op jit(solution)/shard_map/ppermute | solution.py:222
  84.3 3.2 %collective-permute-done.22.refs_10_ = bf16[2,16,256]{2,1,0:T(8,128)(2,1)S(1)} collective-permute-done((bf16[2,16,256]{2,1,0:T(8,128)(2,1)S(1)}, bf16[2,16,256]{2,1,0:T(8,128)(2,1)S(1)}, u32[]{:S(2)}, u32[]{:S(2)}) %collective-permute-start.22) | collective-permute-done | bytes 16416 | tf_op jit(solution)/shard_map/ppermute | solution.py:222
  87.5 1.4 %shard_map.64 = (bf16[2,16,256]{2,1,0:T(8,128)(2,1)S(1)}, bf16[2,16,256]{2,1,0:T(8,128)(2,1)S(1)}) custom-call(s32[3]{0:T(128)S(1)} %pad_add_fusion.info.refs_0_, s32[10,2]{1,0:T(8,128)S(1)} %copy.7.mask.refs_1_, s32[10,2]{1,0:T(8,128)S(1)} %collective-permute-done.mask_other.refs_2_, bf16[4,256,256]{2,1,0:T(8,128)(2,1)S(1)} %collective-permute-done.17.refs_3_, ...), custom_call_target="tpu_custom_call" | custom-call | tf_op jit(solution)/shard_map/pallas_call | solution.py:197
  88.9 5.4 %collective-permute-start.28 = (bf16[2,16,256]{2,1,0:T(8,128)(2,1)S(1)}, bf16[2,16,256]{2,1,0:T(8,128)(2,1)S(1)}, u32[]{:S(2)}, u32[]{:S(2)}) collective-permute-start(bf16[2,16,256]{2,1,0:T(8,128)(2,1)S(1)} %get-tuple-element.31.refs_8_), channel_id=1, source_target_pairs={{0,24},{1,4},{2,12},{3,16},{4,28},{5,0},{6,8},{7,20},{8,25},{9,5},... | collective-permute-start | bytes 49160 | tf_op jit(solution)/shard_map/ppermute | solution.py:222
  94.3 1.4 %collective-permute-done.28.refs_12_ = bf16[2,16,256]{2,1,0:T(8,128)(2,1)S(1)} collective-permute-done((bf16[2,16,256]{2,1,0:T(8,128)(2,1)S(1)}, bf16[2,16,256]{2,1,0:T(8,128)(2,1)S(1)}, u32[]{:S(2)}, u32[]{:S(2)}) %collective-permute-start.28) | collective-permute-done | bytes 16416 | tf_op jit(solution)/shard_map/ppermute | solution.py:222
  95.7 3.3 %collective-permute-done.27.refs_11_ = bf16[2,16,256]{2,1,0:T(8,128)(2,1)S(1)} collective-permute-done((bf16[2,16,256]{2,1,0:T(8,128)(2,1)S(1)}, bf16[2,16,256]{2,1,0:T(8,128)(2,1)S(1)}, u32[]{:S(2)}, u32[]{:S(2)}) %collective-permute-start.27) | collective-permute-done | bytes 16416 | tf_op jit(solution)/shard_map/ppermute | solution.py:222
  99.3 1.4 %shard_map.65 = (bf16[2,16,256]{2,1,0:T(8,128)(2,1)S(1)}, bf16[2,16,256]{2,1,0:T(8,128)(2,1)S(1)}) custom-call(s32[3]{0:T(128)S(1)} %pad_add_fusion.info.refs_0_, s32[10,2]{1,0:T(8,128)S(1)} %copy.7.mask.refs_1_, s32[10,2]{1,0:T(8,128)S(1)} %collective-permute-done.mask_other.refs_2_, bf16[4,256,256]{2,1,0:T(8,128)(2,1)S(1)} %collective-permute-done.17.refs_3_, ...), custom_call_target="tpu_custom_call" | custom-call | tf_op jit(solution)/shard_map/pallas_call | solution.py:197
  100.7 2.8 %collective-permute-start.32 = (bf16[2,16,256]{2,1,0:T(8,128)(2,1)S(1)}, bf16[2,16,256]{2,1,0:T(8,128)(2,1)S(1)}, u32[]{:S(2)}, u32[]{:S(2)}) collective-permute-start(bf16[2,16,256]{2,1,0:T(8,128)(2,1)S(1)} %get-tuple-element.33.refs_8_), channel_id=1, source_target_pairs={{0,24},{1,4},{2,12},{3,16},{4,28},{5,0},{6,8},{7,20},{8,25},{9,5},... | collective-permute-start | bytes 49160 | tf_op jit(solution)/shard_map/ppermute | solution.py:222
  104.7 1.6 %collective-permute-start.30 = (bf16[2,16,256]{2,1,0:T(8,128)(2,1)S(1)}, bf16[2,16,256]{2,1,0:T(8,128)(2,1)S(1)}, u32[]{:S(2)}, u32[]{:S(2)}) collective-permute-start(bf16[2,16,256]{2,1,0:T(8,128)(2,1)S(1)} %get-tuple-element.33.refs_8_), channel_id=1, source_target_pairs={{0,12},{1,16},{2,24},{3,4},{4,8},{5,20},{6,28},{7,0},{8,13},{9,17}... | collective-permute-start | bytes 49160 | tf_op jit(solution)/shard_map/ppermute | solution.py:222
  106.3 2.2 %collective-permute-done.31.refs_11_ = bf16[2,16,256]{2,1,0:T(8,128)(2,1)S(1)} collective-permute-done((bf16[2,16,256]{2,1,0:T(8,128)(2,1)S(1)}, bf16[2,16,256]{2,1,0:T(8,128)(2,1)S(1)}, u32[]{:S(2)}, u32[]{:S(2)}) %collective-permute-start.31) | collective-permute-done | bytes 16416 | tf_op jit(solution)/shard_map/ppermute | solution.py:222
  109.7 1.5 %shard_map.66 = (bf16[2,16,256]{2,1,0:T(8,128)(2,1)S(1)}, bf16[2,16,256]{2,1,0:T(8,128)(2,1)S(1)}) custom-call(s32[3]{0:T(128)S(1)} %pad_add_fusion.info.refs_0_, s32[10,2]{1,0:T(8,128)S(1)} %copy.7.mask.refs_1_, s32[10,2]{1,0:T(8,128)S(1)} %collective-permute-done.mask_other.refs_2_, bf16[4,256,256]{2,1,0:T(8,128)(2,1)S(1)} %collective-permute-done.17.refs_3_, ...), custom_call_target="tpu_custom_call" | custom-call | tf_op jit(solution)/shard_map/pallas_call | solution.py:197
  111.2 5.4 %collective-permute-start.36 = (bf16[2,16,256]{2,1,0:T(8,128)(2,1)S(1)}, bf16[2,16,256]{2,1,0:T(8,128)(2,1)S(1)}, u32[]{:S(2)}, u32[]{:S(2)}) collective-permute-start(bf16[2,16,256]{2,1,0:T(8,128)(2,1)S(1)} %get-tuple-element.35.refs_4_), channel_id=1, source_target_pairs={{0,7},{1,6},{2,5},{3,4},{4,3},{5,2},{6,1},{7,0},{8,15},{9,14},{10,... | collective-permute-start | bytes 49160 | tf_op jit(solution)/shard_map/ppermute | solution.py:222
  118.0 3.3 %collective-permute-done.35.refs_6_ = bf16[2,16,256]{2,1,0:T(8,128)(2,1)S(1)} collective-permute-done((bf16[2,16,256]{2,1,0:T(8,128)(2,1)S(1)}, bf16[2,16,256]{2,1,0:T(8,128)(2,1)S(1)}, u32[]{:S(2)}, u32[]{:S(2)}) %collective-permute-start.35) | collective-permute-done | bytes 16416 | tf_op jit(solution)/shard_map/ppermute | solution.py:222
  (101 shorter events, 30.7 us)
Async XLA Ops:
  0.6 7.9 %collective-permute-start.3 = (bf16[10,2,256,256]{3,2,1,0:T(8,128)(2,1)}, bf16[10,2,256,256]{3,2,1,0:T(8,128)(2,1)S(1)}, u32[]{:S(2)}, u32[]{:S(2)}) collective-permute-start(bf16[10,2,256,256]{3,2,1,0:T(8,128)(2,1)} %bitcast.66), channel_id=1, source_target_pairs={{0,4},{1,5},{2,6},{3,7},{4,0},{5,1},{6,2},{7,3},{8,12},{9,13},{10,... | collective-permute-start | bytes 7864328 | tf_op jit(solution)/shard_map/ppermute | solution.py:223
  1.1 6.6 %collective-permute-start.2 = (bf16[5,256,256]{2,1,0:T(8,128)(2,1)}, bf16[5,256,256]{2,1,0:T(8,128)(2,1)S(1)}, u32[]{:S(2)}, u32[]{:S(2)}) collective-permute-start(bf16[5,256,256]{2,1,0:T(8,128)(2,1)} %bitcast.75), channel_id=1, source_target_pairs={{0,4},{1,5},{2,6},{3,7},{4,0},{5,1},{6,2},{7,3},{8,12},{9,13},{10,... | collective-permute-start | bytes 1966088 | tf_op jit(solution)/shard_map/ppermute | solution.py:223
  3.1 21.8 %collective-permute-start.16 = (bf16[4,256,256]{2,1,0:T(8,128)(2,1)}, bf16[4,256,256]{2,1,0:T(8,128)(2,1)}, u32[]{:S(2)}, u32[]{:S(2)}) collective-permute-start(bf16[4,256,256]{2,1,0:T(8,128)(2,1)} %slice_bitcast_fusion), channel_id=1, source_target_pairs={{0,4},{1,12},{2,20},{3,28},{4,0},{5,8},{6,16},{7,24},{8,5},{9,13},... | collective-permute-start | bytes 1572872 | tf_op jit(solution)/shard_map/ppermute | solution.py:226
  4.4 3.3 %collective-permute-start.1 = (bf16[5,32,256]{2,1,0:T(8,128)(2,1)}, bf16[5,32,256]{2,1,0:T(8,128)(2,1)S(1)}, u32[]{:S(2)}, u32[]{:S(2)}) collective-permute-start(bf16[5,32,256]{2,1,0:T(8,128)(2,1)} %bitcast.82), channel_id=1, source_target_pairs={{0,4},{1,5},{2,6},{3,7},{4,0},{5,1},{6,2},{7,3},{8,12},{9,13},{10,... | collective-permute-start | bytes 245768 | tf_op jit(solution)/shard_map/ppermute | solution.py:223
  17.7 7.2 %collective-permute-start.7 = (bf16[2,16,256]{2,1,0:T(8,128)(2,1)S(1)}, bf16[2,16,256]{2,1,0:T(8,128)(2,1)S(1)}, u32[]{:S(2)}, u32[]{:S(2)}) collective-permute-start(bf16[2,16,256]{2,1,0:T(8,128)(2,1)S(1)} %get-tuple-element.20.refs_9_), channel_id=1, source_target_pairs={{0,7},{1,15},{2,19},{3,27},{4,3},{5,11},{6,23},{7,31},{8,4},{9,12}... | collective-permute-start | bytes 49160 | tf_op jit(solution)/shard_map/ppermute | solution.py:222
  23.5 4.6 %collective-permute-start.5 = (bf16[2,16,256]{2,1,0:T(8,128)(2,1)S(1)}, bf16[2,16,256]{2,1,0:T(8,128)(2,1)S(1)}, u32[]{:S(2)}, u32[]{:S(2)}) collective-permute-start(bf16[2,16,256]{2,1,0:T(8,128)(2,1)S(1)} %get-tuple-element.20.refs_9_), channel_id=1, source_target_pairs={{0,5},{1,13},{2,17},{3,25},{4,1},{5,9},{6,21},{7,29},{8,6},{9,14},... | collective-permute-start | bytes 49160 | tf_op jit(solution)/shard_map/ppermute | solution.py:222
  24.0 4.1 %collective-permute-start.4 = (bf16[2,16,256]{2,1,0:T(8,128)(2,1)S(1)}, bf16[2,16,256]{2,1,0:T(8,128)(2,1)}, u32[]{:S(2)}, u32[]{:S(2)}) collective-permute-start(bf16[2,16,256]{2,1,0:T(8,128)(2,1)S(1)} %get-tuple-element.20.refs_9_), channel_id=1, source_target_pairs={{0,4},{1,8},{2,20},{3,28},{4,0},{5,12},{6,16},{7,24},{8,1},{9,13},... | collective-permute-start | bytes 49160 | tf_op jit(solution)/shard_map/ppermute | solution.py:222
  24.9 48.6 %collective-permute-start.17 = (bf16[4,256,256]{2,1,0:T(8,128)(2,1)}, bf16[4,256,256]{2,1,0:T(8,128)(2,1)S(1)}, u32[]{:S(2)}, u32[]{:S(2)}) collective-permute-start(bf16[4,256,256]{2,1,0:T(8,128)(2,1)} %collective-permute-done.16.refs_4_), channel_id=1, source_target_pairs={{0,4},{1,5},{2,6},{3,7},{4,0},{5,1},{6,2},{7,3},{8,12},{9,13},{10,... | collective-permute-start | bytes 1572872 | tf_op jit(solution)/shard_map/ppermute | solution.py:227
  32.2 20.5 %collective-permute-start.11 = (bf16[2,16,256]{2,1,0:T(8,128)(2,1)S(1)}, bf16[2,16,256]{2,1,0:T(8,128)(2,1)S(1)}, u32[]{:S(2)}, u32[]{:S(2)}) collective-permute-start(bf16[2,16,256]{2,1,0:T(8,128)(2,1)S(1)} %get-tuple-element.22.refs_9_), channel_id=1, source_target_pairs={{0,7},{1,15},{2,19},{3,27},{4,3},{5,11},{6,23},{7,31},{8,4},{9,12}... | collective-permute-start | bytes 49160 | tf_op jit(solution)/shard_map/ppermute | solution.py:222
  36.4 17.7 %collective-permute-start.10 = (bf16[2,16,256]{2,1,0:T(8,128)(2,1)S(1)}, bf16[2,16,256]{2,1,0:T(8,128)(2,1)S(1)}, u32[]{:S(2)}, u32[]{:S(2)}) collective-permute-start(bf16[2,16,256]{2,1,0:T(8,128)(2,1)S(1)} %get-tuple-element.22.refs_9_), channel_id=1, source_target_pairs={{0,2},{1,10},{2,22},{3,30},{4,6},{5,14},{6,18},{7,26},{8,3},{9,11}... | collective-permute-start | bytes 49160 | tf_op jit(solution)/shard_map/ppermute | solution.py:222
  52.7 4.6 %collective-permute-start.9 = (bf16[2,16,256]{2,1,0:T(8,128)(2,1)S(1)}, bf16[2,16,256]{2,1,0:T(8,128)(2,1)S(1)}, u32[]{:S(2)}, u32[]{:S(2)}) collective-permute-start(bf16[2,16,256]{2,1,0:T(8,128)(2,1)S(1)} %get-tuple-element.22.refs_9_), channel_id=1, source_target_pairs={{0,5},{1,13},{2,17},{3,25},{4,1},{5,9},{6,21},{7,29},{8,6},{9,14},... | collective-permute-start | bytes 49160 | tf_op jit(solution)/shard_map/ppermute | solution.py:222
  52.7 4.6 %collective-permute-start.8 = (bf16[2,16,256]{2,1,0:T(8,128)(2,1)S(1)}, bf16[2,16,256]{2,1,0:T(8,128)(2,1)S(1)}, u32[]{:S(2)}, u32[]{:S(2)}) collective-permute-start(bf16[2,16,256]{2,1,0:T(8,128)(2,1)S(1)} %get-tuple-element.22.refs_9_), channel_id=1, source_target_pairs={{0,4},{1,8},{2,20},{3,28},{4,0},{5,12},{6,16},{7,24},{8,1},{9,13},... | collective-permute-start | bytes 49160 | tf_op jit(solution)/shard_map/ppermute | solution.py:222
  58.8 5.0 %collective-permute-start.15 = (bf16[2,16,256]{2,1,0:T(8,128)(2,1)S(1)}, bf16[2,16,256]{2,1,0:T(8,128)(2,1)S(1)}, u32[]{:S(2)}, u32[]{:S(2)}) collective-permute-start(bf16[2,16,256]{2,1,0:T(8,128)(2,1)S(1)} %get-tuple-element.24.refs_9_), channel_id=1, source_target_pairs={{0,7},{1,15},{2,19},{3,27},{4,3},{5,11},{6,23},{7,31},{8,4},{9,12}... | collective-permute-start | bytes 49160 | tf_op jit(solution)/shard_map/ppermute | solution.py:222
  61.9 4.6 %collective-permute-start.13 = (bf16[2,16,256]{2,1,0:T(8,128)(2,1)S(1)}, bf16[2,16,256]{2,1,0:T(8,128)(2,1)S(1)}, u32[]{:S(2)}, u32[]{:S(2)}) collective-permute-start(bf16[2,16,256]{2,1,0:T(8,128)(2,1)S(1)} %get-tuple-element.24.refs_9_), channel_id=1, source_target_pairs={{0,5},{1,13},{2,17},{3,25},{4,1},{5,9},{6,21},{7,29},{8,6},{9,14},... | collective-permute-start | bytes 49160 | tf_op jit(solution)/shard_map/ppermute | solution.py:222
  62.6 3.9 %collective-permute-start.12 = (bf16[2,16,256]{2,1,0:T(8,128)(2,1)S(1)}, bf16[2,16,256]{2,1,0:T(8,128)(2,1)S(1)}, u32[]{:S(2)}, u32[]{:S(2)}) collective-permute-start(bf16[2,16,256]{2,1,0:T(8,128)(2,1)S(1)} %get-tuple-element.24.refs_9_), channel_id=1, source_target_pairs={{0,4},{1,8},{2,20},{3,28},{4,0},{5,12},{6,16},{7,24},{8,1},{9,13},... | collective-permute-start | bytes 49160 | tf_op jit(solution)/shard_map/ppermute | solution.py:222
  68.0 6.8 %collective-permute-start.20 = (bf16[2,16,256]{2,1,0:T(8,128)(2,1)S(1)}, bf16[2,16,256]{2,1,0:T(8,128)(2,1)S(1)}, u32[]{:S(2)}, u32[]{:S(2)}) collective-permute-start(bf16[2,16,256]{2,1,0:T(8,128)(2,1)S(1)} %get-tuple-element.26.refs_8_), channel_id=1, source_target_pairs={{0,24},{1,25},{2,26},{3,27},{4,28},{5,29},{6,30},{7,31},{8,16},{9,... | collective-permute-start | bytes 49160 | tf_op jit(solution)/shard_map/ppermute | solution.py:222
  77.8 5.2 %collective-permute-start.24 = (bf16[2,16,256]{2,1,0:T(8,128)(2,1)S(1)}, bf16[2,16,256]{2,1,0:T(8,128)(2,1)S(1)}, u32[]{:S(2)}, u32[]{:S(2)}) collective-permute-start(bf16[2,16,256]{2,1,0:T(8,128)(2,1)S(1)} %get-tuple-element.29.refs_8_), channel_id=1, source_target_pairs={{0,24},{1,4},{2,12},{3,16},{4,28},{5,0},{6,8},{7,20},{8,25},{9,5},... | collective-permute-start | bytes 49160 | tf_op jit(solution)/shard_map/ppermute | solution.py:222
  79.5 4.8 %collective-permute-start.23 = (bf16[2,16,256]{2,1,0:T(8,128)(2,1)S(1)}, bf16[2,16,256]{2,1,0:T(8,128)(2,1)S(1)}, u32[]{:S(2)}, u32[]{:S(2)}) collective-permute-start(bf16[2,16,256]{2,1,0:T(8,128)(2,1)S(1)} %get-tuple-element.29.refs_8_), channel_id=1, source_target_pairs={{0,20},{1,28},{2,0},{3,8},{4,16},{5,24},{6,4},{7,12},{8,21},{9,29}... | collective-permute-start | bytes 49160 | tf_op jit(solution)/shard_map/ppermute | solution.py:222
  80.4 7.1 %collective-permute-start.22 = (bf16[2,16,256]{2,1,0:T(8,128)(2,1)S(1)}, bf16[2,16,256]{2,1,0:T(8,128)(2,1)S(1)}, u32[]{:S(2)}, u32[]{:S(2)}) collective-permute-start(bf16[2,16,256]{2,1,0:T(8,128)(2,1)S(1)} %get-tuple-element.29.refs_8_), channel_id=1, source_target_pairs={{0,12},{1,16},{2,24},{3,4},{4,8},{5,20},{6,28},{7,0},{8,13},{9,17}... | collective-permute-start | bytes 49160 | tf_op jit(solution)/shard_map/ppermute | solution.py:222
  83.0 4.5 %collective-permute-start.21 = (bf16[2,16,256]{2,1,0:T(8,128)(2,1)S(1)}, bf16[2,16,256]{2,1,0:T(8,128)(2,1)S(1)}, u32[]{:S(2)}, u32[]{:S(2)}) collective-permute-start(bf16[2,16,256]{2,1,0:T(8,128)(2,1)S(1)} %get-tuple-element.29.refs_8_), channel_id=1, source_target_pairs={{0,4},{1,8},{2,20},{3,28},{4,0},{5,12},{6,16},{7,24},{8,1},{9,13},... | collective-permute-start | bytes 49160 | tf_op jit(solution)/shard_map/ppermute | solution.py:222
  88.9 6.8 %collective-permute-start.28 = (bf16[2,16,256]{2,1,0:T(8,128)(2,1)S(1)}, bf16[2,16,256]{2,1,0:T(8,128)(2,1)S(1)}, u32[]{:S(2)}, u32[]{:S(2)}) collective-permute-start(bf16[2,16,256]{2,1,0:T(8,128)(2,1)S(1)} %get-tuple-element.31.refs_8_), channel_id=1, source_target_pairs={{0,24},{1,4},{2,12},{3,16},{4,28},{5,0},{6,8},{7,20},{8,25},{9,5},... | collective-permute-start | bytes 49160 | tf_op jit(solution)/shard_map/ppermute | solution.py:222
  94.3 4.8 %collective-permute-start.27 = (bf16[2,16,256]{2,1,0:T(8,128)(2,1)S(1)}, bf16[2,16,256]{2,1,0:T(8,128)(2,1)S(1)}, u32[]{:S(2)}, u32[]{:S(2)}) collective-permute-start(bf16[2,16,256]{2,1,0:T(8,128)(2,1)S(1)} %get-tuple-element.31.refs_8_), channel_id=1, source_target_pairs={{0,20},{1,28},{2,0},{3,8},{4,16},{5,24},{6,4},{7,12},{8,21},{9,29}... | collective-permute-start | bytes 49160 | tf_op jit(solution)/shard_map/ppermute | solution.py:222
  94.3 5.0 %collective-permute-start.26 = (bf16[2,16,256]{2,1,0:T(8,128)(2,1)S(1)}, bf16[2,16,256]{2,1,0:T(8,128)(2,1)S(1)}, u32[]{:S(2)}, u32[]{:S(2)}) collective-permute-start(bf16[2,16,256]{2,1,0:T(8,128)(2,1)S(1)} %get-tuple-element.31.refs_8_), channel_id=1, source_target_pairs={{0,12},{1,16},{2,24},{3,4},{4,8},{5,20},{6,28},{7,0},{8,13},{9,17}... | collective-permute-start | bytes 49160 | tf_op jit(solution)/shard_map/ppermute | solution.py:222
  94.3 5.0 %collective-permute-start.25 = (bf16[2,16,256]{2,1,0:T(8,128)(2,1)S(1)}, bf16[2,16,256]{2,1,0:T(8,128)(2,1)S(1)}, u32[]{:S(2)}, u32[]{:S(2)}) collective-permute-start(bf16[2,16,256]{2,1,0:T(8,128)(2,1)S(1)} %get-tuple-element.31.refs_8_), channel_id=1, source_target_pairs={{0,4},{1,8},{2,20},{3,28},{4,0},{5,12},{6,16},{7,24},{8,1},{9,13},... | collective-permute-start | bytes 49160 | tf_op jit(solution)/shard_map/ppermute | solution.py:222
  100.7 5.6 %collective-permute-start.32 = (bf16[2,16,256]{2,1,0:T(8,128)(2,1)S(1)}, bf16[2,16,256]{2,1,0:T(8,128)(2,1)S(1)}, u32[]{:S(2)}, u32[]{:S(2)}) collective-permute-start(bf16[2,16,256]{2,1,0:T(8,128)(2,1)S(1)} %get-tuple-element.33.refs_8_), channel_id=1, source_target_pairs={{0,24},{1,4},{2,12},{3,16},{4,28},{5,0},{6,8},{7,20},{8,25},{9,5},... | collective-permute-start | bytes 49160 | tf_op jit(solution)/shard_map/ppermute | solution.py:222
  103.5 5.0 %collective-permute-start.31 = (bf16[2,16,256]{2,1,0:T(8,128)(2,1)S(1)}, bf16[2,16,256]{2,1,0:T(8,128)(2,1)S(1)}, u32[]{:S(2)}, u32[]{:S(2)}) collective-permute-start(bf16[2,16,256]{2,1,0:T(8,128)(2,1)S(1)} %get-tuple-element.33.refs_8_), channel_id=1, source_target_pairs={{0,20},{1,28},{2,0},{3,8},{4,16},{5,24},{6,4},{7,12},{8,21},{9,29}... | collective-permute-start | bytes 49160 | tf_op jit(solution)/shard_map/ppermute | solution.py:222
  104.7 5.0 %collective-permute-start.30 = (bf16[2,16,256]{2,1,0:T(8,128)(2,1)S(1)}, bf16[2,16,256]{2,1,0:T(8,128)(2,1)S(1)}, u32[]{:S(2)}, u32[]{:S(2)}) collective-permute-start(bf16[2,16,256]{2,1,0:T(8,128)(2,1)S(1)} %get-tuple-element.33.refs_8_), channel_id=1, source_target_pairs={{0,12},{1,16},{2,24},{3,4},{4,8},{5,20},{6,28},{7,0},{8,13},{9,17}... | collective-permute-start | bytes 49160 | tf_op jit(solution)/shard_map/ppermute | solution.py:222
  106.3 3.4 %collective-permute-start.29 = (bf16[2,16,256]{2,1,0:T(8,128)(2,1)S(1)}, bf16[2,16,256]{2,1,0:T(8,128)(2,1)S(1)}, u32[]{:S(2)}, u32[]{:S(2)}) collective-permute-start(bf16[2,16,256]{2,1,0:T(8,128)(2,1)S(1)} %get-tuple-element.33.refs_8_), channel_id=1, source_target_pairs={{0,4},{1,8},{2,20},{3,28},{4,0},{5,12},{6,16},{7,24},{8,1},{9,13},... | collective-permute-start | bytes 49160 | tf_op jit(solution)/shard_map/ppermute | solution.py:222
  111.2 6.8 %collective-permute-start.36 = (bf16[2,16,256]{2,1,0:T(8,128)(2,1)S(1)}, bf16[2,16,256]{2,1,0:T(8,128)(2,1)S(1)}, u32[]{:S(2)}, u32[]{:S(2)}) collective-permute-start(bf16[2,16,256]{2,1,0:T(8,128)(2,1)S(1)} %get-tuple-element.35.refs_4_), channel_id=1, source_target_pairs={{0,7},{1,6},{2,5},{3,4},{4,3},{5,2},{6,1},{7,0},{8,15},{9,14},{10,... | collective-permute-start | bytes 49160 | tf_op jit(solution)/shard_map/ppermute | solution.py:222
  116.6 4.7 %collective-permute-start.35 = (bf16[2,16,256]{2,1,0:T(8,128)(2,1)S(1)}, bf16[2,16,256]{2,1,0:T(8,128)(2,1)S(1)}, u32[]{:S(2)}, u32[]{:S(2)}) collective-permute-start(bf16[2,16,256]{2,1,0:T(8,128)(2,1)S(1)} %get-tuple-element.35.refs_4_), channel_id=1, source_target_pairs={{0,2},{1,3},{2,0},{3,1},{4,6},{5,7},{6,4},{7,5},{8,10},{9,11},{10,... | collective-permute-start | bytes 49160 | tf_op jit(solution)/shard_map/ppermute | solution.py:222
  116.6 4.7 %collective-permute-start.34 = (bf16[2,16,256]{2,1,0:T(8,128)(2,1)S(1)}, bf16[2,16,256]{2,1,0:T(8,128)(2,1)S(1)}, u32[]{:S(2)}, u32[]{:S(2)}) collective-permute-start(bf16[2,16,256]{2,1,0:T(8,128)(2,1)S(1)} %get-tuple-element.35.refs_4_), channel_id=1, source_target_pairs={{0,5},{1,4},{2,7},{3,6},{4,1},{5,0},{6,3},{7,2},{8,13},{9,12},{10,... | collective-permute-start | bytes 49160 | tf_op jit(solution)/shard_map/ppermute | solution.py:222
  116.9 5.1 %collective-permute-start.33 = (bf16[5,2,16,256]{3,2,1,0:T(8,128)(2,1)S(1)}, bf16[5,2,16,256]{3,2,1,0:T(8,128)(2,1)S(1)}, u32[]{:S(2)}, u32[]{:S(2)}) collective-permute-start(bf16[5,2,16,256]{3,2,1,0:T(8,128)(2,1)S(1)} %constant_dynamic-update-slice_fusion), channel_id=1, source_target_pairs={{0,4},{1,8},{2,20},{3,28},{4,0},{5,12},{6,16},{7,24},{8,1},{9,13},... | collective-permute-start | bytes 245768 | tf_op jit(solution)/shard_map/ppermute | solution.py:266
  (19 other events, 62.5 us)

commit v2 on v0

v2 whole, which is shorter than its diff:
```python
import functools

import jax
import jax.numpy as jnp
from jax import lax
from jax.experimental import pallas as pl
from jax.experimental.pallas import tpu as pltpu
from jax.sharding import PartitionSpec as P

BOTH = ("row", "col")
NT = (((1,), (1,)), ((), ()))
NN = (((1,), (0,)), ((), ()))


def pair_index(later, earlier):
    return later * (later - 1) // 2 + earlier


def perm(n, target):
    pairs = []
    for q in range(n):
        for k in range(2):
            for z in range(n):
                a, b, c = target(q, k, z)
                assert (a, b, c) != (q, k, z)
                pairs.append(((2 * q + k) * n + z, (2 * a + b) * n + c))
    return pairs


def down_perms(n):
    return [perm(n, lambda q, k, z, j=j: (z, (q & 1) ^ 1, 2 * ((q >> 1) ^ j) + k)) for j in range(n // 2)]


def up_perms(n):
    return [perm(n, lambda q, k, z, j=j: (2 * ((z >> 1) ^ j) + k, (z & 1) ^ 1, q)) for j in range(n // 2)]


def plane_perms(n):
    return [perm(n, lambda q, k, z, m=m: (q ^ m, k ^ (m.bit_count() & 1), z)) for m in range(1, n)]


def line_perms(n):
    return [perm(n, lambda q, k, z, m=m: (q, k ^ (m & 1), z ^ m)) for m in range(1, n)]


def turn_perm(n):
    return perm(n, lambda q, k, z: (z, k ^ 1, q ^ z))


def far_perm(n):
    return perm(n, lambda q, k, z: (q ^ z, k ^ 1, q))


def core_perm(n):
    return perm(n, lambda q, k, z: (q, k ^ 1, z))


def tree(parts):
    while len(parts) > 1:
        half = len(parts) // 2
        parts = [parts[i] + parts[i + half] for i in range(half)]
    return parts[0]


def f32(x):
    return x.astype(jnp.float32)


def bf16(x):
    return x.astype(jnp.bfloat16)


def dot(a, b, dims):
    return lax.dot_general(a, b, dims, preferred_element_type=jnp.float32)


def place():
    row = lax.axis_index("row")
    return row % 2, row // 2 == lax.axis_index("col")


def row_of(mask, p, t):
    return mask[3, pl.ds(2 * p + t, 1), :]


def lower_part(k, pairs, solved, mine, other, keep, gotten):
    outs = []
    for t in range(2):
        acc = None
        for p, y in zip(pairs, solved, strict=True):
            a = dot(y[k], mine[p, t], NT) * row_of(keep, p, t)
            b = dot(y[1 - k], other[p, t], NT) * row_of(gotten, p, t)
            acc = a + b if acc is None else acc + (a + b)
        outs.append(acc)
    return outs


def upper_part(pairs, solved, mine, other, keep, gotten):
    outs = []
    for blocks, mask in ((mine, keep), (other, gotten)):
        acc = None
        for p, x in zip(pairs, solved, strict=True):
            for t in range(2):
                a = dot(x[t], blocks[p, t], NN) * row_of(mask, p, t)
                acc = a if acc is None else acc + a
        outs.append(acc)
    return outs


def start_kernel(pattern, rhs, inv, mine, keep_ref, give_ref, rhs_in, inv_in, mine_in, sems):
    copies = [
        pltpu.make_async_copy(source.at[0], target, sems.at[i])
        for i, (source, target) in enumerate(((rhs, rhs_in), (inv, inv_in), (mine, mine_in)))
    ]
    for copy in copies:
        copy.start()
    for i in range(keep_ref.shape[1]):
        value = f32(pattern[i % 2, 0, i // 2]) if i < 2 * pattern.shape[2] else 0.0
        keep_ref[3, pl.ds(i, 1), :] = jnp.full((1, keep_ref.shape[2]), value, jnp.float32)
    for copy in copies:
        copy.wait()
    y = bf16(dot(rhs_in[...], inv_in[...], NT))
    keep_ref[0] = f32(y)
    for t in range(2):
        keep_ref[1 + t] = dot(y, mine_in[t], NT) * f32(pattern[t, 0, 0])
    give_ref[...] = keep_ref[...]


def join_kernel(keep, gotten, inv, mine, y_ref, msg_ref):
    del inv, mine
    k, _ = place()
    y_ref[k] = bf16(keep[0])
    y_ref[1 - k] = bf16(gotten[0])
    for t in range(2):
        msg_ref[t] = bf16(keep[1 + t] + gotten[1 + t])


def stage_kernel(*refs):
    count = (len(refs) - 1) // 2
    sems, copies = refs[-1], []
    for source, target in zip(refs[:count], refs[count:-1], strict=True):
        for i in range(source.shape[0]):
            copies.append(pltpu.make_async_copy(source.at[i], target.at[i], sems.at[len(copies)]))
    for copy in copies:
        copy.start()
    for copy in copies:
        copy.wait()


def down_kernel(level, pairs, *refs):
    keep, gotten, rhs, rhs_other, inv, inv_other, mine, other, some, rest = refs[:10]
    earlier = refs[10 : 10 + level]
    y_ref, msg_ref, total_ref = refs[10 + level :]
    k, diagonal = place()
    total_ref[...] = some[...] + rest[...]
    for at, b, inverse in ((k, rhs, inv), (1 - k, rhs_other, inv_other)):
        y_ref[at] = bf16(dot(bf16(f32(b[level]) - total_ref[at]), inverse[level], NT))
    parts = lower_part(k, pairs, list(earlier) + [y_ref], mine, other, keep, gotten)
    if level == 3:
        total_ref[k], total_ref[1 - k] = f32(rhs[4]), f32(rhs_other[4])
        parts = [jnp.where(diagonal, p - total_ref[t], p) for t, p in enumerate(parts)]
    for t, part in enumerate(parts):
        msg_ref[t] = bf16(part)


def up_parts(k, diagonal, level, pairs, solved, y, factors, inv, inv_other):
    parts = upper_part(pairs, solved, *factors)
    outs = []
    for part, at, inverse in zip(parts, (k, 1 - k), (inv, inv_other), strict=True):
        part = jnp.where(diagonal, part - f32(y[at]), part)
        outs.append((at, bf16(dot(bf16(part), inverse[level], NN))))
    return outs


def turn_kernel(n, pairs, *refs):
    keep, gotten, inv_k, inv_o, inv, inv_other, mine, other, y3, own = refs[:10]
    got = refs[10 : 10 + n - 1]
    y_ref, x_ref, msg_ref = refs[10 + n - 1 :]
    k, diagonal = place()
    x_ref[...] = bf16(-tree([f32(own[...])] + [f32(g[...]) for g in got]))
    for at, inverse in ((k, inv_k), (1 - k, inv_o)):
        y_ref[at] = bf16(dot(x_ref[at], inverse[...], NT))
    for at, inverse in ((k, inv_k), (1 - k, inv_o)):
        x_ref[at] = bf16(dot(y_ref[at], inverse[...], NN))
    for at, part in up_parts(k, diagonal, 3, pairs, [x_ref], y3, (mine, other, keep, gotten), inv, inv_other):
        msg_ref[at] = part


def up_kernel(level, pairs, *refs):
    keep, gotten, inv, inv_other, mine, other, below, y4, some, rest = refs[:10]
    later = refs[10 : 14 - level]
    outs = refs[14 - level :]
    k, diagonal = place()
    x_ref = outs[0]
    x_ref[...] = bf16(-(some[...] + rest[...]))
    solved = list(later) + [x_ref]
    parts = up_parts(k, diagonal, level - 1, pairs, solved, below, (mine, other, keep, gotten), inv, inv_other)
    if level > 1:
        for at, part in parts:
            outs[1][at] = part
    else:
        for ref, (_, part) in zip(outs[1:], parts, strict=False):
            ref[...] = part
        for i, v in enumerate((y4, *solved)):
            outs[3][i] = v[1 - k]


def out_kernel(n, *refs):
    own, got = refs[0], refs[1:n]
    y, moved = refs[n : n + 4], refs[n + 4]
    forward, solved, forward_ref, solved_ref, sems = refs[n + 5 :]
    k, _ = place()
    for level in range(4):
        forward_ref[level, 0] = y[level][k]
        solved_ref[4 - level, 0] = moved[1 + level]
    forward_ref[4, 0] = moved[0]
    solved_ref[0, 0] = bf16(-tree([f32(own[...])] + [f32(g[...]) for g in got]))
    copies = [
        pltpu.make_async_copy(forward_ref, forward, sems.at[0]),
        pltpu.make_async_copy(solved_ref, solved, sems.at[1]),
    ]
    for copy in copies:
        copy.start()
    for copy in copies:
        copy.wait()


VMEM = pl.BlockSpec(memory_space=pltpu.VMEM)
ANY = pl.BlockSpec(memory_space=pl.ANY)
ROOM = pltpu.CompilerParams(vmem_limit_bytes=16 * 1024 * 1024)


def call(body, outs, args, scratch=()):
    return pl.pallas_call(
        body,
        out_shape=[jax.ShapeDtypeStruct(s, jnp.bfloat16) for s in outs],
        in_specs=[VMEM] * len(args),
        out_specs=[VMEM] * len(outs),
        scratch_shapes=list(scratch),
        compiler_params=ROOM,
    )(*args)


def on_device(rhs, factor, pattern, diag_inverse):
    n = lax.axis_size("col")
    levels, own, count, width = rhs.shape
    assert levels == 5 and own == 1 and factor.shape[1] == 2 and lax.axis_size("row") == 2 * n

    rhs, inv = rhs[:, 0], diag_inverse[:, 0]
    mine = factor[:, :, 0]
    swap = functools.partial(lax.ppermute, axis_name=BOTH, perm=core_perm(n))
    send = lambda x, perms: [lax.ppermute(x, BOTH, p) for p in perms]
    vec, slots = (2, count, width), (4, count, width)

    def share(msg, perms):
        got = send(msg, perms)
        some = tree([f32(g) for g in got])
        return got, some, swap(some)

    last, rhs_first = lax.optimization_barrier((inv[4], rhs))
    inv_to = lax.ppermute(last, BOTH, far_perm(n))
    inv_o, other, rhs_o = swap(inv), swap(mine), swap(rhs)
    keep, give = pl.pallas_call(
        start_kernel,
        out_shape=[jax.ShapeDtypeStruct(slots, jnp.float32)] * 2,
        in_specs=[pl.BlockSpec(memory_space=pltpu.SMEM), ANY, ANY, ANY],
        out_specs=[VMEM] * 2,
        scratch_shapes=[pltpu.VMEM(a.shape[1:], a.dtype) for a in (rhs, inv, mine)] + [pltpu.SemaphoreType.DMA((3,))],
        compiler_params=ROOM,
    )(pattern.transpose(1, 2, 0), rhs_first, inv, mine)
    gotten = swap(give)

    y = [None] * 5
    x = [None] * 5
    y[0], msg = call(join_kernel, [vec, vec], (keep, gotten, inv, mine))
    for level in range(1, 4):
        got, some, rest = share(msg, down_perms(n))
        if level == 1:
            inv_o, other, _ = lax.optimization_barrier((inv_o, other, got[0]))
            inv_o, other = pl.pallas_call(
                stage_kernel,
                out_shape=[jax.ShapeDtypeStruct(a.shape, a.dtype) for a in (inv_o, other)],
                in_specs=[ANY] * 2,
                out_specs=[VMEM] * 2,
                scratch_shapes=[pltpu.SemaphoreType.DMA((inv_o.shape[0] + other.shape[0],))],
                compiler_params=ROOM,
            )(inv_o, other)
            inv_tk = swap(inv_to)
        pairs = [pair_index(level + 1, b) for b in range(level + 1)]
        y[level], msg = call(
            functools.partial(down_kernel, level, pairs),
            [vec, vec],
            (keep, gotten, rhs, rhs_o, inv, inv_o, mine, other, some, rest, *y[:level]),
            [pltpu.VMEM(vec, jnp.float32)],
        )
    got = send(msg, plane_perms(n))
    y[4], x[4], msg = call(
        functools.partial(turn_kernel, n, [pair_index(4, 3)]),
        [vec, vec, vec],
        (keep, gotten, inv_tk, inv_to, inv, inv_o, mine, other, y[3], msg, *got),
    )
    for level in (3, 2, 1):
        got, some, rest = share(msg, up_perms(n))
        pairs = [pair_index(c, level - 1) for c in range(4, level - 1, -1)]
        x[level], msg, *more = call(
            functools.partial(up_kernel, level, pairs),
            [vec, vec] if level > 1 else [vec, vec[1:], vec[1:], (5, *vec[1:])],
            (keep, gotten, inv, inv_o, mine, other, y[level - 1], y[4], some, rest, *x[4:level:-1]),
        )
    moved = lax.ppermute(more[1], BOTH, turn_perm(n))
    got = [lax.ppermute(more[0] if m & 1 else msg, BOTH, p) for m, p in enumerate(line_perms(n), 1)]
    out = jax.ShapeDtypeStruct((levels, 1, count, width), jnp.bfloat16)
    return pl.pallas_call(
        functools.partial(out_kernel, n),
        out_shape=[out, out],
        in_specs=[VMEM] * (n + 5),
        out_specs=[ANY] * 2,
        scratch_shapes=[pltpu.VMEM(out.shape, out.dtype)] * 2 + [pltpu.SemaphoreType.DMA((2,))],
        compiler_params=ROOM,
    )(msg, *got, *y[:4], moved)


def solution(mesh):
    return jax.shard_map(
        on_device,
        mesh=mesh,
        in_specs=(
            P(None, "row", None, None),
            P(None, "col", "row", None, None),
            P(None, "col", "row"),
            P(None, "row", None, None),
        ),
        out_specs=(P(None, "row", None, None), P(None, "row", None, None)),
        check_vma=False,
    )
```

time: 286 us -> 92.5 us (0.32)
  blocking collectives: 258 us -> 0 us
  starting transfers between devices: 0 us -> 41.6 us
  waiting for transfers between devices: 0 us -> 34.3 us
  matrix products: 22.6 us -> 0 us
  Pallas kernels: 0 us -> 10.8 us
  local copies, waits for them, and re-layouts: 0.77 us -> 4.42 us
    psum x12 -> x0, blocking collectives: 223 us -> none  [the longest x4 92.6 us: on_device(): lax.psum(partial_value.astype(jnp.bfloat16), 'row').astype(jnp.float32)]
    ppermute x0 -> x31, starting transfers between devices: none -> 41.6 us  [the longest x15 33.5 us: on_device(): send = lambda x, perms: [lax.ppermute(x, BOTH, p) for p in perms]]
    all_gather x4 -> x0, blocking collectives: 34.9 us -> none  [spread(): whole = lax.all_gather(solved, 'row', axis=0, tiled=True)]
    ppermute x0 -> x31, waiting for transfers between devices: none -> 34.3 us  [the longest x15 22.7 us: on_device(): send = lambda x, perms: [lax.ppermute(x, BOTH, p) for p in perms]]
    dot_general x30 -> x0, matrix products: 22.6 us -> none  [the longest x5 8.15 us: solve_lower(): jnp.einsum('mrj,mij->mri', zeta, inverse, preferred_element_type=jnp.floa...]
    pallas_call x0 -> x11, Pallas kernels: none -> 10.8 us  [the longest x8 7.06 us: call(): pl.pallas_call(body, out_shape=[jax.ShapeDtypeStruct(s, jnp.bfloat16) for...]
  transfers between devices with their start and end apart: 0 -> 31, of which waited for: 0 -> 18; matrix products, arithmetic and copies ran while one was open for 0% -> 1% of each run, Pallas kernels for 0% -> 7%
where the time goes in v2:
time: 92.5 us; the launch traced here: 92.1 us
  starting transfers between devices  41.6 us (45%)
  waiting for transfers between devices  34.3 us (37%)
  Pallas kernels  10.8 us (12%)
  local copies, waits for them, and re-layouts  4.42 us (5%)
    ppermute x15, starting transfers between devices, on_device(): send = lambda x, perms: [lax.ppermute(x, BOTH, p) for p in perms]  33.5 us
    ppermute x15, waiting for transfers between devices, on_device(): send = lambda x, perms: [lax.ppermute(x, BOTH, p) for p in perms]  22.7 us
    pallas_call x8, Pallas kernels, call(): pl.pallas_call(body, out_shape=[jax.ShapeDtypeStruct(s, jnp.bfloat16) for...  7.06 us
    ppermute x6, waiting for transfers between devices, share(): return (got, some, swap(some))  5.88 us
    ppermute x3, waiting for transfers between devices, on_device(): lax.ppermute(more[0] if m & 1 else msg, BOTH, p)  4.76 us
    ppermute x3, starting transfers between devices, on_device(): lax.ppermute(more[0] if m & 1 else msg, BOTH, p)  3.83 us
    unnamed x10, local copies, waits for them, and re-layouts  3.51 us
    ppermute x3, starting transfers between devices, on_device(): inv_o, other, rhs_o = (swap(inv), swap(mine), swap(rhs))  2.54 us
  transfers between devices with their start and end apart: 31, of which 18 were waited for; matrix products, arithmetic and copies ran while one was open for 1% of the time, Pallas kernels for 7%

profile of v2, /device:TPU:0, one launch (start us, length us, event | category | flops | bytes accessed | tf_op | source)
XLA Modules:
  0.0 92.1 jit_solution(18033632331463012138)
XLA Ops:
  2.2 1.7 %copy-done = bf16[10,2,1,256,256]{4,3,2,1,0:T(8,128)(2,1)S(1)} copy-done((bf16[10,2,1,256,256]{4,3,2,1,0:T(8,128)(2,1)S(1)}, bf16[10,2,1,256,256]{4,3,2,1,0:T(8,128)(2,1)}, u32[]{:S(2)}) %copy-start) | copy-done | bytes 2621464
  3.9 1.1 %copy-done.2 = bf16[5,1,256,256]{3,2,1,0:T(8,128)(2,1)S(1)} copy-done((bf16[5,1,256,256]{3,2,1,0:T(8,128)(2,1)S(1)}, bf16[5,1,256,256]{3,2,1,0:T(8,128)(2,1)}, u32[]{:S(2)}) %copy-start.2) | copy-done | bytes 655384
  5.7 1.9 %shard_map.59 = (f32[4,32,256]{2,1,0:T(8,128)S(1)}, f32[4,32,256]{2,1,0:T(8,128)S(1)}) custom-call(s32[2,1,10]{2,1,0:T(1,128)S(1)} %bitcast.26, bf16[5,32,256]{2,1,0:T(8,128)(2,1)} %bitcast.2.rhs.refs_2_, bf16[5,256,256]{2,1,0:T(8,128)(2,1)S(1)} %bitcast.17, bf16[10,2,256,256]{3,2,1,0:T(8,128)(2,1)S(1)} %bitcast.7), custom_call_target="tpu_custom_call" | custom-call | tf_op jit(solution)/shard_map/pallas_call | solution.py:263
  9.5 4.5 %collective-permute-start.7 = (bf16[2,32,256]{2,1,0:T(8,128)(2,1)S(1)}, bf16[2,32,256]{2,1,0:T(8,128)(2,1)S(1)}, u32[]{:S(2)}, u32[]{:S(2)}) collective-permute-start(bf16[2,32,256]{2,1,0:T(8,128)(2,1)S(1)} %get-tuple-element.31), channel_id=1, source_target_pairs={{0,6},{1,14},{2,22},{3,30},{4,7},{5,15},{6,23},{7,31},{8,2},{9,10}... | collective-permute-start | bytes 98312 | tf_op jit(solution)/shard_map/ppermute | solution.py:252
  14.0 1.9 %collective-permute-start.6 = (bf16[5,32,256]{2,1,0:T(8,128)(2,1)}, bf16[5,32,256]{2,1,0:T(8,128)(2,1)S(1)}, u32[]{:S(2)}, u32[]{:S(2)}) collective-permute-start(bf16[5,32,256]{2,1,0:T(8,128)(2,1)} %bitcast.2.rhs.refs_2_), channel_id=1, source_target_pairs={{0,4},{1,5},{2,6},{3,7},{4,0},{5,1},{6,2},{7,3},{8,12},{9,13},{10,... | collective-permute-start | bytes 245768 | tf_op jit(solution)/shard_map/ppermute | solution.py:262
  15.9 1.4 %collective-permute-done.7 = bf16[2,32,256]{2,1,0:T(8,128)(2,1)S(1)} collective-permute-done((bf16[2,32,256]{2,1,0:T(8,128)(2,1)S(1)}, bf16[2,32,256]{2,1,0:T(8,128)(2,1)S(1)}, u32[]{:S(2)}, u32[]{:S(2)}) %collective-permute-start.7) | collective-permute-done | bytes 32800 | tf_op jit(solution)/shard_map/ppermute | solution.py:252
  17.4 1.2 %shard_map.61 = (bf16[5,256,256]{2,1,0:T(8,128)(2,1)S(1)}, bf16[10,2,256,256]{3,2,1,0:T(8,128)(2,1)S(1)}) custom-call(bf16[5,256,256]{2,1,0:T(8,128)(2,1)S(1)} %collective-permute-done.1.refs_0_, bf16[10,2,256,256]{3,2,1,0:T(8,128)(2,1)S(1)} %collective-permute-done.2.refs_1_), custom_call_target="tpu_custom_call" | custom-call | tf_op jit(solution)/shard_map/pallas_call | solution.py:280
  18.7 1.4 %shard_map.62 = (bf16[2,32,256]{2,1,0:T(8,128)(2,1)S(1)}, bf16[2,32,256]{2,1,0:T(8,128)(2,1)S(1)}) custom-call(f32[4,32,256]{2,1,0:T(8,128)S(1)} %get-tuple-element.29.keep.refs_0_, f32[4,32,256]{2,1,0:T(8,128)S(1)} %collective-permute-done.gotten.refs_1_, bf16[5,32,256]{2,1,0:T(8,128)(2,1)} %bitcast.2.rhs.refs_2_, ...), custom_call_target="tpu_custom_call" | custom-call | tf_op jit(solution)/shard_map/pallas_call | solution.py:234
  20.1 2.7 %collective-permute-start.10 = (bf16[2,32,256]{2,1,0:T(8,128)(2,1)S(1)}, bf16[2,32,256]{2,1,0:T(8,128)(2,1)S(1)}, u32[]{:S(2)}, u32[]{:S(2)}) collective-permute-start(bf16[2,32,256]{2,1,0:T(8,128)(2,1)S(1)} %get-tuple-element.38), channel_id=1, source_target_pairs={{0,6},{1,14},{2,22},{3,30},{4,7},{5,15},{6,23},{7,31},{8,2},{9,10}... | collective-permute-start | bytes 98312 | tf_op jit(solution)/shard_map/ppermute | solution.py:252
  22.8 2.2 %collective-permute-start.9 = (bf16[2,32,256]{2,1,0:T(8,128)(2,1)S(1)}, bf16[2,32,256]{2,1,0:T(8,128)(2,1)S(1)}, u32[]{:S(2)}, u32[]{:S(2)}) collective-permute-start(bf16[2,32,256]{2,1,0:T(8,128)(2,1)S(1)} %get-tuple-element.38), channel_id=1, source_target_pairs={{0,4},{1,12},{2,20},{3,28},{4,5},{5,13},{6,21},{7,29},{8,0},{9,8},... | collective-permute-start | bytes 98312 | tf_op jit(solution)/shard_map/ppermute | solution.py:252
  25.0 2.3 %collective-permute-done.10 = bf16[2,32,256]{2,1,0:T(8,128)(2,1)S(1)} collective-permute-done((bf16[2,32,256]{2,1,0:T(8,128)(2,1)S(1)}, bf16[2,32,256]{2,1,0:T(8,128)(2,1)S(1)}, u32[]{:S(2)}, u32[]{:S(2)}) %collective-permute-start.10) | collective-permute-done | bytes 32800 | tf_op jit(solution)/shard_map/ppermute | solution.py:252
  27.4 1.2 %collective-permute-done.11.refs_9_ = f32[2,32,256]{2,1,0:T(8,128)S(1)} collective-permute-done((f32[2,32,256]{2,1,0:T(8,128)S(1)}, f32[2,32,256]{2,1,0:T(8,128)S(1)}, u32[]{:S(2)}, u32[]{:S(2)}) %collective-permute-start.11) | collective-permute-done | bytes 65568 | tf_op jit(solution)/shard_map/ppermute | solution.py:258
  28.6 1.5 %shard_map.63 = (bf16[2,32,256]{2,1,0:T(8,128)(2,1)S(1)}, bf16[2,32,256]{2,1,0:T(8,128)(2,1)S(1)}) custom-call(f32[4,32,256]{2,1,0:T(8,128)S(1)} %get-tuple-element.29.keep.refs_0_, f32[4,32,256]{2,1,0:T(8,128)S(1)} %collective-permute-done.gotten.refs_1_, bf16[5,32,256]{2,1,0:T(8,128)(2,1)} %bitcast.2.rhs.refs_2_, ...), custom_call_target="tpu_custom_call" | custom-call | tf_op jit(solution)/shard_map/pallas_call | solution.py:234
  30.4 5.4 %collective-permute-start.13 = (bf16[2,32,256]{2,1,0:T(8,128)(2,1)S(1)}, bf16[2,32,256]{2,1,0:T(8,128)(2,1)S(1)}, u32[]{:S(2)}, u32[]{:S(2)}) collective-permute-start(bf16[2,32,256]{2,1,0:T(8,128)(2,1)S(1)} %get-tuple-element.40), channel_id=1, source_target_pairs={{0,6},{1,14},{2,22},{3,30},{4,7},{5,15},{6,23},{7,31},{8,2},{9,10}... | collective-permute-start | bytes 98312 | tf_op jit(solution)/shard_map/ppermute | solution.py:252
  35.8 1.8 %collective-permute-done.13 = bf16[2,32,256]{2,1,0:T(8,128)(2,1)S(1)} collective-permute-done((bf16[2,32,256]{2,1,0:T(8,128)(2,1)S(1)}, bf16[2,32,256]{2,1,0:T(8,128)(2,1)S(1)}, u32[]{:S(2)}, u32[]{:S(2)}) %collective-permute-start.13) | collective-permute-done | bytes 32800 | tf_op jit(solution)/shard_map/ppermute | solution.py:252
  37.7 1.2 %collective-permute-done.14.refs_9_ = f32[2,32,256]{2,1,0:T(8,128)S(1)} collective-permute-done((f32[2,32,256]{2,1,0:T(8,128)S(1)}, f32[2,32,256]{2,1,0:T(8,128)S(1)}, u32[]{:S(2)}, u32[]{:S(2)}) %collective-permute-start.14) | collective-permute-done | bytes 65568 | tf_op jit(solution)/shard_map/ppermute | solution.py:258
  38.9 1.7 %shard_map.64 = (bf16[2,32,256]{2,1,0:T(8,128)(2,1)S(1)}, bf16[2,32,256]{2,1,0:T(8,128)(2,1)S(1)}) custom-call(f32[4,32,256]{2,1,0:T(8,128)S(1)} %get-tuple-element.29.keep.refs_0_, f32[4,32,256]{2,1,0:T(8,128)S(1)} %collective-permute-done.gotten.refs_1_, bf16[5,32,256]{2,1,0:T(8,128)(2,1)} %bitcast.2.rhs.refs_2_, ...), custom_call_target="tpu_custom_call" | custom-call | tf_op jit(solution)/shard_map/pallas_call | solution.py:234
  40.6 4.6 %collective-permute-start.15 = (bf16[2,32,256]{2,1,0:T(8,128)(2,1)S(1)}, bf16[2,32,256]{2,1,0:T(8,128)(2,1)S(1)}, u32[]{:S(2)}, u32[]{:S(2)}) collective-permute-start(bf16[2,32,256]{2,1,0:T(8,128)(2,1)S(1)} %get-tuple-element.43.refs_9_), channel_id=1, source_target_pairs={{0,12},{1,13},{2,14},{3,15},{4,8},{5,9},{6,10},{7,11},{8,4},{9,5},... | collective-permute-start | bytes 98312 | tf_op jit(solution)/shard_map/ppermute | solution.py:252
  45.2 2.6 %collective-permute-start.16 = (bf16[2,32,256]{2,1,0:T(8,128)(2,1)S(1)}, bf16[2,32,256]{2,1,0:T(8,128)(2,1)S(1)}, u32[]{:S(2)}, u32[]{:S(2)}) collective-permute-start(bf16[2,32,256]{2,1,0:T(8,128)(2,1)S(1)} %get-tuple-element.43.refs_9_), channel_id=1, source_target_pairs={{0,20},{1,21},{2,22},{3,23},{4,16},{5,17},{6,18},{7,19},{8,28},{9,... | collective-permute-start | bytes 98312 | tf_op jit(solution)/shard_map/ppermute | solution.py:252
  47.9 1.6 %collective-permute-done.16.refs_11_ = bf16[2,32,256]{2,1,0:T(8,128)(2,1)S(1)} collective-permute-done((bf16[2,32,256]{2,1,0:T(8,128)(2,1)S(1)}, bf16[2,32,256]{2,1,0:T(8,128)(2,1)S(1)}, u32[]{:S(2)}, u32[]{:S(2)}) %collective-permute-start.16) | collective-permute-done | bytes 32800 | tf_op jit(solution)/shard_map/ppermute | solution.py:252
  49.5 3.2 %collective-permute-done.17.refs_12_ = bf16[2,32,256]{2,1,0:T(8,128)(2,1)S(1)} collective-permute-done((bf16[2,32,256]{2,1,0:T(8,128)(2,1)S(1)}, bf16[2,32,256]{2,1,0:T(8,128)(2,1)S(1)}, u32[]{:S(2)}, u32[]{:S(2)}) %collective-permute-start.17) | collective-permute-done | bytes 32800 | tf_op jit(solution)/shard_map/ppermute | solution.py:252
  53.3 3.3 %collective-permute-start.19 = (bf16[2,32,256]{2,1,0:T(8,128)(2,1)S(1)}, bf16[2,32,256]{2,1,0:T(8,128)(2,1)S(1)}, u32[]{:S(2)}, u32[]{:S(2)}) collective-permute-start(bf16[2,32,256]{2,1,0:T(8,128)(2,1)S(1)} %get-tuple-element.45), channel_id=1, source_target_pairs={{0,20},{1,16},{2,4},{3,0},{4,28},{5,24},{6,12},{7,8},{8,21},{9,17}... | collective-permute-start | bytes 98312 | tf_op jit(solution)/shard_map/ppermute | solution.py:252
  57.2 2.0 %collective-permute-done.19 = bf16[2,32,256]{2,1,0:T(8,128)(2,1)S(1)} collective-permute-done((bf16[2,32,256]{2,1,0:T(8,128)(2,1)S(1)}, bf16[2,32,256]{2,1,0:T(8,128)(2,1)S(1)}, u32[]{:S(2)}, u32[]{:S(2)}) %collective-permute-start.19) | collective-permute-done | bytes 32800 | tf_op jit(solution)/shard_map/ppermute | solution.py:252
  61.6 4.0 %collective-permute-start.22 = (bf16[2,32,256]{2,1,0:T(8,128)(2,1)S(1)}, bf16[2,32,256]{2,1,0:T(8,128)(2,1)S(1)}, u32[]{:S(2)}, u32[]{:S(2)}) collective-permute-start(bf16[2,32,256]{2,1,0:T(8,128)(2,1)S(1)} %get-tuple-element.47), channel_id=1, source_target_pairs={{0,20},{1,16},{2,4},{3,0},{4,28},{5,24},{6,12},{7,8},{8,21},{9,17}... | collective-permute-start | bytes 98312 | tf_op jit(solution)/shard_map/ppermute | solution.py:252
  65.6 4.7 %collective-permute-done.22 = bf16[2,32,256]{2,1,0:T(8,128)(2,1)S(1)} collective-permute-done((bf16[2,32,256]{2,1,0:T(8,128)(2,1)S(1)}, bf16[2,32,256]{2,1,0:T(8,128)(2,1)S(1)}, u32[]{:S(2)}, u32[]{:S(2)}) %collective-permute-start.22) | collective-permute-done | bytes 32800 | tf_op jit(solution)/shard_map/ppermute | solution.py:252
  70.4 1.2 %collective-permute-done.23.refs_9_ = f32[2,32,256]{2,1,0:T(8,128)S(1)} collective-permute-done((f32[2,32,256]{2,1,0:T(8,128)S(1)}, f32[2,32,256]{2,1,0:T(8,128)S(1)}, u32[]{:S(2)}, u32[]{:S(2)}) %collective-permute-start.23) | collective-permute-done | bytes 65568 | tf_op jit(solution)/shard_map/ppermute | solution.py:258
  72.3 3.0 %collective-permute-start.25 = (bf16[2,32,256]{2,1,0:T(8,128)(2,1)S(1)}, bf16[2,32,256]{2,1,0:T(8,128)(2,1)S(1)}, u32[]{:S(2)}, u32[]{:S(2)}) collective-permute-start(bf16[2,32,256]{2,1,0:T(8,128)(2,1)S(1)} %get-tuple-element.49), channel_id=1, source_target_pairs={{0,20},{1,16},{2,4},{3,0},{4,28},{5,24},{6,12},{7,8},{8,21},{9,17}... | collective-permute-start | bytes 98312 | tf_op jit(solution)/shard_map/ppermute | solution.py:252
  76.1 4.3 %collective-permute-done.25 = bf16[2,32,256]{2,1,0:T(8,128)(2,1)S(1)} collective-permute-done((bf16[2,32,256]{2,1,0:T(8,128)(2,1)S(1)}, bf16[2,32,256]{2,1,0:T(8,128)(2,1)S(1)}, u32[]{:S(2)}, u32[]{:S(2)}) %collective-permute-start.25) | collective-permute-done | bytes 32800 | tf_op jit(solution)/shard_map/ppermute | solution.py:252
  80.4 1.2 %collective-permute-done.26.refs_9_ = f32[2,32,256]{2,1,0:T(8,128)S(1)} collective-permute-done((f32[2,32,256]{2,1,0:T(8,128)S(1)}, f32[2,32,256]{2,1,0:T(8,128)S(1)}, u32[]{:S(2)}, u32[]{:S(2)}) %collective-permute-start.26) | collective-permute-done | bytes 65568 | tf_op jit(solution)/shard_map/ppermute | solution.py:258
  82.8 3.5 %collective-permute-start.28 = (bf16[32,256]{1,0:T(8,128)(2,1)S(1)}, bf16[32,256]{1,0:T(8,128)(2,1)S(1)}, u32[]{:S(2)}, u32[]{:S(2)}) collective-permute-start(bf16[32,256]{1,0:T(8,128)(2,1)S(1)} %get-tuple-element.51.refs_0_), channel_id=1, source_target_pairs={{0,2},{1,3},{2,0},{3,1},{4,6},{5,7},{6,4},{7,5},{8,10},{9,11},{10,... | collective-permute-start | bytes 49160 | tf_op jit(solution)/shard_map/ppermute | solution.py:311
  86.6 1.6 %collective-permute-done.28.refs_2_ = bf16[32,256]{1,0:T(8,128)(2,1)S(1)} collective-permute-done((bf16[32,256]{1,0:T(8,128)(2,1)S(1)}, bf16[32,256]{1,0:T(8,128)(2,1)S(1)}, u32[]{:S(2)}, u32[]{:S(2)}) %collective-permute-start.28) | collective-permute-done | bytes 16416 | tf_op jit(solution)/shard_map/ppermute | solution.py:311
  88.2 3.2 %collective-permute-done.29.refs_3_ = bf16[32,256]{1,0:T(8,128)(2,1)S(1)} collective-permute-done((bf16[32,256]{1,0:T(8,128)(2,1)S(1)}, bf16[32,256]{1,0:T(8,128)(2,1)S(1)}, u32[]{:S(2)}, u32[]{:S(2)}) %collective-permute-start.29) | collective-permute-done | bytes 16416 | tf_op jit(solution)/shard_map/ppermute | solution.py:311
  (58 shorter events, 11.9 us)
Async XLA Ops:
  0.6 16.8 %collective-permute-start.2 = (bf16[10,2,256,256]{3,2,1,0:T(8,128)(2,1)}, bf16[10,2,256,256]{3,2,1,0:T(8,128)(2,1)S(1)}, u32[]{:S(2)}, u32[]{:S(2)}) collective-permute-start(bf16[10,2,256,256]{3,2,1,0:T(8,128)(2,1)} %bitcast.6), channel_id=1, source_target_pairs={{0,4},{1,5},{2,6},{3,7},{4,0},{5,1},{6,2},{7,3},{8,12},{9,13},{10,... | collective-permute-start | bytes 7864328 | tf_op jit(solution)/shard_map/ppermute | solution.py:262
  1.1 16.3 %collective-permute-start.1 = (bf16[5,256,256]{2,1,0:T(8,128)(2,1)}, bf16[5,256,256]{2,1,0:T(8,128)(2,1)S(1)}, u32[]{:S(2)}, u32[]{:S(2)}) collective-permute-start(bf16[5,256,256]{2,1,0:T(8,128)(2,1)} %bitcast.16), channel_id=1, source_target_pairs={{0,4},{1,5},{2,6},{3,7},{4,0},{5,1},{6,2},{7,3},{8,12},{9,13},{10,... | collective-permute-start | bytes 1966088 | tf_op jit(solution)/shard_map/ppermute | solution.py:262
  7.6 1.5 %collective-permute-start = (f32[4,32,256]{2,1,0:T(8,128)S(1)}, f32[4,32,256]{2,1,0:T(8,128)S(1)}, u32[]{:S(2)}, u32[]{:S(2)}) collective-permute-start(f32[4,32,256]{2,1,0:T(8,128)S(1)} %get-tuple-element.30), channel_id=1, source_target_pairs={{0,4},{1,5},{2,6},{3,7},{4,0},{5,1},{6,2},{7,3},{8,12},{9,13},{10,... | collective-permute-start | bytes 393224 | tf_op jit(solution)/shard_map/ppermute | solution.py:271
  9.1 9.6 %copy-start.3 = (bf16[5,1,256,256]{3,2,1,0:T(8,128)(2,1)S(1)}, bf16[5,1,256,256]{3,2,1,0:T(8,128)(2,1)}, u32[]{:S(2)}) copy-start(bf16[5,1,256,256]{3,2,1,0:T(8,128)(2,1)} %param.7) | copy-start | bytes 1966084
  9.1 6.8 %collective-permute-start.3 = (bf16[2,32,256]{2,1,0:T(8,128)(2,1)S(1)}, bf16[2,32,256]{2,1,0:T(8,128)(2,1)S(1)}, u32[]{:S(2)}, u32[]{:S(2)}) collective-permute-start(bf16[2,32,256]{2,1,0:T(8,128)(2,1)S(1)} %get-tuple-element.31), channel_id=1, source_target_pairs={{0,4},{1,12},{2,20},{3,28},{4,5},{5,13},{6,21},{7,29},{8,0},{9,8},... | collective-permute-start | bytes 98312 | tf_op jit(solution)/shard_map/ppermute | solution.py:252
  9.5 7.8 %collective-permute-start.7 = (bf16[2,32,256]{2,1,0:T(8,128)(2,1)S(1)}, bf16[2,32,256]{2,1,0:T(8,128)(2,1)S(1)}, u32[]{:S(2)}, u32[]{:S(2)}) collective-permute-start(bf16[2,32,256]{2,1,0:T(8,128)(2,1)S(1)} %get-tuple-element.31), channel_id=1, source_target_pairs={{0,6},{1,14},{2,22},{3,30},{4,7},{5,15},{6,23},{7,31},{8,2},{9,10}... | collective-permute-start | bytes 98312 | tf_op jit(solution)/shard_map/ppermute | solution.py:252
  14.0 4.7 %collective-permute-start.6 = (bf16[5,32,256]{2,1,0:T(8,128)(2,1)}, bf16[5,32,256]{2,1,0:T(8,128)(2,1)S(1)}, u32[]{:S(2)}, u32[]{:S(2)}) collective-permute-start(bf16[5,32,256]{2,1,0:T(8,128)(2,1)} %bitcast.2.rhs.refs_2_), channel_id=1, source_target_pairs={{0,4},{1,5},{2,6},{3,7},{4,0},{5,1},{6,2},{7,3},{8,12},{9,13},{10,... | collective-permute-start | bytes 245768 | tf_op jit(solution)/shard_map/ppermute | solution.py:262
  17.3 1.3 %collective-permute-start.8 = (f32[2,32,256]{2,1,0:T(8,128)S(1)}, f32[2,32,256]{2,1,0:T(8,128)S(1)}, u32[]{:S(2)}, u32[]{:S(2)}) collective-permute-start(f32[2,32,256]{2,1,0:T(8,128)S(1)} %convert_add_fusion.5.refs_8_), channel_id=1, source_target_pairs={{0,4},{1,5},{2,6},{3,7},{4,0},{5,1},{6,2},{7,3},{8,12},{9,13},{10,... | collective-permute-start | bytes 196616 | tf_op jit(solution)/shard_map/ppermute | solution.py:258
  20.1 7.2 %collective-permute-start.10 = (bf16[2,32,256]{2,1,0:T(8,128)(2,1)S(1)}, bf16[2,32,256]{2,1,0:T(8,128)(2,1)S(1)}, u32[]{:S(2)}, u32[]{:S(2)}) collective-permute-start(bf16[2,32,256]{2,1,0:T(8,128)(2,1)S(1)} %get-tuple-element.38), channel_id=1, source_target_pairs={{0,6},{1,14},{2,22},{3,30},{4,7},{5,15},{6,23},{7,31},{8,2},{9,10}... | collective-permute-start | bytes 98312 | tf_op jit(solution)/shard_map/ppermute | solution.py:252
  22.8 4.5 %collective-permute-start.9 = (bf16[2,32,256]{2,1,0:T(8,128)(2,1)S(1)}, bf16[2,32,256]{2,1,0:T(8,128)(2,1)S(1)}, u32[]{:S(2)}, u32[]{:S(2)}) collective-permute-start(bf16[2,32,256]{2,1,0:T(8,128)(2,1)S(1)} %get-tuple-element.38), channel_id=1, source_target_pairs={{0,4},{1,12},{2,20},{3,28},{4,5},{5,13},{6,21},{7,29},{8,0},{9,8},... | collective-permute-start | bytes 98312 | tf_op jit(solution)/shard_map/ppermute | solution.py:252
  25.0 10.8 %collective-permute-start.4 = (bf16[256,256]{1,0:T(8,128)(2,1)S(1)}, bf16[256,256]{1,0:T(8,128)(2,1)S(1)}, u32[]{:S(2)}, u32[]{:S(2)}) collective-permute-start(bf16[256,256]{1,0:T(8,128)(2,1)S(1)} %slice_bitcast_fusion), channel_id=1, source_target_pairs={{0,4},{1,12},{2,20},{3,28},{4,0},{5,8},{6,16},{7,24},{8,13},{9,5},... | collective-permute-start | bytes 393224 | tf_op jit(solution)/shard_map/ppermute | solution.py:261
  27.3 1.3 %collective-permute-start.11 = (f32[2,32,256]{2,1,0:T(8,128)S(1)}, f32[2,32,256]{2,1,0:T(8,128)S(1)}, u32[]{:S(2)}, u32[]{:S(2)}) collective-permute-start(f32[2,32,256]{2,1,0:T(8,128)S(1)} %convert_add_fusion.4.refs_8_), channel_id=1, source_target_pairs={{0,4},{1,5},{2,6},{3,7},{4,0},{5,1},{6,2},{7,3},{8,12},{9,13},{10,... | collective-permute-start | bytes 196616 | tf_op jit(solution)/shard_map/ppermute | solution.py:258
  30.1 5.6 %collective-permute-start.12 = (bf16[2,32,256]{2,1,0:T(8,128)(2,1)S(1)}, bf16[2,32,256]{2,1,0:T(8,128)(2,1)S(1)}, u32[]{:S(2)}, u32[]{:S(2)}) collective-permute-start(bf16[2,32,256]{2,1,0:T(8,128)(2,1)S(1)} %get-tuple-element.40), channel_id=1, source_target_pairs={{0,4},{1,12},{2,20},{3,28},{4,5},{5,13},{6,21},{7,29},{8,0},{9,8},... | collective-permute-start | bytes 98312 | tf_op jit(solution)/shard_map/ppermute | solution.py:252
  30.4 7.3 %collective-permute-start.13 = (bf16[2,32,256]{2,1,0:T(8,128)(2,1)S(1)}, bf16[2,32,256]{2,1,0:T(8,128)(2,1)S(1)}, u32[]{:S(2)}, u32[]{:S(2)}) collective-permute-start(bf16[2,32,256]{2,1,0:T(8,128)(2,1)S(1)} %get-tuple-element.40), channel_id=1, source_target_pairs={{0,6},{1,14},{2,22},{3,30},{4,7},{5,15},{6,23},{7,31},{8,2},{9,10}... | collective-permute-start | bytes 98312 | tf_op jit(solution)/shard_map/ppermute | solution.py:252
  35.8 12.1 %collective-permute-start.5 = (bf16[256,256]{1,0:T(8,128)(2,1)S(1)}, bf16[256,256]{1,0:T(8,128)(2,1)S(1)}, u32[]{:S(2)}, u32[]{:S(2)}) collective-permute-start(bf16[256,256]{1,0:T(8,128)(2,1)S(1)} %collective-permute-done.4.refs_3_), channel_id=1, source_target_pairs={{0,4},{1,5},{2,6},{3,7},{4,0},{5,1},{6,2},{7,3},{8,12},{9,13},{10,... | collective-permute-start | bytes 393224 | tf_op jit(solution)/shard_map/ppermute | solution.py:288
  37.6 1.3 %collective-permute-start.14 = (f32[2,32,256]{2,1,0:T(8,128)S(1)}, f32[2,32,256]{2,1,0:T(8,128)S(1)}, u32[]{:S(2)}, u32[]{:S(2)}) collective-permute-start(f32[2,32,256]{2,1,0:T(8,128)S(1)} %convert_add_fusion.3.refs_8_), channel_id=1, source_target_pairs={{0,4},{1,5},{2,6},{3,7},{4,0},{5,1},{6,2},{7,3},{8,12},{9,13},{10,... | collective-permute-start | bytes 196616 | tf_op jit(solution)/shard_map/ppermute | solution.py:258
  40.6 7.2 %collective-permute-start.15 = (bf16[2,32,256]{2,1,0:T(8,128)(2,1)S(1)}, bf16[2,32,256]{2,1,0:T(8,128)(2,1)S(1)}, u32[]{:S(2)}, u32[]{:S(2)}) collective-permute-start(bf16[2,32,256]{2,1,0:T(8,128)(2,1)S(1)} %get-tuple-element.43.refs_9_), channel_id=1, source_target_pairs={{0,12},{1,13},{2,14},{3,15},{4,8},{5,9},{6,10},{7,11},{8,4},{9,5},... | collective-permute-start | bytes 98312 | tf_op jit(solution)/shard_map/ppermute | solution.py:252
  45.2 4.2 %collective-permute-start.16 = (bf16[2,32,256]{2,1,0:T(8,128)(2,1)S(1)}, bf16[2,32,256]{2,1,0:T(8,128)(2,1)S(1)}, u32[]{:S(2)}, u32[]{:S(2)}) collective-permute-start(bf16[2,32,256]{2,1,0:T(8,128)(2,1)S(1)} %get-tuple-element.43.refs_9_), channel_id=1, source_target_pairs={{0,20},{1,21},{2,22},{3,23},{4,16},{5,17},{6,18},{7,19},{8,28},{9,... | collective-permute-start | bytes 98312 | tf_op jit(solution)/shard_map/ppermute | solution.py:252
  47.9 4.8 %collective-permute-start.17 = (bf16[2,32,256]{2,1,0:T(8,128)(2,1)S(1)}, bf16[2,32,256]{2,1,0:T(8,128)(2,1)S(1)}, u32[]{:S(2)}, u32[]{:S(2)}) collective-permute-start(bf16[2,32,256]{2,1,0:T(8,128)(2,1)S(1)} %get-tuple-element.43.refs_9_), channel_id=1, source_target_pairs={{0,24},{1,25},{2,26},{3,27},{4,28},{5,29},{6,30},{7,31},{8,16},{9,... | collective-permute-start | bytes 98312 | tf_op jit(solution)/shard_map/ppermute | solution.py:252
  53.3 4.0 %collective-permute-start.18 = (bf16[2,32,256]{2,1,0:T(8,128)(2,1)S(1)}, bf16[2,32,256]{2,1,0:T(8,128)(2,1)S(1)}, u32[]{:S(2)}, u32[]{:S(2)}) collective-permute-start(bf16[2,32,256]{2,1,0:T(8,128)(2,1)S(1)} %get-tuple-element.45), channel_id=1, source_target_pairs={{0,4},{1,0},{2,20},{3,16},{4,12},{5,8},{6,28},{7,24},{8,5},{9,1},{... | collective-permute-start | bytes 98312 | tf_op jit(solution)/shard_map/ppermute | solution.py:252
  53.3 5.9 %collective-permute-start.19 = (bf16[2,32,256]{2,1,0:T(8,128)(2,1)S(1)}, bf16[2,32,256]{2,1,0:T(8,128)(2,1)S(1)}, u32[]{:S(2)}, u32[]{:S(2)}) collective-permute-start(bf16[2,32,256]{2,1,0:T(8,128)(2,1)S(1)} %get-tuple-element.45), channel_id=1, source_target_pairs={{0,20},{1,16},{2,4},{3,0},{4,28},{5,24},{6,12},{7,8},{8,21},{9,17}... | collective-permute-start | bytes 98312 | tf_op jit(solution)/shard_map/ppermute | solution.py:252
  59.3 1.6 %collective-permute-start.20 = (f32[2,32,256]{2,1,0:T(8,128)S(1)}, f32[2,32,256]{2,1,0:T(8,128)S(1)}, u32[]{:S(2)}, u32[]{:S(2)}) collective-permute-start(f32[2,32,256]{2,1,0:T(8,128)S(1)} %convert_add_fusion.2.refs_8_), channel_id=1, source_target_pairs={{0,4},{1,5},{2,6},{3,7},{4,0},{5,1},{6,2},{7,3},{8,12},{9,13},{10,... | collective-permute-start | bytes 196616 | tf_op jit(solution)/shard_map/ppermute | solution.py:258
  61.2 4.4 %collective-permute-start.21 = (bf16[2,32,256]{2,1,0:T(8,128)(2,1)S(1)}, bf16[2,32,256]{2,1,0:T(8,128)(2,1)S(1)}, u32[]{:S(2)}, u32[]{:S(2)}) collective-permute-start(bf16[2,32,256]{2,1,0:T(8,128)(2,1)S(1)} %get-tuple-element.47), channel_id=1, source_target_pairs={{0,4},{1,0},{2,20},{3,16},{4,12},{5,8},{6,28},{7,24},{8,5},{9,1},{... | collective-permute-start | bytes 98312 | tf_op jit(solution)/shard_map/ppermute | solution.py:252
  61.6 8.7 %collective-permute-start.22 = (bf16[2,32,256]{2,1,0:T(8,128)(2,1)S(1)}, bf16[2,32,256]{2,1,0:T(8,128)(2,1)S(1)}, u32[]{:S(2)}, u32[]{:S(2)}) collective-permute-start(bf16[2,32,256]{2,1,0:T(8,128)(2,1)S(1)} %get-tuple-element.47), channel_id=1, source_target_pairs={{0,20},{1,16},{2,4},{3,0},{4,28},{5,24},{6,12},{7,8},{8,21},{9,17}... | collective-permute-start | bytes 98312 | tf_op jit(solution)/shard_map/ppermute | solution.py:252
  70.3 1.3 %collective-permute-start.23 = (f32[2,32,256]{2,1,0:T(8,128)S(1)}, f32[2,32,256]{2,1,0:T(8,128)S(1)}, u32[]{:S(2)}, u32[]{:S(2)}) collective-permute-start(f32[2,32,256]{2,1,0:T(8,128)S(1)} %convert_add_fusion.1.refs_8_), channel_id=1, source_target_pairs={{0,4},{1,5},{2,6},{3,7},{4,0},{5,1},{6,2},{7,3},{8,12},{9,13},{10,... | collective-permute-start | bytes 196616 | tf_op jit(solution)/shard_map/ppermute | solution.py:258
  72.2 3.9 %collective-permute-start.24 = (bf16[2,32,256]{2,1,0:T(8,128)(2,1)S(1)}, bf16[2,32,256]{2,1,0:T(8,128)(2,1)S(1)}, u32[]{:S(2)}, u32[]{:S(2)}) collective-permute-start(bf16[2,32,256]{2,1,0:T(8,128)(2,1)S(1)} %get-tuple-element.49), channel_id=1, source_target_pairs={{0,4},{1,0},{2,20},{3,16},{4,12},{5,8},{6,28},{7,24},{8,5},{9,1},{... | collective-permute-start | bytes 98312 | tf_op jit(solution)/shard_map/ppermute | solution.py:252
  72.3 8.0 %collective-permute-start.25 = (bf16[2,32,256]{2,1,0:T(8,128)(2,1)S(1)}, bf16[2,32,256]{2,1,0:T(8,128)(2,1)S(1)}, u32[]{:S(2)}, u32[]{:S(2)}) collective-permute-start(bf16[2,32,256]{2,1,0:T(8,128)(2,1)S(1)} %get-tuple-element.49), channel_id=1, source_target_pairs={{0,20},{1,16},{2,4},{3,0},{4,28},{5,24},{6,12},{7,8},{8,21},{9,17}... | collective-permute-start | bytes 98312 | tf_op jit(solution)/shard_map/ppermute | solution.py:252
  80.4 1.3 %collective-permute-start.26 = (f32[2,32,256]{2,1,0:T(8,128)S(1)}, f32[2,32,256]{2,1,0:T(8,128)S(1)}, u32[]{:S(2)}, u32[]{:S(2)}) collective-permute-start(f32[2,32,256]{2,1,0:T(8,128)S(1)} %convert_add_fusion.refs_8_), channel_id=1, source_target_pairs={{0,4},{1,5},{2,6},{3,7},{4,0},{5,1},{6,2},{7,3},{8,12},{9,13},{10,... | collective-permute-start | bytes 196616 | tf_op jit(solution)/shard_map/ppermute | solution.py:258
  82.6 8.8 %collective-permute-start.30 = (bf16[5,32,256]{2,1,0:T(8,128)(2,1)S(1)}, bf16[5,32,256]{2,1,0:T(8,128)(2,1)S(1)}, u32[]{:S(2)}, u32[]{:S(2)}) collective-permute-start(bf16[5,32,256]{2,1,0:T(8,128)(2,1)S(1)} %get-tuple-element.53), channel_id=1, source_target_pairs={{0,4},{1,13},{2,22},{3,31},{4,0},{5,9},{6,18},{7,27},{8,5},{9,12},... | collective-permute-start | bytes 245768 | tf_op jit(solution)/shard_map/ppermute | solution.py:310
  82.8 3.8 %collective-permute-start.27 = (bf16[32,256]{1,0:T(8,128)(2,1)S(1)}, bf16[32,256]{1,0:T(8,128)(2,1)S(1)}, u32[]{:S(2)}, u32[]{:S(2)}) collective-permute-start(bf16[32,256]{1,0:T(8,128)(2,1)S(1)} %get-tuple-element.52), channel_id=1, source_target_pairs={{0,5},{1,4},{2,7},{3,6},{4,1},{5,0},{6,3},{7,2},{8,13},{9,12},{10,... | collective-permute-start | bytes 49160 | tf_op jit(solution)/shard_map/ppermute | solution.py:311
  82.8 5.4 %collective-permute-start.28 = (bf16[32,256]{1,0:T(8,128)(2,1)S(1)}, bf16[32,256]{1,0:T(8,128)(2,1)S(1)}, u32[]{:S(2)}, u32[]{:S(2)}) collective-permute-start(bf16[32,256]{1,0:T(8,128)(2,1)S(1)} %get-tuple-element.51.refs_0_), channel_id=1, source_target_pairs={{0,2},{1,3},{2,0},{3,1},{4,6},{5,7},{6,4},{7,5},{8,10},{9,11},{10,... | collective-permute-start | bytes 49160 | tf_op jit(solution)/shard_map/ppermute | solution.py:311
  86.3 5.1 %collective-permute-start.29 = (bf16[32,256]{1,0:T(8,128)(2,1)S(1)}, bf16[32,256]{1,0:T(8,128)(2,1)S(1)}, u32[]{:S(2)}, u32[]{:S(2)}) collective-permute-start(bf16[32,256]{1,0:T(8,128)(2,1)S(1)} %get-tuple-element.52), channel_id=1, source_target_pairs={{0,7},{1,6},{2,5},{3,4},{4,3},{5,2},{6,1},{7,0},{8,15},{9,14},{10,... | collective-permute-start | bytes 49160 | tf_op jit(solution)/shard_map/ppermute | solution.py:311
  (4 other events, 6.9 us)

commit v3 on v2

--- a/solution.py
+++ b/solution.py
@@ -44,11 +44,11 @@
 
 
 def turn_perm(n):
-    return perm(n, lambda q, k, z: (z, k ^ 1, q ^ z))
+    return perm(n, lambda q, k, z: (z, k ^ 1, q ^ (n - 1)))
 
 
 def far_perm(n):
-    return perm(n, lambda q, k, z: (q ^ z, k ^ 1, q))
+    return perm(n, lambda q, k, z: (z ^ (n - 1), k ^ 1, q))
 
 
 def core_perm(n):
@@ -107,55 +107,68 @@
     return outs
 
 
-def start_kernel(pattern, rhs, inv, mine, keep_ref, give_ref, rhs_in, inv_in, mine_in, sems):
-    copies = [
-        pltpu.make_async_copy(source.at[0], target, sems.at[i])
-        for i, (source, target) in enumerate(((rhs, rhs_in), (inv, inv_in), (mine, mine_in)))
-    ]
-    for copy in copies:
-        copy.start()
+def start_kernel(pattern, rhs, inv, last, mine, keep_ref, give_ref, last_ref):
+    low = last.shape[1] // 2
+    last_ref[:low] = last[0, low:, :]
+    last_ref[low:, :low] = last[0, : low // 2, :low]
+    last_ref[low:, low:] = last[0, low // 2 : low, :low]
+    y = bf16(dot(rhs[0], inv[0], NT))
+    keep_ref[0] = f32(y)
+    for t in range(2):
+        keep_ref[1 + t] = dot(y, mine[0, t], NT) * f32(pattern[t, 0, 0])
     for i in range(keep_ref.shape[1]):
         value = f32(pattern[i % 2, 0, i // 2]) if i < 2 * pattern.shape[2] else 0.0
         keep_ref[3, pl.ds(i, 1), :] = jnp.full((1, keep_ref.shape[2]), value, jnp.float32)
+    give_ref[...] = keep_ref[...]
+
+
+def start_all(sems, moves):
+    copies = [pltpu.make_async_copy(a, b, sems.at[i]) for i, (a, b) in enumerate(moves)]
+    for copy in copies:
+        copy.start()
+    return copies
+
+
+def near_kernel(mine, keep_in, gotten_in, inv_in, other_in, keep, gotten, inv, other, y_ref, sum_ref, sems):
+    pairs = [pair_index(2, 0), pair_index(2, 1)]
+    moves = [(keep_in, keep), (gotten_in, gotten), (inv_in.at[1], inv.at[1])]
+    copies = start_all(sems, moves + [(other_in.at[p], other.at[p]) for p in pairs])
     for copy in copies:
         copy.wait()
-    y = bf16(dot(rhs_in[...], inv_in[...], NT))
-    keep_ref[0] = f32(y)
-    for t in range(2):
-        keep_ref[1 + t] = dot(y, mine_in[t], NT) * f32(pattern[t, 0, 0])
-    give_ref[...] = keep_ref[...]
-
-
-def join_kernel(keep, gotten, inv, mine, y_ref, msg_ref):
-    del inv, mine
     k, _ = place()
-    y_ref[k] = bf16(keep[0])
-    y_ref[1 - k] = bf16(gotten[0])
-    for t in range(2):
-        msg_ref[t] = bf16(keep[1 + t] + gotten[1 + t])
-
-
-def stage_kernel(*refs):
-    count = (len(refs) - 1) // 2
-    sems, copies = refs[-1], []
-    for source, target in zip(refs[:count], refs[count:-1], strict=True):
-        for i in range(source.shape[0]):
-            copies.append(pltpu.make_async_copy(source.at[i], target.at[i], sems.at[len(copies)]))
-    for copy in copies:
-        copy.start()
-    for copy in copies:
+    y_ref[k], y_ref[1 - k] = bf16(keep[0]), bf16(gotten[0])
+    for t, part in enumerate(lower_part(k, pairs[:1], [y_ref], mine, other, keep, gotten)):
+        sum_ref[t] = part
+
+
+def rest_kernel(keep, gotten, mine, y0, y1, inv_in, other_in, inv, other, sum_ref, sems):
+    pairs = [pair_index(3, 0), pair_index(3, 1)]
+    order = pairs + [p for p in range(other.shape[0]) if p not in pairs]
+    moves = [(other_in.at[p], other.at[p]) for p in order] + [(inv_in.at[i], inv.at[i]) for i in range(inv.shape[0])]
+    copies = start_all(sems, moves)
+    for copy in copies[:2]:
         copy.wait()
-
-
-def down_kernel(level, pairs, *refs):
-    keep, gotten, rhs, rhs_other, inv, inv_other, mine, other, some, rest = refs[:10]
-    earlier = refs[10 : 10 + level]
-    y_ref, msg_ref, total_ref = refs[10 + level :]
+    for t, part in enumerate(lower_part(place()[0], pairs, [y0, y1], mine, other, keep, gotten)):
+        sum_ref[t] = part
+    for copy in copies[2:]:
+        copy.wait()
+
+
+def ahead_kernel(keep, gotten, mine, other, y0, y1, y2, sum_ref):
+    pairs = [pair_index(4, b) for b in range(3)]
+    for t, part in enumerate(lower_part(place()[0], pairs, [y0, y1, y2], mine, other, keep, gotten)):
+        sum_ref[t] = part
+
+
+def down_kernel(level, pair, *refs):
+    keep, gotten, rhs, rhs_other, inv, inv_other, mine, other, ahead, some, rest = refs[:11]
+    y_ref, msg_ref, total_ref = refs[11:]
     k, diagonal = place()
     total_ref[...] = some[...] + rest[...]
     for at, b, inverse in ((k, rhs, inv), (1 - k, rhs_other, inv_other)):
         y_ref[at] = bf16(dot(bf16(f32(b[level]) - total_ref[at]), inverse[level], NT))
-    parts = lower_part(k, pairs, list(earlier) + [y_ref], mine, other, keep, gotten)
+    parts = lower_part(k, [pair], [y_ref], mine, other, keep, gotten)
+    parts = [ahead[t] + part for t, part in enumerate(parts)]
     if level == 3:
         total_ref[k], total_ref[1 - k] = f32(rhs[4]), f32(rhs_other[4])
         parts = [jnp.where(diagonal, p - total_ref[t], p) for t, p in enumerate(parts)]
@@ -175,12 +188,18 @@
 def turn_kernel(n, pairs, *refs):
     keep, gotten, inv_k, inv_o, inv, inv_other, mine, other, y3, own = refs[:10]
     got = refs[10 : 10 + n - 1]
-    y_ref, x_ref, msg_ref = refs[10 + n - 1 :]
+    y_ref, x_ref, msg_ref, whole_k, whole_o = refs[10 + n - 1 :]
     k, diagonal = place()
+    low = whole_k.shape[0] // 2
+    for packed, inverse in ((inv_k, whole_k), (inv_o, whole_o)):
+        inverse[low:, :] = packed[:low]
+        inverse[: low // 2, :low] = packed[low:, :low]
+        inverse[low // 2 : low, :low] = packed[low:, low:]
+        inverse[:low, low:] = jnp.zeros_like(inverse[:low, low:])
     x_ref[...] = bf16(-tree([f32(own[...])] + [f32(g[...]) for g in got]))
-    for at, inverse in ((k, inv_k), (1 - k, inv_o)):
+    for at, inverse in ((k, whole_k), (1 - k, whole_o)):
         y_ref[at] = bf16(dot(x_ref[at], inverse[...], NT))
-    for at, inverse in ((k, inv_k), (1 - k, inv_o)):
+    for at, inverse in ((k, whole_k), (1 - k, whole_o)):
         x_ref[at] = bf16(dot(y_ref[at], inverse[...], NN))
     for at, part in up_parts(k, diagonal, 3, pairs, [x_ref], y3, (mine, other, keep, gotten), inv, inv_other):
         msg_ref[at] = part
@@ -230,10 +249,10 @@
 ROOM = pltpu.CompilerParams(vmem_limit_bytes=16 * 1024 * 1024)
 
 
-def call(body, outs, args, scratch=()):
+def call(body, outs, args, scratch=(), dtype=jnp.bfloat16):
     return pl.pallas_call(
         body,
-        out_shape=[jax.ShapeDtypeStruct(s, jnp.bfloat16) for s in outs],
+        out_shape=[jax.ShapeDtypeStruct(s, dtype) for s in outs],
         in_specs=[VMEM] * len(args),
         out_specs=[VMEM] * len(outs),
         scratch_shapes=list(scratch),
@@ -257,47 +276,66 @@
         some = tree([f32(g) for g in got])
         return got, some, swap(some)
 
-    last, rhs_first = lax.optimization_barrier((inv[4], rhs))
+    first = lambda x, at: pl.BlockSpec((1, *x.shape[1:]), lambda i: (at,) + (0,) * (len(x.shape) - 1))
+    keep, give, last = pl.pallas_call(
+        start_kernel,
+        grid=(1,),
+        out_shape=[jax.ShapeDtypeStruct(slots, jnp.float32)] * 2 + [jax.ShapeDtypeStruct((3 * width // 4, width), inv.dtype)],
+        in_specs=[pl.BlockSpec(memory_space=pltpu.SMEM), first(rhs, 0), first(inv, 0), first(inv, 4), first(mine, 0)],
+        out_specs=[VMEM] * 3,
+        compiler_params=pltpu.CompilerParams(vmem_limit_bytes=61 * 1024 * 1024),
+    )(pattern.transpose(1, 2, 0), rhs, inv, inv, mine)
+    gotten = swap(give)
+    inv_s, mine_s, rhs_s, _ = lax.optimization_barrier((inv, mine, rhs, gotten))
+    inv_o, other, rhs_o = swap(inv_s), swap(mine_s), swap(rhs_s)
     inv_to = lax.ppermute(last, BOTH, far_perm(n))
-    inv_o, other, rhs_o = swap(inv), swap(mine), swap(rhs)
-    keep, give = pl.pallas_call(
-        start_kernel,
-        out_shape=[jax.ShapeDtypeStruct(slots, jnp.float32)] * 2,
-        in_specs=[pl.BlockSpec(memory_space=pltpu.SMEM), ANY, ANY, ANY],
-        out_specs=[VMEM] * 2,
-        scratch_shapes=[pltpu.VMEM(a.shape[1:], a.dtype) for a in (rhs, inv, mine)] + [pltpu.SemaphoreType.DMA((3,))],
-        compiler_params=ROOM,
-    )(pattern.transpose(1, 2, 0), rhs_first, inv, mine)
-    gotten = swap(give)
 
     y = [None] * 5
     x = [None] * 5
-    y[0], msg = call(join_kernel, [vec, vec], (keep, gotten, inv, mine))
+    msg = bf16(keep[1:3] + gotten[1:3])
     for level in range(1, 4):
         got, some, rest = share(msg, down_perms(n))
+        early, solved, _ = lax.optimization_barrier(((inv_o, other), y[:level], got[0]))
         if level == 1:
-            inv_o, other, _ = lax.optimization_barrier((inv_o, other, got[0]))
-            inv_o, other = pl.pallas_call(
-                stage_kernel,
-                out_shape=[jax.ShapeDtypeStruct(a.shape, a.dtype) for a in (inv_o, other)],
-                in_specs=[ANY] * 2,
-                out_specs=[VMEM] * 2,
+            inv_near, other_near = early
+            keep, gotten, inv_near, other_near, y[0], ahead = pl.pallas_call(
+                near_kernel,
+                out_shape=[jax.ShapeDtypeStruct(a.shape, a.dtype) for a in (keep, gotten, inv_o, other)]
+                + [jax.ShapeDtypeStruct(vec, jnp.bfloat16), jax.ShapeDtypeStruct(vec, jnp.float32)],
+                in_specs=[VMEM] + [ANY] * 4,
+                out_specs=[VMEM] * 6,
+                scratch_shapes=[pltpu.SemaphoreType.DMA((5,))],
+                compiler_params=ROOM,
+            )(mine, keep, gotten, *early)
+            held = inv_near, other_near
+        elif level == 2:
+            *held, ahead = pl.pallas_call(
+                rest_kernel,
+                out_shape=[jax.ShapeDtypeStruct(a.shape, a.dtype) for a in (inv_o, other)]
+                + [jax.ShapeDtypeStruct(vec, jnp.float32)],
+                in_specs=[VMEM] * 5 + [ANY] * 2,
+                out_specs=[VMEM] * 3,
                 scratch_shapes=[pltpu.SemaphoreType.DMA((inv_o.shape[0] + other.shape[0],))],
                 compiler_params=ROOM,
-            )(inv_o, other)
-            inv_tk = swap(inv_to)
-        pairs = [pair_index(level + 1, b) for b in range(level + 1)]
+            )(keep, gotten, mine, *solved, *early)
+            inv_o, other = held
+        else:
+            (ahead,) = call(ahead_kernel, [vec], (keep, gotten, mine, other, *solved), dtype=jnp.float32)
         y[level], msg = call(
-            functools.partial(down_kernel, level, pairs),
+            functools.partial(down_kernel, level, pair_index(level + 1, level)),
             [vec, vec],
-            (keep, gotten, rhs, rhs_o, inv, inv_o, mine, other, some, rest, *y[:level]),
+            (keep, gotten, rhs, rhs_o, inv, held[0], mine, held[1], ahead, some, rest),
             [pltpu.VMEM(vec, jnp.float32)],
         )
+        if level == 1:
+            msg, inv_to = lax.optimization_barrier((msg, inv_to))
+            inv_tk = swap(inv_to)
     got = send(msg, plane_perms(n))
     y[4], x[4], msg = call(
         functools.partial(turn_kernel, n, [pair_index(4, 3)]),
         [vec, vec, vec],
         (keep, gotten, inv_tk, inv_to, inv, inv_o, mine, other, y[3], msg, *got),
+        [pltpu.VMEM((width, width), inv.dtype)] * 2,
     )
     for level in (3, 2, 1):
         got, some, rest = share(msg, up_perms(n))

time: 92.5 us -> 85.1 us (0.920)
  starting transfers between devices: 41.6 us -> 37.8 us
  local copies, waits for them, and re-layouts: 4.42 us -> 0.97 us
  Pallas kernels: 10.8 us -> 9.66 us
    ppermute x15, starting transfers between devices: 33.5 us -> 23.1 us  [on_device(): send = lambda x, perms: [lax.ppermute(x, BOTH, p) for p in perms]]
    ppermute x15, waiting for transfers between devices: 22.7 us -> 27.5 us  [on_device(): send = lambda x, perms: [lax.ppermute(x, BOTH, p) for p in perms]]
    ppermute x1, starting transfers between devices: 0.16 us -> 4.87 us  [on_device(): moved = lax.ppermute(more[1], BOTH, turn_perm(n))]
    ppermute x3, waiting for transfers between devices: 4.76 us -> 1.7 us  [on_device(): lax.ppermute(more[0] if m & 1 else msg, BOTH, p)]
    unnamed x10 -> x8, local copies, waits for them, and re-layouts: 3.51 us -> 0.97 us
    ppermute x6, waiting for transfers between devices: 5.88 us -> 3.56 us  [share(): return (got, some, swap(some))]
    ppermute x1, starting transfers between devices: 0.01 us -> 2.22 us  [on_device(): inv_to = lax.ppermute(last, BOTH, far_perm(n))]
    ppermute x3, starting transfers between devices: 2.54 us -> 0.51 us  [on_device(): inv_o, other, rhs_o = (swap(inv_s), swap(mine_s), swap(rhs_s))]
  transfers between devices with their start and end apart: 31 -> 31, of which waited for: 18 -> 19; matrix products, arithmetic and copies ran while one was open for 1% -> 1% of each run, Pallas kernels for 7% -> 4%
where the time goes in v3:
time: 85.1 us; the launch traced here: 85 us
  starting transfers between devices  37.8 us (44%)
  waiting for transfers between devices  34.7 us (41%)
  Pallas kernels  9.66 us (11%)
  local copies, waits for them, and re-layouts  0.97 us (1%)
  other arithmetic  0.91 us (1%)
    ppermute x15, waiting for transfers between devices, on_device(): send = lambda x, perms: [lax.ppermute(x, BOTH, p) for p in perms]  27.5 us
    ppermute x15, starting transfers between devices, on_device(): send = lambda x, perms: [lax.ppermute(x, BOTH, p) for p in perms]  23.1 us
    ppermute x1, starting transfers between devices, on_device(): moved = lax.ppermute(more[1], BOTH, turn_perm(n))  4.87 us
    pallas_call x8, Pallas kernels, call(): pl.pallas_call(body, out_shape=[jax.ShapeDtypeStruct(s, dtype) for s in o...  4.18 us
    ppermute x3, starting transfers between devices, on_device(): lax.ppermute(more[0] if m & 1 else msg, BOTH, p)  3.83 us
    ppermute x6, waiting for transfers between devices, share(): return (got, some, swap(some))  3.56 us
    ppermute x6, starting transfers between devices, share(): return (got, some, swap(some))  2.38 us
    pallas_call x1, Pallas kernels, on_device(): pl.pallas_call(start_kernel, grid=(1,), out_shape=[jax.ShapeDtypeStruct(s...  2.35 us
  transfers between devices with their start and end apart: 31, of which 19 were waited for; matrix products, arithmetic and copies ran while one was open for 1% of the time, Pallas kernels for 4%

profile of v3, /device:TPU:0, one launch (start us, length us, event | category | flops | bytes accessed | tf_op | source)
XLA Modules:
  0.0 85.0 jit_solution(3579074680090738853)
XLA Ops:
  0.6 2.4 %shard_map.59 = (f32[4,32,256]{2,1,0:T(8,128)}, f32[4,32,256]{2,1,0:T(8,128)}, bf16[192,256]{1,0:T(8,128)(2,1)}) custom-call(s32[2,1,10]{2,1,0:T(1,128)} %bitcast.31, bf16[5,32,256]{2,1,0:T(8,128)(2,1)} %bitcast.26, bf16[5,256,256]{2,1,0:T(8,128)(2,1)} %bitcast.16, bf16[5,256,256]{2,1,0:T(8,128)(2,1)} %bitcast.17, bf16[10,2,256,256]{3,2,1,0:T(8,128)(2,1)} %bitcast.4), custom_call_target="tpu_custom_call" | custom-call | tf_op jit(solution)/shard_map/pallas_call | solution.py:280
  3.5 1.2 %collective-permute-done.gotten_in = f32[4,32,256]{2,1,0:T(8,128)S(1)} collective-permute-done((f32[4,32,256]{2,1,0:T(8,128)}, f32[4,32,256]{2,1,0:T(8,128)S(1)}, u32[]{:S(2)}, u32[]{:S(2)}) %collective-permute-start) | collective-permute-done | bytes 131104 | tf_op jit(solution)/shard_map/ppermute | solution.py:288
  6.4 4.5 %collective-permute-start.5 = (bf16[2,32,256]{2,1,0:T(8,128)(2,1)S(1)}, bf16[2,32,256]{2,1,0:T(8,128)(2,1)S(1)}, u32[]{:S(2)}, u32[]{:S(2)}) collective-permute-start(bf16[2,32,256]{2,1,0:T(8,128)(2,1)S(1)} %fusion), channel_id=1, source_target_pairs={{0,6},{1,14},{2,22},{3,30},{4,7},{5,15},{6,23},{7,31},{8,2},{9,10}... | collective-permute-start | bytes 98312 | tf_op jit(solution)/shard_map/ppermute | solution.py:271
  10.9 2.2 %collective-permute-start.7 = (bf16[192,256]{1,0:T(8,128)(2,1)}, bf16[192,256]{1,0:T(8,128)(2,1)S(1)}, u32[]{:S(2)}, u32[]{:S(2)}) collective-permute-start(bf16[192,256]{1,0:T(8,128)(2,1)} %get-tuple-element.59), channel_id=1, source_target_pairs={{0,28},{1,20},{2,12},{3,4},{4,24},{5,16},{6,8},{7,0},{8,29},{9,21}... | collective-permute-start | bytes 294920 | tf_op jit(solution)/shard_map/ppermute | solution.py:291
  13.1 1.1 %collective-permute-done.5 = bf16[2,32,256]{2,1,0:T(8,128)(2,1)S(1)} collective-permute-done((bf16[2,32,256]{2,1,0:T(8,128)(2,1)S(1)}, bf16[2,32,256]{2,1,0:T(8,128)(2,1)S(1)}, u32[]{:S(2)}, u32[]{:S(2)}) %collective-permute-start.5) | collective-permute-done | bytes 32800 | tf_op jit(solution)/shard_map/ppermute | solution.py:271
  14.4 1.0 %copy-done.3 = f32[4,32,256]{2,1,0:T(8,128)S(1)} copy-done((f32[4,32,256]{2,1,0:T(8,128)S(1)}, f32[4,32,256]{2,1,0:T(8,128)}, u32[]{:S(2)}) %copy-start.3) | copy-done | bytes 131096
  17.4 1.9 %collective-permute-start.10 = (bf16[2,32,256]{2,1,0:T(8,128)(2,1)S(1)}, bf16[2,32,256]{2,1,0:T(8,128)(2,1)S(1)}, u32[]{:S(2)}, u32[]{:S(2)}) collective-permute-start(bf16[2,32,256]{2,1,0:T(8,128)(2,1)S(1)} %get-tuple-element.60), channel_id=1, source_target_pairs={{0,6},{1,14},{2,22},{3,30},{4,7},{5,15},{6,23},{7,31},{8,2},{9,10}... | collective-permute-start | bytes 98312 | tf_op jit(solution)/shard_map/ppermute | solution.py:271
  19.3 2.4 %collective-permute-start.8 = (bf16[2,32,256]{2,1,0:T(8,128)(2,1)S(1)}, bf16[2,32,256]{2,1,0:T(8,128)(2,1)S(1)}, u32[]{:S(2)}, u32[]{:S(2)}) collective-permute-start(bf16[2,32,256]{2,1,0:T(8,128)(2,1)S(1)} %get-tuple-element.60), channel_id=1, source_target_pairs={{0,4},{1,12},{2,20},{3,28},{4,5},{5,13},{6,21},{7,29},{8,0},{9,8},... | collective-permute-start | bytes 98312 | tf_op jit(solution)/shard_map/ppermute | solution.py:271
  21.7 2.1 %collective-permute-done.10 = bf16[2,32,256]{2,1,0:T(8,128)(2,1)S(1)} collective-permute-done((bf16[2,32,256]{2,1,0:T(8,128)(2,1)S(1)}, bf16[2,32,256]{2,1,0:T(8,128)(2,1)S(1)}, u32[]{:S(2)}, u32[]{:S(2)}) %collective-permute-start.10) | collective-permute-done | bytes 32800 | tf_op jit(solution)/shard_map/ppermute | solution.py:271
  23.8 1.6 %collective-permute-start.11 = (f32[2,32,256]{2,1,0:T(8,128)S(1)}, f32[2,32,256]{2,1,0:T(8,128)S(1)}, u32[]{:S(2)}, u32[]{:S(2)}) collective-permute-start(f32[2,32,256]{2,1,0:T(8,128)S(1)} %convert_add_fusion.4.refs_9_), channel_id=1, source_target_pairs={{0,4},{1,5},{2,6},{3,7},{4,0},{5,1},{6,2},{7,3},{8,12},{9,13},{10,... | collective-permute-start | bytes 196616 | tf_op jit(solution)/shard_map/ppermute | solution.py:277
  25.4 1.6 %shard_map.62 = (bf16[5,256,256]{2,1,0:T(8,128)(2,1)S(1)}, bf16[10,2,256,256]{3,2,1,0:T(8,128)(2,1)S(1)}, f32[2,32,256]{2,1,0:T(8,128)S(1)}) custom-call(f32[4,32,256]{2,1,0:T(8,128)S(1)} %get-tuple-element.50.refs_0_.keep, f32[4,32,256]{2,1,0:T(8,128)S(1)} %get-tuple-element.51.refs_1_.gotten, bf16[10,2,256,256]{3,2,1,0:T(8,128)(2,1)S(1)} %bitcast.8, ...), custom_call_target="tpu_custom_call" | custom-call | tf_op jit(solution)/shard_map/pallas_call | solution.py:312
  27.5 5.2 %collective-permute-start.13 = (bf16[2,32,256]{2,1,0:T(8,128)(2,1)S(1)}, bf16[2,32,256]{2,1,0:T(8,128)(2,1)S(1)}, u32[]{:S(2)}, u32[]{:S(2)}) collective-permute-start(bf16[2,32,256]{2,1,0:T(8,128)(2,1)S(1)} %get-tuple-element.70), channel_id=1, source_target_pairs={{0,6},{1,14},{2,22},{3,30},{4,7},{5,15},{6,23},{7,31},{8,2},{9,10}... | collective-permute-start | bytes 98312 | tf_op jit(solution)/shard_map/ppermute | solution.py:271
  32.7 3.5 %collective-permute-done.13 = bf16[2,32,256]{2,1,0:T(8,128)(2,1)S(1)} collective-permute-done((bf16[2,32,256]{2,1,0:T(8,128)(2,1)S(1)}, bf16[2,32,256]{2,1,0:T(8,128)(2,1)S(1)}, u32[]{:S(2)}, u32[]{:S(2)}) %collective-permute-start.13) | collective-permute-done | bytes 32800 | tf_op jit(solution)/shard_map/ppermute | solution.py:271
  38.0 1.3 %collective-permute-start.15 = (bf16[2,32,256]{2,1,0:T(8,128)(2,1)S(1)}, bf16[2,32,256]{2,1,0:T(8,128)(2,1)S(1)}, u32[]{:S(2)}, u32[]{:S(2)}) collective-permute-start(bf16[2,32,256]{2,1,0:T(8,128)(2,1)S(1)} %get-tuple-element.75.refs_9_), channel_id=1, source_target_pairs={{0,12},{1,13},{2,14},{3,15},{4,8},{5,9},{6,10},{7,11},{8,4},{9,5},... | collective-permute-start | bytes 98312 | tf_op jit(solution)/shard_map/ppermute | solution.py:271
  39.2 2.9 %collective-permute-start.16 = (bf16[2,32,256]{2,1,0:T(8,128)(2,1)S(1)}, bf16[2,32,256]{2,1,0:T(8,128)(2,1)S(1)}, u32[]{:S(2)}, u32[]{:S(2)}) collective-permute-start(bf16[2,32,256]{2,1,0:T(8,128)(2,1)S(1)} %get-tuple-element.75.refs_9_), channel_id=1, source_target_pairs={{0,20},{1,21},{2,22},{3,23},{4,16},{5,17},{6,18},{7,19},{8,28},{9,... | collective-permute-start | bytes 98312 | tf_op jit(solution)/shard_map/ppermute | solution.py:271
  42.3 1.4 %collective-permute-done.16.refs_11_ = bf16[2,32,256]{2,1,0:T(8,128)(2,1)S(1)} collective-permute-done((bf16[2,32,256]{2,1,0:T(8,128)(2,1)S(1)}, bf16[2,32,256]{2,1,0:T(8,128)(2,1)S(1)}, u32[]{:S(2)}, u32[]{:S(2)}) %collective-permute-start.16) | collective-permute-done | bytes 32800 | tf_op jit(solution)/shard_map/ppermute | solution.py:271
  43.7 3.2 %collective-permute-done.17.refs_12_ = bf16[2,32,256]{2,1,0:T(8,128)(2,1)S(1)} collective-permute-done((bf16[2,32,256]{2,1,0:T(8,128)(2,1)S(1)}, bf16[2,32,256]{2,1,0:T(8,128)(2,1)S(1)}, u32[]{:S(2)}, u32[]{:S(2)}) %collective-permute-start.17) | collective-permute-done | bytes 32800 | tf_op jit(solution)/shard_map/ppermute | solution.py:271
  48.1 4.0 %collective-permute-done.18 = bf16[2,32,256]{2,1,0:T(8,128)(2,1)S(1)} collective-permute-done((bf16[2,32,256]{2,1,0:T(8,128)(2,1)S(1)}, bf16[2,32,256]{2,1,0:T(8,128)(2,1)S(1)}, u32[]{:S(2)}, u32[]{:S(2)}) %collective-permute-start.18) | collective-permute-done | bytes 32800 | tf_op jit(solution)/shard_map/ppermute | solution.py:271
  52.1 1.5 %collective-permute-done.19 = bf16[2,32,256]{2,1,0:T(8,128)(2,1)S(1)} collective-permute-done((bf16[2,32,256]{2,1,0:T(8,128)(2,1)S(1)}, bf16[2,32,256]{2,1,0:T(8,128)(2,1)S(1)}, u32[]{:S(2)}, u32[]{:S(2)}) %collective-permute-start.19) | collective-permute-done | bytes 32800 | tf_op jit(solution)/shard_map/ppermute | solution.py:271
  53.7 1.2 %collective-permute-done.20.refs_9_ = f32[2,32,256]{2,1,0:T(8,128)S(1)} collective-permute-done((f32[2,32,256]{2,1,0:T(8,128)S(1)}, f32[2,32,256]{2,1,0:T(8,128)S(1)}, u32[]{:S(2)}, u32[]{:S(2)}) %collective-permute-start.20) | collective-permute-done | bytes 65568 | tf_op jit(solution)/shard_map/ppermute | solution.py:277
  55.5 1.7 %collective-permute-start.22 = (bf16[2,32,256]{2,1,0:T(8,128)(2,1)S(1)}, bf16[2,32,256]{2,1,0:T(8,128)(2,1)S(1)}, u32[]{:S(2)}, u32[]{:S(2)}) collective-permute-start(bf16[2,32,256]{2,1,0:T(8,128)(2,1)S(1)} %get-tuple-element.79), channel_id=1, source_target_pairs={{0,20},{1,16},{2,4},{3,0},{4,28},{5,24},{6,12},{7,8},{8,21},{9,17}... | collective-permute-start | bytes 98312 | tf_op jit(solution)/shard_map/ppermute | solution.py:271
  57.1 2.4 %collective-permute-done.21 = bf16[2,32,256]{2,1,0:T(8,128)(2,1)S(1)} collective-permute-done((bf16[2,32,256]{2,1,0:T(8,128)(2,1)S(1)}, bf16[2,32,256]{2,1,0:T(8,128)(2,1)S(1)}, u32[]{:S(2)}, u32[]{:S(2)}) %collective-permute-start.21) | collective-permute-done | bytes 32800 | tf_op jit(solution)/shard_map/ppermute | solution.py:271
  59.5 3.7 %collective-permute-done.22 = bf16[2,32,256]{2,1,0:T(8,128)(2,1)S(1)} collective-permute-done((bf16[2,32,256]{2,1,0:T(8,128)(2,1)S(1)}, bf16[2,32,256]{2,1,0:T(8,128)(2,1)S(1)}, u32[]{:S(2)}, u32[]{:S(2)}) %collective-permute-start.22) | collective-permute-done | bytes 32800 | tf_op jit(solution)/shard_map/ppermute | solution.py:271
  63.4 1.2 %collective-permute-done.23.refs_9_ = f32[2,32,256]{2,1,0:T(8,128)S(1)} collective-permute-done((f32[2,32,256]{2,1,0:T(8,128)S(1)}, f32[2,32,256]{2,1,0:T(8,128)S(1)}, u32[]{:S(2)}, u32[]{:S(2)}) %collective-permute-start.23) | collective-permute-done | bytes 65568 | tf_op jit(solution)/shard_map/ppermute | solution.py:277
  65.3 1.7 %collective-permute-start.25 = (bf16[2,32,256]{2,1,0:T(8,128)(2,1)S(1)}, bf16[2,32,256]{2,1,0:T(8,128)(2,1)S(1)}, u32[]{:S(2)}, u32[]{:S(2)}) collective-permute-start(bf16[2,32,256]{2,1,0:T(8,128)(2,1)S(1)} %get-tuple-element.81), channel_id=1, source_target_pairs={{0,20},{1,16},{2,4},{3,0},{4,28},{5,24},{6,12},{7,8},{8,21},{9,17}... | collective-permute-start | bytes 98312 | tf_op jit(solution)/shard_map/ppermute | solution.py:271
  67.0 2.0 %collective-permute-done.24 = bf16[2,32,256]{2,1,0:T(8,128)(2,1)S(1)} collective-permute-done((bf16[2,32,256]{2,1,0:T(8,128)(2,1)S(1)}, bf16[2,32,256]{2,1,0:T(8,128)(2,1)S(1)}, u32[]{:S(2)}, u32[]{:S(2)}) %collective-permute-start.24) | collective-permute-done | bytes 32800 | tf_op jit(solution)/shard_map/ppermute | solution.py:271
  69.0 2.5 %collective-permute-done.25 = bf16[2,32,256]{2,1,0:T(8,128)(2,1)S(1)} collective-permute-done((bf16[2,32,256]{2,1,0:T(8,128)(2,1)S(1)}, bf16[2,32,256]{2,1,0:T(8,128)(2,1)S(1)}, u32[]{:S(2)}, u32[]{:S(2)}) %collective-permute-start.25) | collective-permute-done | bytes 32800 | tf_op jit(solution)/shard_map/ppermute | solution.py:271
  72.0 0.9 %collective-permute-done.26.refs_9_ = f32[2,32,256]{2,1,0:T(8,128)S(1)} collective-permute-done((f32[2,32,256]{2,1,0:T(8,128)S(1)}, f32[2,32,256]{2,1,0:T(8,128)S(1)}, u32[]{:S(2)}, u32[]{:S(2)}) %collective-permute-start.26) | collective-permute-done | bytes 65568 | tf_op jit(solution)/shard_map/ppermute | solution.py:277
  72.9 1.0 %shard_map.69 = (bf16[2,32,256]{2,1,0:T(8,128)(2,1)}, bf16[32,256]{1,0:T(8,128)(2,1)S(1)}, bf16[32,256]{1,0:T(8,128)(2,1)S(1)}, bf16[5,32,256]{2,1,0:T(8,128)(2,1)S(1)}) custom-call(f32[4,32,256]{2,1,0:T(8,128)S(1)} %get-tuple-element.50.refs_0_.keep, f32[4,32,256]{2,1,0:T(8,128)S(1)} %get-tuple-element.51.refs_1_.gotten, bf16[5,256,256]{2,1,0:T(8,128)(2,1)S(1)} %bitcast.25, ...), custom_call_target="tpu_custom_call" | custom-call | tf_op jit(solution)/shard_map/pallas_call | solution.py:253
  73.9 4.9 %collective-permute-start.30 = (bf16[5,32,256]{2,1,0:T(8,128)(2,1)S(1)}, bf16[5,32,256]{2,1,0:T(8,128)(2,1)S(1)}, u32[]{:S(2)}, u32[]{:S(2)}) collective-permute-start(bf16[5,32,256]{2,1,0:T(8,128)(2,1)S(1)} %get-tuple-element.85), channel_id=1, source_target_pairs={{0,7},{1,15},{2,23},{3,31},{4,3},{5,11},{6,19},{7,27},{8,6},{9,14}... | collective-permute-start | bytes 245768 | tf_op jit(solution)/shard_map/ppermute | solution.py:348
  79.3 3.3 %collective-permute-start.29 = (bf16[32,256]{1,0:T(8,128)(2,1)S(1)}, bf16[32,256]{1,0:T(8,128)(2,1)S(1)}, u32[]{:S(2)}, u32[]{:S(2)}) collective-permute-start(bf16[32,256]{1,0:T(8,128)(2,1)S(1)} %get-tuple-element.84), channel_id=1, source_target_pairs={{0,7},{1,6},{2,5},{3,4},{4,3},{5,2},{6,1},{7,0},{8,15},{9,14},{10,... | collective-permute-start | bytes 49160 | tf_op jit(solution)/shard_map/ppermute | solution.py:349
  83.4 0.9 %collective-permute-done.29.refs_3_ = bf16[32,256]{1,0:T(8,128)(2,1)S(1)} collective-permute-done((bf16[32,256]{1,0:T(8,128)(2,1)S(1)}, bf16[32,256]{1,0:T(8,128)(2,1)S(1)}, u32[]{:S(2)}, u32[]{:S(2)}) %collective-permute-start.29) | collective-permute-done | bytes 16416 | tf_op jit(solution)/shard_map/ppermute | solution.py:349
  (57 shorter events, 11.8 us)
Async XLA Ops:
  0.6 12.5 %copy-start.2 = (bf16[5,1,32,256]{3,2,1,0:T(8,128)(2,1)S(1)}, bf16[5,1,32,256]{3,2,1,0:T(8,128)(2,1)}, u32[]{:S(2)}) copy-start(bf16[5,1,32,256]{3,2,1,0:T(8,128)(2,1)} %param.4) | copy-start | bytes 245764
  3.0 1.6 %collective-permute-start = (f32[4,32,256]{2,1,0:T(8,128)}, f32[4,32,256]{2,1,0:T(8,128)S(1)}, u32[]{:S(2)}, u32[]{:S(2)}) collective-permute-start(f32[4,32,256]{2,1,0:T(8,128)} %get-tuple-element.45), channel_id=1, source_target_pairs={{0,4},{1,5},{2,6},{3,7},{4,0},{5,1},{6,2},{7,3},{8,12},{9,13},{10,... | collective-permute-start | bytes 393224 | tf_op jit(solution)/shard_map/ppermute | solution.py:288
  4.7 9.7 %collective-permute-start.2 = (bf16[10,2,256,256]{3,2,1,0:T(8,128)(2,1)S(1)}, bf16[10,2,256,256]{3,2,1,0:T(8,128)(2,1)S(1)}, u32[]{:S(2)}, u32[]{:S(2)}) collective-permute-start(bf16[10,2,256,256]{3,2,1,0:T(8,128)(2,1)S(1)} %bitcast.5), channel_id=1, source_target_pairs={{0,4},{1,5},{2,6},{3,7},{4,0},{5,1},{6,2},{7,3},{8,12},{9,13},{10,... | collective-permute-start | bytes 7864328 | tf_op jit(solution)/shard_map/ppermute | solution.py:290
  5.0 9.4 %collective-permute-start.1 = (bf16[5,256,256]{2,1,0:T(8,128)(2,1)}, bf16[5,256,256]{2,1,0:T(8,128)(2,1)S(1)}, u32[]{:S(2)}, u32[]{:S(2)}) collective-permute-start(bf16[5,256,256]{2,1,0:T(8,128)(2,1)} %bitcast.18), channel_id=1, source_target_pairs={{0,4},{1,5},{2,6},{3,7},{4,0},{5,1},{6,2},{7,3},{8,12},{9,13},{10,... | collective-permute-start | bytes 1966088 | tf_op jit(solution)/shard_map/ppermute | solution.py:290
  6.0 7.1 %collective-permute-start.3 = (bf16[2,32,256]{2,1,0:T(8,128)(2,1)S(1)}, bf16[2,32,256]{2,1,0:T(8,128)(2,1)S(1)}, u32[]{:S(2)}, u32[]{:S(2)}) collective-permute-start(bf16[2,32,256]{2,1,0:T(8,128)(2,1)S(1)} %fusion), channel_id=1, source_target_pairs={{0,4},{1,12},{2,20},{3,28},{4,5},{5,13},{6,21},{7,29},{8,0},{9,8},... | collective-permute-start | bytes 98312 | tf_op jit(solution)/shard_map/ppermute | solution.py:271
  6.4 7.8 %collective-permute-start.5 = (bf16[2,32,256]{2,1,0:T(8,128)(2,1)S(1)}, bf16[2,32,256]{2,1,0:T(8,128)(2,1)S(1)}, u32[]{:S(2)}, u32[]{:S(2)}) collective-permute-start(bf16[2,32,256]{2,1,0:T(8,128)(2,1)S(1)} %fusion), channel_id=1, source_target_pairs={{0,6},{1,14},{2,22},{3,30},{4,7},{5,15},{6,23},{7,31},{8,2},{9,10}... | collective-permute-start | bytes 98312 | tf_op jit(solution)/shard_map/ppermute | solution.py:271
  10.9 6.5 %collective-permute-start.7 = (bf16[192,256]{1,0:T(8,128)(2,1)}, bf16[192,256]{1,0:T(8,128)(2,1)S(1)}, u32[]{:S(2)}, u32[]{:S(2)}) collective-permute-start(bf16[192,256]{1,0:T(8,128)(2,1)} %get-tuple-element.59), channel_id=1, source_target_pairs={{0,28},{1,20},{2,12},{3,4},{4,24},{5,16},{6,8},{7,0},{8,29},{9,21}... | collective-permute-start | bytes 294920 | tf_op jit(solution)/shard_map/ppermute | solution.py:291
  13.1 3.1 %collective-permute-start.4 = (bf16[5,32,256]{2,1,0:T(8,128)(2,1)S(1)}, bf16[5,32,256]{2,1,0:T(8,128)(2,1)S(1)}, u32[]{:S(2)}, u32[]{:S(2)}) collective-permute-start(bf16[5,32,256]{2,1,0:T(8,128)(2,1)S(1)} %bitcast.27), channel_id=1, source_target_pairs={{0,4},{1,5},{2,6},{3,7},{4,0},{5,1},{6,2},{7,3},{8,12},{9,13},{10,... | collective-permute-start | bytes 245768 | tf_op jit(solution)/shard_map/ppermute | solution.py:290
  14.3 1.9 %collective-permute-start.6 = (f32[2,32,256]{2,1,0:T(8,128)S(1)}, f32[2,32,256]{2,1,0:T(8,128)S(1)}, u32[]{:S(2)}, u32[]{:S(2)}) collective-permute-start(f32[2,32,256]{2,1,0:T(8,128)S(1)} %convert_add_fusion.5.refs_9_), channel_id=1, source_target_pairs={{0,4},{1,5},{2,6},{3,7},{4,0},{5,1},{6,2},{7,3},{8,12},{9,13},{10,... | collective-permute-start | bytes 196616 | tf_op jit(solution)/shard_map/ppermute | solution.py:277
  17.4 6.4 %collective-permute-start.10 = (bf16[2,32,256]{2,1,0:T(8,128)(2,1)S(1)}, bf16[2,32,256]{2,1,0:T(8,128)(2,1)S(1)}, u32[]{:S(2)}, u32[]{:S(2)}) collective-permute-start(bf16[2,32,256]{2,1,0:T(8,128)(2,1)S(1)} %get-tuple-element.60), channel_id=1, source_target_pairs={{0,6},{1,14},{2,22},{3,30},{4,7},{5,15},{6,23},{7,31},{8,2},{9,10}... | collective-permute-start | bytes 98312 | tf_op jit(solution)/shard_map/ppermute | solution.py:271
  19.3 4.5 %collective-permute-start.8 = (bf16[2,32,256]{2,1,0:T(8,128)(2,1)S(1)}, bf16[2,32,256]{2,1,0:T(8,128)(2,1)S(1)}, u32[]{:S(2)}, u32[]{:S(2)}) collective-permute-start(bf16[2,32,256]{2,1,0:T(8,128)(2,1)S(1)} %get-tuple-element.60), channel_id=1, source_target_pairs={{0,4},{1,12},{2,20},{3,28},{4,5},{5,13},{6,21},{7,29},{8,0},{9,8},... | collective-permute-start | bytes 98312 | tf_op jit(solution)/shard_map/ppermute | solution.py:271
  23.8 3.2 %collective-permute-start.11 = (f32[2,32,256]{2,1,0:T(8,128)S(1)}, f32[2,32,256]{2,1,0:T(8,128)S(1)}, u32[]{:S(2)}, u32[]{:S(2)}) collective-permute-start(f32[2,32,256]{2,1,0:T(8,128)S(1)} %convert_add_fusion.4.refs_9_), channel_id=1, source_target_pairs={{0,4},{1,5},{2,6},{3,7},{4,0},{5,1},{6,2},{7,3},{8,12},{9,13},{10,... | collective-permute-start | bytes 196616 | tf_op jit(solution)/shard_map/ppermute | solution.py:277
  27.4 5.3 %collective-permute-start.12 = (bf16[2,32,256]{2,1,0:T(8,128)(2,1)S(1)}, bf16[2,32,256]{2,1,0:T(8,128)(2,1)S(1)}, u32[]{:S(2)}, u32[]{:S(2)}) collective-permute-start(bf16[2,32,256]{2,1,0:T(8,128)(2,1)S(1)} %get-tuple-element.70), channel_id=1, source_target_pairs={{0,4},{1,12},{2,20},{3,28},{4,5},{5,13},{6,21},{7,29},{8,0},{9,8},... | collective-permute-start | bytes 98312 | tf_op jit(solution)/shard_map/ppermute | solution.py:271
  27.5 8.7 %collective-permute-start.13 = (bf16[2,32,256]{2,1,0:T(8,128)(2,1)S(1)}, bf16[2,32,256]{2,1,0:T(8,128)(2,1)S(1)}, u32[]{:S(2)}, u32[]{:S(2)}) collective-permute-start(bf16[2,32,256]{2,1,0:T(8,128)(2,1)S(1)} %get-tuple-element.70), channel_id=1, source_target_pairs={{0,6},{1,14},{2,22},{3,30},{4,7},{5,15},{6,23},{7,31},{8,2},{9,10}... | collective-permute-start | bytes 98312 | tf_op jit(solution)/shard_map/ppermute | solution.py:271
  36.2 1.3 %collective-permute-start.14 = (f32[2,32,256]{2,1,0:T(8,128)S(1)}, f32[2,32,256]{2,1,0:T(8,128)S(1)}, u32[]{:S(2)}, u32[]{:S(2)}) collective-permute-start(f32[2,32,256]{2,1,0:T(8,128)S(1)} %convert_add_fusion.3.refs_9_), channel_id=1, source_target_pairs={{0,4},{1,5},{2,6},{3,7},{4,0},{5,1},{6,2},{7,3},{8,12},{9,13},{10,... | collective-permute-start | bytes 196616 | tf_op jit(solution)/shard_map/ppermute | solution.py:277
  36.3 6.0 %collective-permute-start.9 = (bf16[192,256]{1,0:T(8,128)(2,1)S(1)}, bf16[192,256]{1,0:T(8,128)(2,1)S(1)}, u32[]{:S(2)}, u32[]{:S(2)}) collective-permute-start(bf16[192,256]{1,0:T(8,128)(2,1)S(1)} %collective-permute-done.7.refs_3_), channel_id=1, source_target_pairs={{0,4},{1,5},{2,6},{3,7},{4,0},{5,1},{6,2},{7,3},{8,12},{9,13},{10,... | collective-permute-start | bytes 294920 | tf_op jit(solution)/shard_map/ppermute | solution.py:332
  38.0 4.4 %collective-permute-start.15 = (bf16[2,32,256]{2,1,0:T(8,128)(2,1)S(1)}, bf16[2,32,256]{2,1,0:T(8,128)(2,1)S(1)}, u32[]{:S(2)}, u32[]{:S(2)}) collective-permute-start(bf16[2,32,256]{2,1,0:T(8,128)(2,1)S(1)} %get-tuple-element.75.refs_9_), channel_id=1, source_target_pairs={{0,12},{1,13},{2,14},{3,15},{4,8},{5,9},{6,10},{7,11},{8,4},{9,5},... | collective-permute-start | bytes 98312 | tf_op jit(solution)/shard_map/ppermute | solution.py:271
  39.2 4.5 %collective-permute-start.16 = (bf16[2,32,256]{2,1,0:T(8,128)(2,1)S(1)}, bf16[2,32,256]{2,1,0:T(8,128)(2,1)S(1)}, u32[]{:S(2)}, u32[]{:S(2)}) collective-permute-start(bf16[2,32,256]{2,1,0:T(8,128)(2,1)S(1)} %get-tuple-element.75.refs_9_), channel_id=1, source_target_pairs={{0,20},{1,21},{2,22},{3,23},{4,16},{5,17},{6,18},{7,19},{8,28},{9,... | collective-permute-start | bytes 98312 | tf_op jit(solution)/shard_map/ppermute | solution.py:271
  42.1 4.8 %collective-permute-start.17 = (bf16[2,32,256]{2,1,0:T(8,128)(2,1)S(1)}, bf16[2,32,256]{2,1,0:T(8,128)(2,1)S(1)}, u32[]{:S(2)}, u32[]{:S(2)}) collective-permute-start(bf16[2,32,256]{2,1,0:T(8,128)(2,1)S(1)} %get-tuple-element.75.refs_9_), channel_id=1, source_target_pairs={{0,24},{1,25},{2,26},{3,27},{4,28},{5,29},{6,30},{7,31},{8,16},{9,... | collective-permute-start | bytes 98312 | tf_op jit(solution)/shard_map/ppermute | solution.py:271
  47.5 4.5 %collective-permute-start.18 = (bf16[2,32,256]{2,1,0:T(8,128)(2,1)S(1)}, bf16[2,32,256]{2,1,0:T(8,128)(2,1)S(1)}, u32[]{:S(2)}, u32[]{:S(2)}) collective-permute-start(bf16[2,32,256]{2,1,0:T(8,128)(2,1)S(1)} %get-tuple-element.77), channel_id=1, source_target_pairs={{0,4},{1,0},{2,20},{3,16},{4,12},{5,8},{6,28},{7,24},{8,5},{9,1},{... | collective-permute-start | bytes 98312 | tf_op jit(solution)/shard_map/ppermute | solution.py:271
  47.6 6.0 %collective-permute-start.19 = (bf16[2,32,256]{2,1,0:T(8,128)(2,1)S(1)}, bf16[2,32,256]{2,1,0:T(8,128)(2,1)S(1)}, u32[]{:S(2)}, u32[]{:S(2)}) collective-permute-start(bf16[2,32,256]{2,1,0:T(8,128)(2,1)S(1)} %get-tuple-element.77), channel_id=1, source_target_pairs={{0,20},{1,16},{2,4},{3,0},{4,28},{5,24},{6,12},{7,8},{8,21},{9,17}... | collective-permute-start | bytes 98312 | tf_op jit(solution)/shard_map/ppermute | solution.py:271
  53.6 1.3 %collective-permute-start.20 = (f32[2,32,256]{2,1,0:T(8,128)S(1)}, f32[2,32,256]{2,1,0:T(8,128)S(1)}, u32[]{:S(2)}, u32[]{:S(2)}) collective-permute-start(f32[2,32,256]{2,1,0:T(8,128)S(1)} %convert_add_fusion.2.refs_8_), channel_id=1, source_target_pairs={{0,4},{1,5},{2,6},{3,7},{4,0},{5,1},{6,2},{7,3},{8,12},{9,13},{10,... | collective-permute-start | bytes 196616 | tf_op jit(solution)/shard_map/ppermute | solution.py:277
  55.3 4.2 %collective-permute-start.21 = (bf16[2,32,256]{2,1,0:T(8,128)(2,1)S(1)}, bf16[2,32,256]{2,1,0:T(8,128)(2,1)S(1)}, u32[]{:S(2)}, u32[]{:S(2)}) collective-permute-start(bf16[2,32,256]{2,1,0:T(8,128)(2,1)S(1)} %get-tuple-element.79), channel_id=1, source_target_pairs={{0,4},{1,0},{2,20},{3,16},{4,12},{5,8},{6,28},{7,24},{8,5},{9,1},{... | collective-permute-start | bytes 98312 | tf_op jit(solution)/shard_map/ppermute | solution.py:271
  55.5 7.8 %collective-permute-start.22 = (bf16[2,32,256]{2,1,0:T(8,128)(2,1)S(1)}, bf16[2,32,256]{2,1,0:T(8,128)(2,1)S(1)}, u32[]{:S(2)}, u32[]{:S(2)}) collective-permute-start(bf16[2,32,256]{2,1,0:T(8,128)(2,1)S(1)} %get-tuple-element.79), channel_id=1, source_target_pairs={{0,20},{1,16},{2,4},{3,0},{4,28},{5,24},{6,12},{7,8},{8,21},{9,17}... | collective-permute-start | bytes 98312 | tf_op jit(solution)/shard_map/ppermute | solution.py:271
  63.3 1.3 %collective-permute-start.23 = (f32[2,32,256]{2,1,0:T(8,128)S(1)}, f32[2,32,256]{2,1,0:T(8,128)S(1)}, u32[]{:S(2)}, u32[]{:S(2)}) collective-permute-start(f32[2,32,256]{2,1,0:T(8,128)S(1)} %convert_add_fusion.1.refs_8_), channel_id=1, source_target_pairs={{0,4},{1,5},{2,6},{3,7},{4,0},{5,1},{6,2},{7,3},{8,12},{9,13},{10,... | collective-permute-start | bytes 196616 | tf_op jit(solution)/shard_map/ppermute | solution.py:277
  65.1 3.9 %collective-permute-start.24 = (bf16[2,32,256]{2,1,0:T(8,128)(2,1)S(1)}, bf16[2,32,256]{2,1,0:T(8,128)(2,1)S(1)}, u32[]{:S(2)}, u32[]{:S(2)}) collective-permute-start(bf16[2,32,256]{2,1,0:T(8,128)(2,1)S(1)} %get-tuple-element.81), channel_id=1, source_target_pairs={{0,4},{1,0},{2,20},{3,16},{4,12},{5,8},{6,28},{7,24},{8,5},{9,1},{... | collective-permute-start | bytes 98312 | tf_op jit(solution)/shard_map/ppermute | solution.py:271
  65.3 6.2 %collective-permute-start.25 = (bf16[2,32,256]{2,1,0:T(8,128)(2,1)S(1)}, bf16[2,32,256]{2,1,0:T(8,128)(2,1)S(1)}, u32[]{:S(2)}, u32[]{:S(2)}) collective-permute-start(bf16[2,32,256]{2,1,0:T(8,128)(2,1)S(1)} %get-tuple-element.81), channel_id=1, source_target_pairs={{0,20},{1,16},{2,4},{3,0},{4,28},{5,24},{6,12},{7,8},{8,21},{9,17}... | collective-permute-start | bytes 98312 | tf_op jit(solution)/shard_map/ppermute | solution.py:271
  71.5 1.4 %collective-permute-start.26 = (f32[2,32,256]{2,1,0:T(8,128)S(1)}, f32[2,32,256]{2,1,0:T(8,128)S(1)}, u32[]{:S(2)}, u32[]{:S(2)}) collective-permute-start(f32[2,32,256]{2,1,0:T(8,128)S(1)} %convert_add_fusion.refs_8_), channel_id=1, source_target_pairs={{0,4},{1,5},{2,6},{3,7},{4,0},{5,1},{6,2},{7,3},{8,12},{9,13},{10,... | collective-permute-start | bytes 196616 | tf_op jit(solution)/shard_map/ppermute | solution.py:277
  73.9 10.4 %collective-permute-start.30 = (bf16[5,32,256]{2,1,0:T(8,128)(2,1)S(1)}, bf16[5,32,256]{2,1,0:T(8,128)(2,1)S(1)}, u32[]{:S(2)}, u32[]{:S(2)}) collective-permute-start(bf16[5,32,256]{2,1,0:T(8,128)(2,1)S(1)} %get-tuple-element.85), channel_id=1, source_target_pairs={{0,7},{1,15},{2,23},{3,31},{4,3},{5,11},{6,19},{7,27},{8,6},{9,14}... | collective-permute-start | bytes 245768 | tf_op jit(solution)/shard_map/ppermute | solution.py:348
  78.7 3.8 %collective-permute-start.27 = (bf16[32,256]{1,0:T(8,128)(2,1)S(1)}, bf16[32,256]{1,0:T(8,128)(2,1)S(1)}, u32[]{:S(2)}, u32[]{:S(2)}) collective-permute-start(bf16[32,256]{1,0:T(8,128)(2,1)S(1)} %get-tuple-element.84), channel_id=1, source_target_pairs={{0,5},{1,4},{2,7},{3,6},{4,1},{5,0},{6,3},{7,2},{8,13},{9,12},{10,... | collective-permute-start | bytes 49160 | tf_op jit(solution)/shard_map/ppermute | solution.py:349
  78.7 4.6 %collective-permute-start.28 = (bf16[32,256]{1,0:T(8,128)(2,1)S(1)}, bf16[32,256]{1,0:T(8,128)(2,1)S(1)}, u32[]{:S(2)}, u32[]{:S(2)}) collective-permute-start(bf16[32,256]{1,0:T(8,128)(2,1)S(1)} %get-tuple-element.83.refs_0_), channel_id=1, source_target_pairs={{0,2},{1,3},{2,0},{3,1},{4,6},{5,7},{6,4},{7,5},{8,10},{9,11},{10,... | collective-permute-start | bytes 49160 | tf_op jit(solution)/shard_map/ppermute | solution.py:349
  79.3 5.0 %collective-permute-start.29 = (bf16[32,256]{1,0:T(8,128)(2,1)S(1)}, bf16[32,256]{1,0:T(8,128)(2,1)S(1)}, u32[]{:S(2)}, u32[]{:S(2)}) collective-permute-start(bf16[32,256]{1,0:T(8,128)(2,1)S(1)} %get-tuple-element.84), channel_id=1, source_target_pairs={{0,7},{1,6},{2,5},{3,4},{4,3},{5,2},{6,1},{7,0},{8,15},{9,14},{10,... | collective-permute-start | bytes 49160 | tf_op jit(solution)/shard_map/ppermute | solution.py:349
  (3 other events, 6.9 us)

commit v4 on v3

--- a/solution.py
+++ b/solution.py
@@ -32,15 +32,15 @@
 
 
 def up_perms(n):
-    return [perm(n, lambda q, k, z, j=j: (2 * ((z >> 1) ^ j) + k, (z & 1) ^ 1, q)) for j in range(n // 2)]
+    return [perm(n, lambda q, k, z, j=j: (2 * ((z >> 1) ^ j) + k, (z & 1) ^ 1, q)) for j in reversed(range(n // 2))]
 
 
 def plane_perms(n):
-    return [perm(n, lambda q, k, z, m=m: (q ^ m, k ^ (m.bit_count() & 1), z)) for m in range(1, n)]
+    return [perm(n, lambda q, k, z, m=m: (q ^ m, k ^ 1, z)) for m in range(1, n)]
 
 
 def line_perms(n):
-    return [perm(n, lambda q, k, z, m=m: (q, k ^ (m & 1), z ^ m)) for m in range(1, n)]
+    return [perm(n, lambda q, k, z, m=m: (q, k ^ 1, z ^ m)) for m in range(1, n)]
 
 
 def turn_perm(n):
@@ -176,8 +176,16 @@
         msg_ref[t] = bf16(part)
 
 
-def up_parts(k, diagonal, level, pairs, solved, y, factors, inv, inv_other):
+def above_kernel(pairs, *refs):
+    keep, gotten, mine, other = refs[:4]
+    for i, part in enumerate(upper_part(pairs, refs[4:-1], mine, other, keep, gotten)):
+        refs[-1][i] = part
+
+
+def up_parts(k, diagonal, level, pairs, solved, y, factors, inv, inv_other, ahead=None):
     parts = upper_part(pairs, solved, *factors)
+    if ahead is not None:
+        parts = [ahead[i] + part for i, part in enumerate(parts)]
     outs = []
     for part, at, inverse in zip(parts, (k, 1 - k), (inv, inv_other), strict=True):
         part = jnp.where(diagonal, part - f32(y[at]), part)
@@ -206,14 +214,15 @@
 
 
 def up_kernel(level, pairs, *refs):
-    keep, gotten, inv, inv_other, mine, other, below, y4, some, rest = refs[:10]
-    later = refs[10 : 14 - level]
-    outs = refs[14 - level :]
+    keep, gotten, inv, inv_other, mine, other, below, y4, some, rest, ahead = refs[:11]
+    later = refs[11 : 15 - level]
+    outs = refs[15 - level :]
     k, diagonal = place()
     x_ref = outs[0]
     x_ref[...] = bf16(-(some[...] + rest[...]))
     solved = list(later) + [x_ref]
-    parts = up_parts(k, diagonal, level - 1, pairs, solved, below, (mine, other, keep, gotten), inv, inv_other)
+    factors = (mine, other, keep, gotten)
+    parts = up_parts(k, diagonal, level - 1, pairs, [x_ref], below, factors, inv, inv_other, ahead)
     if level > 1:
         for at, part in parts:
             outs[1][at] = part
@@ -286,13 +295,13 @@
         compiler_params=pltpu.CompilerParams(vmem_limit_bytes=61 * 1024 * 1024),
     )(pattern.transpose(1, 2, 0), rhs, inv, inv, mine)
     gotten = swap(give)
-    inv_s, mine_s, rhs_s, _ = lax.optimization_barrier((inv, mine, rhs, gotten))
+    msg = bf16(keep[1:3] + gotten[1:3])
+    inv_s, mine_s, rhs_s, _ = lax.optimization_barrier((inv, mine, rhs, msg))
     inv_o, other, rhs_o = swap(inv_s), swap(mine_s), swap(rhs_s)
     inv_to = lax.ppermute(last, BOTH, far_perm(n))
 
     y = [None] * 5
     x = [None] * 5
-    msg = bf16(keep[1:3] + gotten[1:3])
     for level in range(1, 4):
         got, some, rest = share(msg, down_perms(n))
         early, solved, _ = lax.optimization_barrier(((inv_o, other), y[:level], got[0]))
@@ -339,14 +348,22 @@
     )
     for level in (3, 2, 1):
         got, some, rest = share(msg, up_perms(n))
-        pairs = [pair_index(c, level - 1) for c in range(4, level - 1, -1)]
+        later, _ = lax.optimization_barrier((x[4:level:-1], got[0]))
+        pairs = [pair_index(c, level - 1) for c in range(4, level, -1)]
+        (ahead,) = call(
+            functools.partial(above_kernel, pairs), [vec], (keep, gotten, mine, other, *later), dtype=jnp.float32
+        )
+        pairs = [pair_index(level, level - 1)]
         x[level], msg, *more = call(
             functools.partial(up_kernel, level, pairs),
             [vec, vec] if level > 1 else [vec, vec[1:], vec[1:], (5, *vec[1:])],
-            (keep, gotten, inv, inv_o, mine, other, y[level - 1], y[4], some, rest, *x[4:level:-1]),
+            (keep, gotten, inv, inv_o, mine, other, y[level - 1], y[4], some, rest, ahead, *x[4:level:-1]),
         )
     moved = lax.ppermute(more[1], BOTH, turn_perm(n))
-    got = [lax.ppermute(more[0] if m & 1 else msg, BOTH, p) for m, p in enumerate(line_perms(n), 1)]
+    lines = line_perms(n)
+    order = sorted(range(1, n), key=lambda m: (m & (m + 1) != 0, m))
+    got = {m: lax.ppermute(more[0], BOTH, lines[m - 1]) for m in order}
+    got = [got[m] for m in range(1, n)]
     out = jax.ShapeDtypeStruct((levels, 1, count, width), jnp.bfloat16)
     return pl.pallas_call(
         functools.partial(out_kernel, n),

time: 85.1 us -> 84.6 us (level)
  waiting for transfers between devices: 34.7 us -> 27.1 us
  starting transfers between devices: 37.8 us -> 44.4 us
    ppermute x15, waiting for transfers between devices: 27.5 us -> 20.6 us  [on_device(): send = lambda x, perms: [lax.ppermute(x, BOTH, p) for p in perms]]
    ppermute x15, starting transfers between devices: 23.1 us -> 28.7 us  [on_device(): send = lambda x, perms: [lax.ppermute(x, BOTH, p) for p in perms]]
    ppermute x1, starting transfers between devices: 4.87 us -> 6.12 us  [on_device(): moved = lax.ppermute(more[1], BOTH, turn_perm(n))]
    pallas_call x8 -> x11, Pallas kernels: 4.18 us -> 4.63 us  [call(): pl.pallas_call(body, out_shape=[jax.ShapeDtypeStruct(s, dtype) for s in o...]
  transfers between devices with their start and end apart: 31 -> 31, of which waited for: 19 -> 16; matrix products, arithmetic and copies ran while one was open for 1% -> 0% of each run, Pallas kernels for 4% -> 5%
where the time goes in v4:
time: 84.6 us; the launch traced here: 84.4 us
  starting transfers between devices  44.4 us (52%)
  waiting for transfers between devices  27.1 us (32%)
  Pallas kernels  10.1 us (12%)
  local copies, waits for them, and re-layouts  0.97 us (1%)
  other arithmetic  0.91 us (1%)
  between operations  0.89 us (1%)
    ppermute x15, starting transfers between devices, on_device(): send = lambda x, perms: [lax.ppermute(x, BOTH, p) for p in perms]  28.7 us
    ppermute x15, waiting for transfers between devices, on_device(): send = lambda x, perms: [lax.ppermute(x, BOTH, p) for p in perms]  20.6 us
    ppermute x1, starting transfers between devices, on_device(): moved = lax.ppermute(more[1], BOTH, turn_perm(n))  6.12 us
    pallas_call x11, Pallas kernels, call(): pl.pallas_call(body, out_shape=[jax.ShapeDtypeStruct(s, dtype) for s in o...  4.63 us
    ppermute x3, starting transfers between devices, on_device(): got = {m: lax.ppermute(more[0], BOTH, lines[m - 1]) for m in order}  3.87 us
    ppermute x6, waiting for transfers between devices, share(): return (got, some, swap(some))  3.01 us
    pallas_call x1, Pallas kernels, on_device(): pl.pallas_call(start_kernel, grid=(1,), out_shape=[jax.ShapeDtypeStruct(s...  2.35 us
    ppermute x1, starting transfers between devices, on_device(): inv_to = lax.ppermute(last, BOTH, far_perm(n))  2.22 us
  transfers between devices with their start and end apart: 31, of which 16 were waited for; matrix products, arithmetic and copies ran while one was open for 0% of the time, Pallas kernels for 5%

profile of v4, /device:TPU:0, one launch (start us, length us, event | category | flops | bytes accessed | tf_op | source)
XLA Modules:
  0.0 84.4 jit_solution(11327703380741352098)
XLA Ops:
  0.6 2.4 %shard_map.59 = (f32[4,32,256]{2,1,0:T(8,128)}, f32[4,32,256]{2,1,0:T(8,128)}, bf16[192,256]{1,0:T(8,128)(2,1)}) custom-call(s32[2,1,10]{2,1,0:T(1,128)} %bitcast.34, bf16[5,32,256]{2,1,0:T(8,128)(2,1)} %bitcast.29, bf16[5,256,256]{2,1,0:T(8,128)(2,1)} %bitcast.19, bf16[5,256,256]{2,1,0:T(8,128)(2,1)} %bitcast.20, bf16[10,2,256,256]{3,2,1,0:T(8,128)(2,1)} %bitcast.4), custom_call_target="tpu_custom_call" | custom-call | tf_op jit(solution)/shard_map/pallas_call | solution.py:289
  3.5 1.2 %collective-permute-done.gotten_in = f32[4,32,256]{2,1,0:T(8,128)S(1)} collective-permute-done((f32[4,32,256]{2,1,0:T(8,128)}, f32[4,32,256]{2,1,0:T(8,128)S(1)}, u32[]{:S(2)}, u32[]{:S(2)}) %collective-permute-start) | collective-permute-done | bytes 131104 | tf_op jit(solution)/shard_map/ppermute | solution.py:297
  4.7 0.8 %fusion = bf16[2,32,256]{2,1,0:T(8,128)(2,1)S(1)} fusion(f32[4,32,256]{2,1,0:T(8,128)S(1)} %collective-permute-done.gotten_in, f32[4,32,256]{2,1,0:T(8,128)} %get-tuple-element.50.keep_in), kind=kLoop, calls=%fused_computation.1 | loop fusion | flops 32768 | bytes 163840 | tf_op jit(solution)/shard_map/convert_element_type | solution.py:70
  6.5 4.5 %collective-permute-start.5 = (bf16[2,32,256]{2,1,0:T(8,128)(2,1)S(1)}, bf16[2,32,256]{2,1,0:T(8,128)(2,1)S(1)}, u32[]{:S(2)}, u32[]{:S(2)}) collective-permute-start(bf16[2,32,256]{2,1,0:T(8,128)(2,1)S(1)} %fusion), channel_id=1, source_target_pairs={{0,6},{1,14},{2,22},{3,30},{4,7},{5,15},{6,23},{7,31},{8,2},{9,10}... | collective-permute-start | bytes 98312 | tf_op jit(solution)/shard_map/ppermute | solution.py:280
  10.9 2.2 %collective-permute-start.7 = (bf16[192,256]{1,0:T(8,128)(2,1)}, bf16[192,256]{1,0:T(8,128)(2,1)S(1)}, u32[]{:S(2)}, u32[]{:S(2)}) collective-permute-start(bf16[192,256]{1,0:T(8,128)(2,1)} %get-tuple-element.65), channel_id=1, source_target_pairs={{0,28},{1,20},{2,12},{3,4},{4,24},{5,16},{6,8},{7,0},{8,29},{9,21}... | collective-permute-start | bytes 294920 | tf_op jit(solution)/shard_map/ppermute | solution.py:301
  13.1 1.1 %collective-permute-done.5 = bf16[2,32,256]{2,1,0:T(8,128)(2,1)S(1)} collective-permute-done((bf16[2,32,256]{2,1,0:T(8,128)(2,1)S(1)}, bf16[2,32,256]{2,1,0:T(8,128)(2,1)S(1)}, u32[]{:S(2)}, u32[]{:S(2)}) %collective-permute-start.5) | collective-permute-done | bytes 32800 | tf_op jit(solution)/shard_map/ppermute | solution.py:280
  14.4 1.0 %copy-done.3 = f32[4,32,256]{2,1,0:T(8,128)S(1)} copy-done((f32[4,32,256]{2,1,0:T(8,128)S(1)}, f32[4,32,256]{2,1,0:T(8,128)}, u32[]{:S(2)}) %copy-start.3) | copy-done | bytes 131096
  15.4 0.8 shard_map.60
  17.4 1.9 %collective-permute-start.10 = (bf16[2,32,256]{2,1,0:T(8,128)(2,1)S(1)}, bf16[2,32,256]{2,1,0:T(8,128)(2,1)S(1)}, u32[]{:S(2)}, u32[]{:S(2)}) collective-permute-start(bf16[2,32,256]{2,1,0:T(8,128)(2,1)S(1)} %get-tuple-element.66), channel_id=1, source_target_pairs={{0,6},{1,14},{2,22},{3,30},{4,7},{5,15},{6,23},{7,31},{8,2},{9,10}... | collective-permute-start | bytes 98312 | tf_op jit(solution)/shard_map/ppermute | solution.py:280
  19.3 2.4 %collective-permute-start.8 = (bf16[2,32,256]{2,1,0:T(8,128)(2,1)S(1)}, bf16[2,32,256]{2,1,0:T(8,128)(2,1)S(1)}, u32[]{:S(2)}, u32[]{:S(2)}) collective-permute-start(bf16[2,32,256]{2,1,0:T(8,128)(2,1)S(1)} %get-tuple-element.66), channel_id=1, source_target_pairs={{0,4},{1,12},{2,20},{3,28},{4,5},{5,13},{6,21},{7,29},{8,0},{9,8},... | collective-permute-start | bytes 98312 | tf_op jit(solution)/shard_map/ppermute | solution.py:280
  21.7 2.1 %collective-permute-done.10 = bf16[2,32,256]{2,1,0:T(8,128)(2,1)S(1)} collective-permute-done((bf16[2,32,256]{2,1,0:T(8,128)(2,1)S(1)}, bf16[2,32,256]{2,1,0:T(8,128)(2,1)S(1)}, u32[]{:S(2)}, u32[]{:S(2)}) %collective-permute-start.10) | collective-permute-done | bytes 32800 | tf_op jit(solution)/shard_map/ppermute | solution.py:280
  23.8 1.6 %collective-permute-start.11 = (f32[2,32,256]{2,1,0:T(8,128)S(1)}, f32[2,32,256]{2,1,0:T(8,128)S(1)}, u32[]{:S(2)}, u32[]{:S(2)}) collective-permute-start(f32[2,32,256]{2,1,0:T(8,128)S(1)} %convert_add_fusion.4.refs_9_), channel_id=1, source_target_pairs={{0,4},{1,5},{2,6},{3,7},{4,0},{5,1},{6,2},{7,3},{8,12},{9,13},{10,... | collective-permute-start | bytes 196616 | tf_op jit(solution)/shard_map/ppermute | solution.py:286
  25.4 1.6 %shard_map.62 = (bf16[5,256,256]{2,1,0:T(8,128)(2,1)S(1)}, bf16[10,2,256,256]{3,2,1,0:T(8,128)(2,1)S(1)}, f32[2,32,256]{2,1,0:T(8,128)S(1)}) custom-call(f32[4,32,256]{2,1,0:T(8,128)S(1)} %get-tuple-element.56.refs_0_.keep, f32[4,32,256]{2,1,0:T(8,128)S(1)} %get-tuple-element.57.refs_1_.gotten, bf16[10,2,256,256]{3,2,1,0:T(8,128)(2,1)S(1)} %bitcast.8, ...), custom_call_target="tpu_custom_call" | custom-call | tf_op jit(solution)/shard_map/pallas_call | solution.py:321
  27.5 5.2 %collective-permute-start.13 = (bf16[2,32,256]{2,1,0:T(8,128)(2,1)S(1)}, bf16[2,32,256]{2,1,0:T(8,128)(2,1)S(1)}, u32[]{:S(2)}, u32[]{:S(2)}) collective-permute-start(bf16[2,32,256]{2,1,0:T(8,128)(2,1)S(1)} %get-tuple-element.76), channel_id=1, source_target_pairs={{0,6},{1,14},{2,22},{3,30},{4,7},{5,15},{6,23},{7,31},{8,2},{9,10}... | collective-permute-start | bytes 98312 | tf_op jit(solution)/shard_map/ppermute | solution.py:280
  32.7 3.5 %collective-permute-done.13 = bf16[2,32,256]{2,1,0:T(8,128)(2,1)S(1)} collective-permute-done((bf16[2,32,256]{2,1,0:T(8,128)(2,1)S(1)}, bf16[2,32,256]{2,1,0:T(8,128)(2,1)S(1)}, u32[]{:S(2)}, u32[]{:S(2)}) %collective-permute-start.13) | collective-permute-done | bytes 32800 | tf_op jit(solution)/shard_map/ppermute | solution.py:280
  38.0 1.3 %collective-permute-start.15 = (bf16[2,32,256]{2,1,0:T(8,128)(2,1)S(1)}, bf16[2,32,256]{2,1,0:T(8,128)(2,1)S(1)}, u32[]{:S(2)}, u32[]{:S(2)}) collective-permute-start(bf16[2,32,256]{2,1,0:T(8,128)(2,1)S(1)} %get-tuple-element.81.refs_9_), channel_id=1, source_target_pairs={{0,12},{1,13},{2,14},{3,15},{4,8},{5,9},{6,10},{7,11},{8,4},{9,5},... | collective-permute-start | bytes 98312 | tf_op jit(solution)/shard_map/ppermute | solution.py:280
  39.2 2.9 %collective-permute-start.16 = (bf16[2,32,256]{2,1,0:T(8,128)(2,1)S(1)}, bf16[2,32,256]{2,1,0:T(8,128)(2,1)S(1)}, u32[]{:S(2)}, u32[]{:S(2)}) collective-permute-start(bf16[2,32,256]{2,1,0:T(8,128)(2,1)S(1)} %get-tuple-element.81.refs_9_), channel_id=1, source_target_pairs={{0,20},{1,21},{2,22},{3,23},{4,16},{5,17},{6,18},{7,19},{8,28},{9,... | collective-permute-start | bytes 98312 | tf_op jit(solution)/shard_map/ppermute | solution.py:280
  42.3 1.5 %collective-permute-done.16.refs_11_ = bf16[2,32,256]{2,1,0:T(8,128)(2,1)S(1)} collective-permute-done((bf16[2,32,256]{2,1,0:T(8,128)(2,1)S(1)}, bf16[2,32,256]{2,1,0:T(8,128)(2,1)S(1)}, u32[]{:S(2)}, u32[]{:S(2)}) %collective-permute-start.16) | collective-permute-done | bytes 32800 | tf_op jit(solution)/shard_map/ppermute | solution.py:280
  43.7 2.6 %collective-permute-done.17.refs_12_ = bf16[2,32,256]{2,1,0:T(8,128)(2,1)S(1)} collective-permute-done((bf16[2,32,256]{2,1,0:T(8,128)(2,1)S(1)}, bf16[2,32,256]{2,1,0:T(8,128)(2,1)S(1)}, u32[]{:S(2)}, u32[]{:S(2)}) %collective-permute-start.17) | collective-permute-done | bytes 32800 | tf_op jit(solution)/shard_map/ppermute | solution.py:280
  47.3 5.4 %collective-permute-done.18 = bf16[2,32,256]{2,1,0:T(8,128)(2,1)S(1)} collective-permute-done((bf16[2,32,256]{2,1,0:T(8,128)(2,1)S(1)}, bf16[2,32,256]{2,1,0:T(8,128)(2,1)S(1)}, u32[]{:S(2)}, u32[]{:S(2)}) %collective-permute-start.18) | collective-permute-done | bytes 32800 | tf_op jit(solution)/shard_map/ppermute | solution.py:280
  53.0 1.0 %collective-permute-done.20.refs_9_ = f32[2,32,256]{2,1,0:T(8,128)S(1)} collective-permute-done((f32[2,32,256]{2,1,0:T(8,128)S(1)}, f32[2,32,256]{2,1,0:T(8,128)S(1)}, u32[]{:S(2)}, u32[]{:S(2)}) %collective-permute-start.20) | collective-permute-done | bytes 65568 | tf_op jit(solution)/shard_map/ppermute | solution.py:286
  54.4 1.9 %collective-permute-start.21 = (bf16[2,32,256]{2,1,0:T(8,128)(2,1)S(1)}, bf16[2,32,256]{2,1,0:T(8,128)(2,1)S(1)}, u32[]{:S(2)}, u32[]{:S(2)}) collective-permute-start(bf16[2,32,256]{2,1,0:T(8,128)(2,1)S(1)} %get-tuple-element.86), channel_id=1, source_target_pairs={{0,20},{1,16},{2,4},{3,0},{4,28},{5,24},{6,12},{7,8},{8,21},{9,17}... | collective-permute-start | bytes 98312 | tf_op jit(solution)/shard_map/ppermute | solution.py:280
  56.3 2.9 %collective-permute-start.22 = (bf16[2,32,256]{2,1,0:T(8,128)(2,1)S(1)}, bf16[2,32,256]{2,1,0:T(8,128)(2,1)S(1)}, u32[]{:S(2)}, u32[]{:S(2)}) collective-permute-start(bf16[2,32,256]{2,1,0:T(8,128)(2,1)S(1)} %get-tuple-element.86), channel_id=1, source_target_pairs={{0,4},{1,0},{2,20},{3,16},{4,12},{5,8},{6,28},{7,24},{8,5},{9,1},{... | collective-permute-start | bytes 98312 | tf_op jit(solution)/shard_map/ppermute | solution.py:280
  59.2 2.2 %collective-permute-done.21 = bf16[2,32,256]{2,1,0:T(8,128)(2,1)S(1)} collective-permute-done((bf16[2,32,256]{2,1,0:T(8,128)(2,1)S(1)}, bf16[2,32,256]{2,1,0:T(8,128)(2,1)S(1)}, u32[]{:S(2)}, u32[]{:S(2)}) %collective-permute-start.21) | collective-permute-done | bytes 32800 | tf_op jit(solution)/shard_map/ppermute | solution.py:280
  61.7 0.9 %collective-permute-done.23.refs_9_ = f32[2,32,256]{2,1,0:T(8,128)S(1)} collective-permute-done((f32[2,32,256]{2,1,0:T(8,128)S(1)}, f32[2,32,256]{2,1,0:T(8,128)S(1)}, u32[]{:S(2)}, u32[]{:S(2)}) %collective-permute-start.23) | collective-permute-done | bytes 65568 | tf_op jit(solution)/shard_map/ppermute | solution.py:286
  63.0 1.7 %collective-permute-start.24 = (bf16[2,32,256]{2,1,0:T(8,128)(2,1)S(1)}, bf16[2,32,256]{2,1,0:T(8,128)(2,1)S(1)}, u32[]{:S(2)}, u32[]{:S(2)}) collective-permute-start(bf16[2,32,256]{2,1,0:T(8,128)(2,1)S(1)} %get-tuple-element.90), channel_id=1, source_target_pairs={{0,20},{1,16},{2,4},{3,0},{4,28},{5,24},{6,12},{7,8},{8,21},{9,17}... | collective-permute-start | bytes 98312 | tf_op jit(solution)/shard_map/ppermute | solution.py:280
  64.7 3.2 %collective-permute-start.25 = (bf16[2,32,256]{2,1,0:T(8,128)(2,1)S(1)}, bf16[2,32,256]{2,1,0:T(8,128)(2,1)S(1)}, u32[]{:S(2)}, u32[]{:S(2)}) collective-permute-start(bf16[2,32,256]{2,1,0:T(8,128)(2,1)S(1)} %get-tuple-element.90), channel_id=1, source_target_pairs={{0,4},{1,0},{2,20},{3,16},{4,12},{5,8},{6,28},{7,24},{8,5},{9,1},{... | collective-permute-start | bytes 98312 | tf_op jit(solution)/shard_map/ppermute | solution.py:280
  67.8 2.1 %collective-permute-done.24 = bf16[2,32,256]{2,1,0:T(8,128)(2,1)S(1)} collective-permute-done((bf16[2,32,256]{2,1,0:T(8,128)(2,1)S(1)}, bf16[2,32,256]{2,1,0:T(8,128)(2,1)S(1)}, u32[]{:S(2)}, u32[]{:S(2)}) %collective-permute-start.24) | collective-permute-done | bytes 32800 | tf_op jit(solution)/shard_map/ppermute | solution.py:280
  70.4 0.9 %collective-permute-done.26.refs_9_ = f32[2,32,256]{2,1,0:T(8,128)S(1)} collective-permute-done((f32[2,32,256]{2,1,0:T(8,128)S(1)}, f32[2,32,256]{2,1,0:T(8,128)S(1)}, u32[]{:S(2)}, u32[]{:S(2)}) %collective-permute-start.26) | collective-permute-done | bytes 65568 | tf_op jit(solution)/shard_map/ppermute | solution.py:286
  72.1 6.1 %collective-permute-start.30 = (bf16[5,32,256]{2,1,0:T(8,128)(2,1)S(1)}, bf16[5,32,256]{2,1,0:T(8,128)(2,1)S(1)}, u32[]{:S(2)}, u32[]{:S(2)}) collective-permute-start(bf16[5,32,256]{2,1,0:T(8,128)(2,1)S(1)} %get-tuple-element.97), channel_id=1, source_target_pairs={{0,7},{1,15},{2,23},{3,31},{4,3},{5,11},{6,19},{7,27},{8,6},{9,14}... | collective-permute-start | bytes 245768 | tf_op jit(solution)/shard_map/ppermute | solution.py:362
  78.6 3.5 %collective-permute-start.29 = (bf16[32,256]{1,0:T(8,128)(2,1)S(1)}, bf16[32,256]{1,0:T(8,128)(2,1)S(1)}, u32[]{:S(2)}, u32[]{:S(2)}) collective-permute-start(bf16[32,256]{1,0:T(8,128)(2,1)S(1)} %get-tuple-element.96), channel_id=1, source_target_pairs={{0,7},{1,6},{2,5},{3,4},{4,3},{5,2},{6,1},{7,0},{8,15},{9,14},{10,... | collective-permute-start | bytes 49160 | tf_op jit(solution)/shard_map/ppermute | solution.py:365
  82.3 1.4 %collective-permute-done.29.refs_3_ = bf16[32,256]{1,0:T(8,128)(2,1)S(1)} collective-permute-done((bf16[32,256]{1,0:T(8,128)(2,1)S(1)}, bf16[32,256]{1,0:T(8,128)(2,1)S(1)}, u32[]{:S(2)}, u32[]{:S(2)}) %collective-permute-start.29) | collective-permute-done | bytes 16416 | tf_op jit(solution)/shard_map/ppermute | solution.py:365
  (60 shorter events, 9.7 us)
Async XLA Ops:
  0.6 12.5 %copy-start.2 = (bf16[5,1,32,256]{3,2,1,0:T(8,128)(2,1)S(1)}, bf16[5,1,32,256]{3,2,1,0:T(8,128)(2,1)}, u32[]{:S(2)}) copy-start(bf16[5,1,32,256]{3,2,1,0:T(8,128)(2,1)} %param.4) | copy-start | bytes 245764
  3.0 1.6 %collective-permute-start = (f32[4,32,256]{2,1,0:T(8,128)}, f32[4,32,256]{2,1,0:T(8,128)S(1)}, u32[]{:S(2)}, u32[]{:S(2)}) collective-permute-start(f32[4,32,256]{2,1,0:T(8,128)} %get-tuple-element.51), channel_id=1, source_target_pairs={{0,4},{1,5},{2,6},{3,7},{4,0},{5,1},{6,2},{7,3},{8,12},{9,13},{10,... | collective-permute-start | bytes 393224 | tf_op jit(solution)/shard_map/ppermute | solution.py:297
  5.5 8.9 %collective-permute-start.2 = (bf16[10,2,256,256]{3,2,1,0:T(8,128)(2,1)S(1)}, bf16[10,2,256,256]{3,2,1,0:T(8,128)(2,1)S(1)}, u32[]{:S(2)}, u32[]{:S(2)}) collective-permute-start(bf16[10,2,256,256]{3,2,1,0:T(8,128)(2,1)S(1)} %bitcast.5), channel_id=1, source_target_pairs={{0,4},{1,5},{2,6},{3,7},{4,0},{5,1},{6,2},{7,3},{8,12},{9,13},{10,... | collective-permute-start | bytes 7864328 | tf_op jit(solution)/shard_map/ppermute | solution.py:300
  5.9 8.5 %collective-permute-start.1 = (bf16[5,256,256]{2,1,0:T(8,128)(2,1)}, bf16[5,256,256]{2,1,0:T(8,128)(2,1)S(1)}, u32[]{:S(2)}, u32[]{:S(2)}) collective-permute-start(bf16[5,256,256]{2,1,0:T(8,128)(2,1)} %bitcast.21), channel_id=1, source_target_pairs={{0,4},{1,5},{2,6},{3,7},{4,0},{5,1},{6,2},{7,3},{8,12},{9,13},{10,... | collective-permute-start | bytes 1966088 | tf_op jit(solution)/shard_map/ppermute | solution.py:300
  6.1 7.0 %collective-permute-start.3 = (bf16[2,32,256]{2,1,0:T(8,128)(2,1)S(1)}, bf16[2,32,256]{2,1,0:T(8,128)(2,1)S(1)}, u32[]{:S(2)}, u32[]{:S(2)}) collective-permute-start(bf16[2,32,256]{2,1,0:T(8,128)(2,1)S(1)} %fusion), channel_id=1, source_target_pairs={{0,4},{1,12},{2,20},{3,28},{4,5},{5,13},{6,21},{7,29},{8,0},{9,8},... | collective-permute-start | bytes 98312 | tf_op jit(solution)/shard_map/ppermute | solution.py:280
  6.5 7.8 %collective-permute-start.5 = (bf16[2,32,256]{2,1,0:T(8,128)(2,1)S(1)}, bf16[2,32,256]{2,1,0:T(8,128)(2,1)S(1)}, u32[]{:S(2)}, u32[]{:S(2)}) collective-permute-start(bf16[2,32,256]{2,1,0:T(8,128)(2,1)S(1)} %fusion), channel_id=1, source_target_pairs={{0,6},{1,14},{2,22},{3,30},{4,7},{5,15},{6,23},{7,31},{8,2},{9,10}... | collective-permute-start | bytes 98312 | tf_op jit(solution)/shard_map/ppermute | solution.py:280
  10.9 6.5 %collective-permute-start.7 = (bf16[192,256]{1,0:T(8,128)(2,1)}, bf16[192,256]{1,0:T(8,128)(2,1)S(1)}, u32[]{:S(2)}, u32[]{:S(2)}) collective-permute-start(bf16[192,256]{1,0:T(8,128)(2,1)} %get-tuple-element.65), channel_id=1, source_target_pairs={{0,28},{1,20},{2,12},{3,4},{4,24},{5,16},{6,8},{7,0},{8,29},{9,21}... | collective-permute-start | bytes 294920 | tf_op jit(solution)/shard_map/ppermute | solution.py:301
  13.1 3.1 %collective-permute-start.4 = (bf16[5,32,256]{2,1,0:T(8,128)(2,1)S(1)}, bf16[5,32,256]{2,1,0:T(8,128)(2,1)S(1)}, u32[]{:S(2)}, u32[]{:S(2)}) collective-permute-start(bf16[5,32,256]{2,1,0:T(8,128)(2,1)S(1)} %bitcast.30), channel_id=1, source_target_pairs={{0,4},{1,5},{2,6},{3,7},{4,0},{5,1},{6,2},{7,3},{8,12},{9,13},{10,... | collective-permute-start | bytes 245768 | tf_op jit(solution)/shard_map/ppermute | solution.py:300
  14.3 1.9 %collective-permute-start.6 = (f32[2,32,256]{2,1,0:T(8,128)S(1)}, f32[2,32,256]{2,1,0:T(8,128)S(1)}, u32[]{:S(2)}, u32[]{:S(2)}) collective-permute-start(f32[2,32,256]{2,1,0:T(8,128)S(1)} %convert_add_fusion.5.refs_9_), channel_id=1, source_target_pairs={{0,4},{1,5},{2,6},{3,7},{4,0},{5,1},{6,2},{7,3},{8,12},{9,13},{10,... | collective-permute-start | bytes 196616 | tf_op jit(solution)/shard_map/ppermute | solution.py:286
  17.4 6.4 %collective-permute-start.10 = (bf16[2,32,256]{2,1,0:T(8,128)(2,1)S(1)}, bf16[2,32,256]{2,1,0:T(8,128)(2,1)S(1)}, u32[]{:S(2)}, u32[]{:S(2)}) collective-permute-start(bf16[2,32,256]{2,1,0:T(8,128)(2,1)S(1)} %get-tuple-element.66), channel_id=1, source_target_pairs={{0,6},{1,14},{2,22},{3,30},{4,7},{5,15},{6,23},{7,31},{8,2},{9,10}... | collective-permute-start | bytes 98312 | tf_op jit(solution)/shard_map/ppermute | solution.py:280
  19.3 4.5 %collective-permute-start.8 = (bf16[2,32,256]{2,1,0:T(8,128)(2,1)S(1)}, bf16[2,32,256]{2,1,0:T(8,128)(2,1)S(1)}, u32[]{:S(2)}, u32[]{:S(2)}) collective-permute-start(bf16[2,32,256]{2,1,0:T(8,128)(2,1)S(1)} %get-tuple-element.66), channel_id=1, source_target_pairs={{0,4},{1,12},{2,20},{3,28},{4,5},{5,13},{6,21},{7,29},{8,0},{9,8},... | collective-permute-start | bytes 98312 | tf_op jit(solution)/shard_map/ppermute | solution.py:280
  23.8 3.2 %collective-permute-start.11 = (f32[2,32,256]{2,1,0:T(8,128)S(1)}, f32[2,32,256]{2,1,0:T(8,128)S(1)}, u32[]{:S(2)}, u32[]{:S(2)}) collective-permute-start(f32[2,32,256]{2,1,0:T(8,128)S(1)} %convert_add_fusion.4.refs_9_), channel_id=1, source_target_pairs={{0,4},{1,5},{2,6},{3,7},{4,0},{5,1},{6,2},{7,3},{8,12},{9,13},{10,... | collective-permute-start | bytes 196616 | tf_op jit(solution)/shard_map/ppermute | solution.py:286
  27.4 5.3 %collective-permute-start.12 = (bf16[2,32,256]{2,1,0:T(8,128)(2,1)S(1)}, bf16[2,32,256]{2,1,0:T(8,128)(2,1)S(1)}, u32[]{:S(2)}, u32[]{:S(2)}) collective-permute-start(bf16[2,32,256]{2,1,0:T(8,128)(2,1)S(1)} %get-tuple-element.76), channel_id=1, source_target_pairs={{0,4},{1,12},{2,20},{3,28},{4,5},{5,13},{6,21},{7,29},{8,0},{9,8},... | collective-permute-start | bytes 98312 | tf_op jit(solution)/shard_map/ppermute | solution.py:280
  27.5 8.7 %collective-permute-start.13 = (bf16[2,32,256]{2,1,0:T(8,128)(2,1)S(1)}, bf16[2,32,256]{2,1,0:T(8,128)(2,1)S(1)}, u32[]{:S(2)}, u32[]{:S(2)}) collective-permute-start(bf16[2,32,256]{2,1,0:T(8,128)(2,1)S(1)} %get-tuple-element.76), channel_id=1, source_target_pairs={{0,6},{1,14},{2,22},{3,30},{4,7},{5,15},{6,23},{7,31},{8,2},{9,10}... | collective-permute-start | bytes 98312 | tf_op jit(solution)/shard_map/ppermute | solution.py:280
  36.2 1.3 %collective-permute-start.14 = (f32[2,32,256]{2,1,0:T(8,128)S(1)}, f32[2,32,256]{2,1,0:T(8,128)S(1)}, u32[]{:S(2)}, u32[]{:S(2)}) collective-permute-start(f32[2,32,256]{2,1,0:T(8,128)S(1)} %convert_add_fusion.3.refs_9_), channel_id=1, source_target_pairs={{0,4},{1,5},{2,6},{3,7},{4,0},{5,1},{6,2},{7,3},{8,12},{9,13},{10,... | collective-permute-start | bytes 196616 | tf_op jit(solution)/shard_map/ppermute | solution.py:286
  36.3 5.9 %collective-permute-start.9 = (bf16[192,256]{1,0:T(8,128)(2,1)S(1)}, bf16[192,256]{1,0:T(8,128)(2,1)S(1)}, u32[]{:S(2)}, u32[]{:S(2)}) collective-permute-start(bf16[192,256]{1,0:T(8,128)(2,1)S(1)} %collective-permute-done.7.refs_3_), channel_id=1, source_target_pairs={{0,4},{1,5},{2,6},{3,7},{4,0},{5,1},{6,2},{7,3},{8,12},{9,13},{10,... | collective-permute-start | bytes 294920 | tf_op jit(solution)/shard_map/ppermute | solution.py:341
  38.0 4.3 %collective-permute-start.15 = (bf16[2,32,256]{2,1,0:T(8,128)(2,1)S(1)}, bf16[2,32,256]{2,1,0:T(8,128)(2,1)S(1)}, u32[]{:S(2)}, u32[]{:S(2)}) collective-permute-start(bf16[2,32,256]{2,1,0:T(8,128)(2,1)S(1)} %get-tuple-element.81.refs_9_), channel_id=1, source_target_pairs={{0,12},{1,13},{2,14},{3,15},{4,8},{5,9},{6,10},{7,11},{8,4},{9,5},... | collective-permute-start | bytes 98312 | tf_op jit(solution)/shard_map/ppermute | solution.py:280
  39.2 4.5 %collective-permute-start.16 = (bf16[2,32,256]{2,1,0:T(8,128)(2,1)S(1)}, bf16[2,32,256]{2,1,0:T(8,128)(2,1)S(1)}, u32[]{:S(2)}, u32[]{:S(2)}) collective-permute-start(bf16[2,32,256]{2,1,0:T(8,128)(2,1)S(1)} %get-tuple-element.81.refs_9_), channel_id=1, source_target_pairs={{0,20},{1,21},{2,22},{3,23},{4,16},{5,17},{6,18},{7,19},{8,28},{9,... | collective-permute-start | bytes 98312 | tf_op jit(solution)/shard_map/ppermute | solution.py:280
  42.1 4.2 %collective-permute-start.17 = (bf16[2,32,256]{2,1,0:T(8,128)(2,1)S(1)}, bf16[2,32,256]{2,1,0:T(8,128)(2,1)S(1)}, u32[]{:S(2)}, u32[]{:S(2)}) collective-permute-start(bf16[2,32,256]{2,1,0:T(8,128)(2,1)S(1)} %get-tuple-element.81.refs_9_), channel_id=1, source_target_pairs={{0,28},{1,29},{2,30},{3,31},{4,24},{5,25},{6,26},{7,27},{8,20},{9,... | collective-permute-start | bytes 98312 | tf_op jit(solution)/shard_map/ppermute | solution.py:280
  47.0 5.7 %collective-permute-start.18 = (bf16[2,32,256]{2,1,0:T(8,128)(2,1)S(1)}, bf16[2,32,256]{2,1,0:T(8,128)(2,1)S(1)}, u32[]{:S(2)}, u32[]{:S(2)}) collective-permute-start(bf16[2,32,256]{2,1,0:T(8,128)(2,1)S(1)} %get-tuple-element.83), channel_id=1, source_target_pairs={{0,20},{1,16},{2,4},{3,0},{4,28},{5,24},{6,12},{7,8},{8,21},{9,17}... | collective-permute-start | bytes 98312 | tf_op jit(solution)/shard_map/ppermute | solution.py:280
  47.0 5.7 %collective-permute-start.19 = (bf16[2,32,256]{2,1,0:T(8,128)(2,1)S(1)}, bf16[2,32,256]{2,1,0:T(8,128)(2,1)S(1)}, u32[]{:S(2)}, u32[]{:S(2)}) collective-permute-start(bf16[2,32,256]{2,1,0:T(8,128)(2,1)S(1)} %get-tuple-element.83), channel_id=1, source_target_pairs={{0,4},{1,0},{2,20},{3,16},{4,12},{5,8},{6,28},{7,24},{8,5},{9,1},{... | collective-permute-start | bytes 98312 | tf_op jit(solution)/shard_map/ppermute | solution.py:280
  52.8 1.3 %collective-permute-start.20 = (f32[2,32,256]{2,1,0:T(8,128)S(1)}, f32[2,32,256]{2,1,0:T(8,128)S(1)}, u32[]{:S(2)}, u32[]{:S(2)}) collective-permute-start(f32[2,32,256]{2,1,0:T(8,128)S(1)} %convert_add_fusion.2.refs_8_), channel_id=1, source_target_pairs={{0,4},{1,5},{2,6},{3,7},{4,0},{5,1},{6,2},{7,3},{8,12},{9,13},{10,... | collective-permute-start | bytes 196616 | tf_op jit(solution)/shard_map/ppermute | solution.py:286
  54.4 7.0 %collective-permute-start.21 = (bf16[2,32,256]{2,1,0:T(8,128)(2,1)S(1)}, bf16[2,32,256]{2,1,0:T(8,128)(2,1)S(1)}, u32[]{:S(2)}, u32[]{:S(2)}) collective-permute-start(bf16[2,32,256]{2,1,0:T(8,128)(2,1)S(1)} %get-tuple-element.86), channel_id=1, source_target_pairs={{0,20},{1,16},{2,4},{3,0},{4,28},{5,24},{6,12},{7,8},{8,21},{9,17}... | collective-permute-start | bytes 98312 | tf_op jit(solution)/shard_map/ppermute | solution.py:280
  56.3 5.1 %collective-permute-start.22 = (bf16[2,32,256]{2,1,0:T(8,128)(2,1)S(1)}, bf16[2,32,256]{2,1,0:T(8,128)(2,1)S(1)}, u32[]{:S(2)}, u32[]{:S(2)}) collective-permute-start(bf16[2,32,256]{2,1,0:T(8,128)(2,1)S(1)} %get-tuple-element.86), channel_id=1, source_target_pairs={{0,4},{1,0},{2,20},{3,16},{4,12},{5,8},{6,28},{7,24},{8,5},{9,1},{... | collective-permute-start | bytes 98312 | tf_op jit(solution)/shard_map/ppermute | solution.py:280
  61.4 1.3 %collective-permute-start.23 = (f32[2,32,256]{2,1,0:T(8,128)S(1)}, f32[2,32,256]{2,1,0:T(8,128)S(1)}, u32[]{:S(2)}, u32[]{:S(2)}) collective-permute-start(f32[2,32,256]{2,1,0:T(8,128)S(1)} %convert_add_fusion.1.refs_8_), channel_id=1, source_target_pairs={{0,4},{1,5},{2,6},{3,7},{4,0},{5,1},{6,2},{7,3},{8,12},{9,13},{10,... | collective-permute-start | bytes 196616 | tf_op jit(solution)/shard_map/ppermute | solution.py:286
  63.0 7.0 %collective-permute-start.24 = (bf16[2,32,256]{2,1,0:T(8,128)(2,1)S(1)}, bf16[2,32,256]{2,1,0:T(8,128)(2,1)S(1)}, u32[]{:S(2)}, u32[]{:S(2)}) collective-permute-start(bf16[2,32,256]{2,1,0:T(8,128)(2,1)S(1)} %get-tuple-element.90), channel_id=1, source_target_pairs={{0,20},{1,16},{2,4},{3,0},{4,28},{5,24},{6,12},{7,8},{8,21},{9,17}... | collective-permute-start | bytes 98312 | tf_op jit(solution)/shard_map/ppermute | solution.py:280
  64.7 5.3 %collective-permute-start.25 = (bf16[2,32,256]{2,1,0:T(8,128)(2,1)S(1)}, bf16[2,32,256]{2,1,0:T(8,128)(2,1)S(1)}, u32[]{:S(2)}, u32[]{:S(2)}) collective-permute-start(bf16[2,32,256]{2,1,0:T(8,128)(2,1)S(1)} %get-tuple-element.90), channel_id=1, source_target_pairs={{0,4},{1,0},{2,20},{3,16},{4,12},{5,8},{6,28},{7,24},{8,5},{9,1},{... | collective-permute-start | bytes 98312 | tf_op jit(solution)/shard_map/ppermute | solution.py:280
  70.0 1.3 %collective-permute-start.26 = (f32[2,32,256]{2,1,0:T(8,128)S(1)}, f32[2,32,256]{2,1,0:T(8,128)S(1)}, u32[]{:S(2)}, u32[]{:S(2)}) collective-permute-start(f32[2,32,256]{2,1,0:T(8,128)S(1)} %convert_add_fusion.refs_8_), channel_id=1, source_target_pairs={{0,4},{1,5},{2,6},{3,7},{4,0},{5,1},{6,2},{7,3},{8,12},{9,13},{10,... | collective-permute-start | bytes 196616 | tf_op jit(solution)/shard_map/ppermute | solution.py:286
  72.1 11.6 %collective-permute-start.30 = (bf16[5,32,256]{2,1,0:T(8,128)(2,1)S(1)}, bf16[5,32,256]{2,1,0:T(8,128)(2,1)S(1)}, u32[]{:S(2)}, u32[]{:S(2)}) collective-permute-start(bf16[5,32,256]{2,1,0:T(8,128)(2,1)S(1)} %get-tuple-element.97), channel_id=1, source_target_pairs={{0,7},{1,15},{2,23},{3,31},{4,3},{5,11},{6,19},{7,27},{8,6},{9,14}... | collective-permute-start | bytes 245768 | tf_op jit(solution)/shard_map/ppermute | solution.py:362
  78.2 3.9 %collective-permute-start.27 = (bf16[32,256]{1,0:T(8,128)(2,1)S(1)}, bf16[32,256]{1,0:T(8,128)(2,1)S(1)}, u32[]{:S(2)}, u32[]{:S(2)}) collective-permute-start(bf16[32,256]{1,0:T(8,128)(2,1)S(1)} %get-tuple-element.96), channel_id=1, source_target_pairs={{0,5},{1,4},{2,7},{3,6},{4,1},{5,0},{6,3},{7,2},{8,13},{9,12},{10,... | collective-permute-start | bytes 49160 | tf_op jit(solution)/shard_map/ppermute | solution.py:365
  78.2 4.1 %collective-permute-start.28 = (bf16[32,256]{1,0:T(8,128)(2,1)S(1)}, bf16[32,256]{1,0:T(8,128)(2,1)S(1)}, u32[]{:S(2)}, u32[]{:S(2)}) collective-permute-start(bf16[32,256]{1,0:T(8,128)(2,1)S(1)} %get-tuple-element.96), channel_id=1, source_target_pairs={{0,6},{1,7},{2,4},{3,5},{4,2},{5,3},{6,0},{7,1},{8,14},{9,15},{10,... | collective-permute-start | bytes 49160 | tf_op jit(solution)/shard_map/ppermute | solution.py:365
  78.6 5.1 %collective-permute-start.29 = (bf16[32,256]{1,0:T(8,128)(2,1)S(1)}, bf16[32,256]{1,0:T(8,128)(2,1)S(1)}, u32[]{:S(2)}, u32[]{:S(2)}) collective-permute-start(bf16[32,256]{1,0:T(8,128)(2,1)S(1)} %get-tuple-element.96), channel_id=1, source_target_pairs={{0,7},{1,6},{2,5},{3,4},{4,3},{5,2},{6,1},{7,0},{8,15},{9,14},{10,... | collective-permute-start | bytes 49160 | tf_op jit(solution)/shard_map/ppermute | solution.py:365
  (3 other events, 7.8 us)

commit v5 on v4

--- a/solution.py
+++ b/solution.py
@@ -164,7 +164,7 @@
     keep, gotten, rhs, rhs_other, inv, inv_other, mine, other, ahead, some, rest = refs[:11]
     y_ref, msg_ref, total_ref = refs[11:]
     k, diagonal = place()
-    total_ref[...] = some[...] + rest[...]
+    total_ref[...] = f32(some[...]) + f32(rest[...])
     for at, b, inverse in ((k, rhs, inv), (1 - k, rhs_other, inv_other)):
         y_ref[at] = bf16(dot(bf16(f32(b[level]) - total_ref[at]), inverse[level], NT))
     parts = lower_part(k, [pair], [y_ref], mine, other, keep, gotten)
@@ -219,7 +219,7 @@
     outs = refs[15 - level :]
     k, diagonal = place()
     x_ref = outs[0]
-    x_ref[...] = bf16(-(some[...] + rest[...]))
+    x_ref[...] = bf16(-(f32(some[...]) + f32(rest[...])))
     solved = list(later) + [x_ref]
     factors = (mine, other, keep, gotten)
     parts = up_parts(k, diagonal, level - 1, pairs, [x_ref], below, factors, inv, inv_other, ahead)
@@ -282,7 +282,7 @@
 
     def share(msg, perms):
         got = send(msg, perms)
-        some = tree([f32(g) for g in got])
+        some = bf16(tree([f32(g) for g in got]))
         return got, some, swap(some)
 
     first = lambda x, at: pl.BlockSpec((1, *x.shape[1:]), lambda i: (at,) + (0,) * (len(x.shape) - 1))

time: 84.6 us -> 84.4 us (level)
  transfers between devices with their start and end apart: 31 -> 31, of which waited for: 16 -> 16; matrix products, arithmetic and copies ran while one was open for 0% -> 0% of each run, Pallas kernels for 5% -> 6%
where the time goes in v5:
time: 84.4 us; the launch traced here: 84.2 us
  starting transfers between devices  43.9 us (52%)
  waiting for transfers between devices  27.4 us (32%)
  Pallas kernels  10.1 us (12%)
  local copies, waits for them, and re-layouts  0.97 us (1%)
  other arithmetic  0.91 us (1%)
  between operations  0.89 us (1%)
    ppermute x15, starting transfers between devices, on_device(): send = lambda x, perms: [lax.ppermute(x, BOTH, p) for p in perms]  28.7 us
    ppermute x15, waiting for transfers between devices, on_device(): send = lambda x, perms: [lax.ppermute(x, BOTH, p) for p in perms]  20.5 us
    ppermute x1, starting transfers between devices, on_device(): moved = lax.ppermute(more[1], BOTH, turn_perm(n))  6.12 us
    pallas_call x11, Pallas kernels, call(): pl.pallas_call(body, out_shape=[jax.ShapeDtypeStruct(s, dtype) for s in o...  4.64 us
    ppermute x3, starting transfers between devices, on_device(): got = {m: lax.ppermute(more[0], BOTH, lines[m - 1]) for m in order}  3.87 us
    ppermute x6, waiting for transfers between devices, share(): return (got, some, swap(some))  3.32 us
    pallas_call x1, Pallas kernels, on_device(): pl.pallas_call(start_kernel, grid=(1,), out_shape=[jax.ShapeDtypeStruct(s...  2.35 us
    ppermute x1, starting transfers between devices, on_device(): inv_to = lax.ppermute(last, BOTH, far_perm(n))  2.22 us
  transfers between devices with their start and end apart: 31, of which 16 were waited for; matrix products, arithmetic and copies ran while one was open for 0% of the time, Pallas kernels for 6%

profile of v5, /device:TPU:0, one launch (start us, length us, event | category | flops | bytes accessed | tf_op | source)
XLA Modules:
  0.0 84.2 jit_solution(1881634873715056956)
XLA Ops:
  0.6 2.4 %shard_map.59 = (f32[4,32,256]{2,1,0:T(8,128)}, f32[4,32,256]{2,1,0:T(8,128)}, bf16[192,256]{1,0:T(8,128)(2,1)}) custom-call(s32[2,1,10]{2,1,0:T(1,128)} %bitcast.34, bf16[5,32,256]{2,1,0:T(8,128)(2,1)} %bitcast.29, bf16[5,256,256]{2,1,0:T(8,128)(2,1)} %bitcast.19, bf16[5,256,256]{2,1,0:T(8,128)(2,1)} %bitcast.20, bf16[10,2,256,256]{3,2,1,0:T(8,128)(2,1)} %bitcast.4), custom_call_target="tpu_custom_call" | custom-call | tf_op jit(solution)/shard_map/pallas_call | solution.py:289
  3.5 1.2 %collective-permute-done.gotten_in = f32[4,32,256]{2,1,0:T(8,128)S(1)} collective-permute-done((f32[4,32,256]{2,1,0:T(8,128)}, f32[4,32,256]{2,1,0:T(8,128)S(1)}, u32[]{:S(2)}, u32[]{:S(2)}) %collective-permute-start) | collective-permute-done | bytes 131104 | tf_op jit(solution)/shard_map/ppermute | solution.py:297
  4.7 0.8 %fusion = bf16[2,32,256]{2,1,0:T(8,128)(2,1)S(1)} fusion(f32[4,32,256]{2,1,0:T(8,128)S(1)} %collective-permute-done.gotten_in, f32[4,32,256]{2,1,0:T(8,128)} %get-tuple-element.50.keep_in), kind=kLoop, calls=%fused_computation.1 | loop fusion | flops 32768 | bytes 163840 | tf_op jit(solution)/shard_map/convert_element_type | solution.py:70
  6.5 4.5 %collective-permute-start.5 = (bf16[2,32,256]{2,1,0:T(8,128)(2,1)S(1)}, bf16[2,32,256]{2,1,0:T(8,128)(2,1)S(1)}, u32[]{:S(2)}, u32[]{:S(2)}) collective-permute-start(bf16[2,32,256]{2,1,0:T(8,128)(2,1)S(1)} %fusion), channel_id=1, source_target_pairs={{0,6},{1,14},{2,22},{3,30},{4,7},{5,15},{6,23},{7,31},{8,2},{9,10}... | collective-permute-start | bytes 98312 | tf_op jit(solution)/shard_map/ppermute | solution.py:280
  10.9 2.2 %collective-permute-start.7 = (bf16[192,256]{1,0:T(8,128)(2,1)}, bf16[192,256]{1,0:T(8,128)(2,1)S(1)}, u32[]{:S(2)}, u32[]{:S(2)}) collective-permute-start(bf16[192,256]{1,0:T(8,128)(2,1)} %get-tuple-element.65), channel_id=1, source_target_pairs={{0,28},{1,20},{2,12},{3,4},{4,24},{5,16},{6,8},{7,0},{8,29},{9,21}... | collective-permute-start | bytes 294920 | tf_op jit(solution)/shard_map/ppermute | solution.py:301
  13.1 1.1 %collective-permute-done.5 = bf16[2,32,256]{2,1,0:T(8,128)(2,1)S(1)} collective-permute-done((bf16[2,32,256]{2,1,0:T(8,128)(2,1)S(1)}, bf16[2,32,256]{2,1,0:T(8,128)(2,1)S(1)}, u32[]{:S(2)}, u32[]{:S(2)}) %collective-permute-start.5) | collective-permute-done | bytes 32800 | tf_op jit(solution)/shard_map/ppermute | solution.py:280
  14.4 1.0 %copy-done.3 = f32[4,32,256]{2,1,0:T(8,128)S(1)} copy-done((f32[4,32,256]{2,1,0:T(8,128)S(1)}, f32[4,32,256]{2,1,0:T(8,128)}, u32[]{:S(2)}) %copy-start.3) | copy-done | bytes 131096
  15.4 0.8 shard_map.60
  17.4 1.9 %collective-permute-start.10 = (bf16[2,32,256]{2,1,0:T(8,128)(2,1)S(1)}, bf16[2,32,256]{2,1,0:T(8,128)(2,1)S(1)}, u32[]{:S(2)}, u32[]{:S(2)}) collective-permute-start(bf16[2,32,256]{2,1,0:T(8,128)(2,1)S(1)} %get-tuple-element.66), channel_id=1, source_target_pairs={{0,6},{1,14},{2,22},{3,30},{4,7},{5,15},{6,23},{7,31},{8,2},{9,10}... | collective-permute-start | bytes 98312 | tf_op jit(solution)/shard_map/ppermute | solution.py:280
  19.3 2.4 %collective-permute-start.8 = (bf16[2,32,256]{2,1,0:T(8,128)(2,1)S(1)}, bf16[2,32,256]{2,1,0:T(8,128)(2,1)S(1)}, u32[]{:S(2)}, u32[]{:S(2)}) collective-permute-start(bf16[2,32,256]{2,1,0:T(8,128)(2,1)S(1)} %get-tuple-element.66), channel_id=1, source_target_pairs={{0,4},{1,12},{2,20},{3,28},{4,5},{5,13},{6,21},{7,29},{8,0},{9,8},... | collective-permute-start | bytes 98312 | tf_op jit(solution)/shard_map/ppermute | solution.py:280
  21.7 2.1 %collective-permute-done.10 = bf16[2,32,256]{2,1,0:T(8,128)(2,1)S(1)} collective-permute-done((bf16[2,32,256]{2,1,0:T(8,128)(2,1)S(1)}, bf16[2,32,256]{2,1,0:T(8,128)(2,1)S(1)}, u32[]{:S(2)}, u32[]{:S(2)}) %collective-permute-start.10) | collective-permute-done | bytes 32800 | tf_op jit(solution)/shard_map/ppermute | solution.py:280
  23.8 1.6 %collective-permute-start.11 = (bf16[2,32,256]{2,1,0:T(8,128)(2,1)S(1)}, bf16[2,32,256]{2,1,0:T(8,128)(2,1)S(1)}, u32[]{:S(2)}, u32[]{:S(2)}) collective-permute-start(bf16[2,32,256]{2,1,0:T(8,128)(2,1)S(1)} %add_convert_fusion.4.refs_9_), channel_id=1, source_target_pairs={{0,4},{1,5},{2,6},{3,7},{4,0},{5,1},{6,2},{7,3},{8,12},{9,13},{10,... | collective-permute-start | bytes 98312 | tf_op jit(solution)/shard_map/ppermute | solution.py:286
  25.4 1.6 %shard_map.62 = (bf16[5,256,256]{2,1,0:T(8,128)(2,1)S(1)}, bf16[10,2,256,256]{3,2,1,0:T(8,128)(2,1)S(1)}, f32[2,32,256]{2,1,0:T(8,128)S(1)}) custom-call(f32[4,32,256]{2,1,0:T(8,128)S(1)} %get-tuple-element.56.refs_0_.keep, f32[4,32,256]{2,1,0:T(8,128)S(1)} %get-tuple-element.57.refs_1_.gotten, bf16[10,2,256,256]{3,2,1,0:T(8,128)(2,1)S(1)} %bitcast.8, ...), custom_call_target="tpu_custom_call" | custom-call | tf_op jit(solution)/shard_map/pallas_call | solution.py:321
  27.5 5.2 %collective-permute-start.13 = (bf16[2,32,256]{2,1,0:T(8,128)(2,1)S(1)}, bf16[2,32,256]{2,1,0:T(8,128)(2,1)S(1)}, u32[]{:S(2)}, u32[]{:S(2)}) collective-permute-start(bf16[2,32,256]{2,1,0:T(8,128)(2,1)S(1)} %get-tuple-element.76), channel_id=1, source_target_pairs={{0,6},{1,14},{2,22},{3,30},{4,7},{5,15},{6,23},{7,31},{8,2},{9,10}... | collective-permute-start | bytes 98312 | tf_op jit(solution)/shard_map/ppermute | solution.py:280
  32.7 3.5 %collective-permute-done.13 = bf16[2,32,256]{2,1,0:T(8,128)(2,1)S(1)} collective-permute-done((bf16[2,32,256]{2,1,0:T(8,128)(2,1)S(1)}, bf16[2,32,256]{2,1,0:T(8,128)(2,1)S(1)}, u32[]{:S(2)}, u32[]{:S(2)}) %collective-permute-start.13) | collective-permute-done | bytes 32800 | tf_op jit(solution)/shard_map/ppermute | solution.py:280
  37.9 1.3 %collective-permute-start.15 = (bf16[2,32,256]{2,1,0:T(8,128)(2,1)S(1)}, bf16[2,32,256]{2,1,0:T(8,128)(2,1)S(1)}, u32[]{:S(2)}, u32[]{:S(2)}) collective-permute-start(bf16[2,32,256]{2,1,0:T(8,128)(2,1)S(1)} %get-tuple-element.81.refs_9_), channel_id=1, source_target_pairs={{0,12},{1,13},{2,14},{3,15},{4,8},{5,9},{6,10},{7,11},{8,4},{9,5},... | collective-permute-start | bytes 98312 | tf_op jit(solution)/shard_map/ppermute | solution.py:280
  39.2 2.9 %collective-permute-start.16 = (bf16[2,32,256]{2,1,0:T(8,128)(2,1)S(1)}, bf16[2,32,256]{2,1,0:T(8,128)(2,1)S(1)}, u32[]{:S(2)}, u32[]{:S(2)}) collective-permute-start(bf16[2,32,256]{2,1,0:T(8,128)(2,1)S(1)} %get-tuple-element.81.refs_9_), channel_id=1, source_target_pairs={{0,20},{1,21},{2,22},{3,23},{4,16},{5,17},{6,18},{7,19},{8,28},{9,... | collective-permute-start | bytes 98312 | tf_op jit(solution)/shard_map/ppermute | solution.py:280
  42.2 1.5 %collective-permute-done.16.refs_11_ = bf16[2,32,256]{2,1,0:T(8,128)(2,1)S(1)} collective-permute-done((bf16[2,32,256]{2,1,0:T(8,128)(2,1)S(1)}, bf16[2,32,256]{2,1,0:T(8,128)(2,1)S(1)}, u32[]{:S(2)}, u32[]{:S(2)}) %collective-permute-start.16) | collective-permute-done | bytes 32800 | tf_op jit(solution)/shard_map/ppermute | solution.py:280
  43.7 2.6 %collective-permute-done.17.refs_12_ = bf16[2,32,256]{2,1,0:T(8,128)(2,1)S(1)} collective-permute-done((bf16[2,32,256]{2,1,0:T(8,128)(2,1)S(1)}, bf16[2,32,256]{2,1,0:T(8,128)(2,1)S(1)}, u32[]{:S(2)}, u32[]{:S(2)}) %collective-permute-start.17) | collective-permute-done | bytes 32800 | tf_op jit(solution)/shard_map/ppermute | solution.py:280
  47.3 5.4 %collective-permute-done.18 = bf16[2,32,256]{2,1,0:T(8,128)(2,1)S(1)} collective-permute-done((bf16[2,32,256]{2,1,0:T(8,128)(2,1)S(1)}, bf16[2,32,256]{2,1,0:T(8,128)(2,1)S(1)}, u32[]{:S(2)}, u32[]{:S(2)}) %collective-permute-start.18) | collective-permute-done | bytes 32800 | tf_op jit(solution)/shard_map/ppermute | solution.py:280
  53.0 1.0 %collective-permute-done.20.refs_9_ = bf16[2,32,256]{2,1,0:T(8,128)(2,1)S(1)} collective-permute-done((bf16[2,32,256]{2,1,0:T(8,128)(2,1)S(1)}, bf16[2,32,256]{2,1,0:T(8,128)(2,1)S(1)}, u32[]{:S(2)}, u32[]{:S(2)}) %collective-permute-start.20) | collective-permute-done | bytes 32800 | tf_op jit(solution)/shard_map/ppermute | solution.py:286
  54.3 1.9 %collective-permute-start.21 = (bf16[2,32,256]{2,1,0:T(8,128)(2,1)S(1)}, bf16[2,32,256]{2,1,0:T(8,128)(2,1)S(1)}, u32[]{:S(2)}, u32[]{:S(2)}) collective-permute-start(bf16[2,32,256]{2,1,0:T(8,128)(2,1)S(1)} %get-tuple-element.86), channel_id=1, source_target_pairs={{0,20},{1,16},{2,4},{3,0},{4,28},{5,24},{6,12},{7,8},{8,21},{9,17}... | collective-permute-start | bytes 98312 | tf_op jit(solution)/shard_map/ppermute | solution.py:280
  56.2 2.9 %collective-permute-start.22 = (bf16[2,32,256]{2,1,0:T(8,128)(2,1)S(1)}, bf16[2,32,256]{2,1,0:T(8,128)(2,1)S(1)}, u32[]{:S(2)}, u32[]{:S(2)}) collective-permute-start(bf16[2,32,256]{2,1,0:T(8,128)(2,1)S(1)} %get-tuple-element.86), channel_id=1, source_target_pairs={{0,4},{1,0},{2,20},{3,16},{4,12},{5,8},{6,28},{7,24},{8,5},{9,1},{... | collective-permute-start | bytes 98312 | tf_op jit(solution)/shard_map/ppermute | solution.py:280
  59.1 2.2 %collective-permute-done.21 = bf16[2,32,256]{2,1,0:T(8,128)(2,1)S(1)} collective-permute-done((bf16[2,32,256]{2,1,0:T(8,128)(2,1)S(1)}, bf16[2,32,256]{2,1,0:T(8,128)(2,1)S(1)}, u32[]{:S(2)}, u32[]{:S(2)}) %collective-permute-start.21) | collective-permute-done | bytes 32800 | tf_op jit(solution)/shard_map/ppermute | solution.py:280
  61.6 0.9 %collective-permute-done.23.refs_9_ = bf16[2,32,256]{2,1,0:T(8,128)(2,1)S(1)} collective-permute-done((bf16[2,32,256]{2,1,0:T(8,128)(2,1)S(1)}, bf16[2,32,256]{2,1,0:T(8,128)(2,1)S(1)}, u32[]{:S(2)}, u32[]{:S(2)}) %collective-permute-start.23) | collective-permute-done | bytes 32800 | tf_op jit(solution)/shard_map/ppermute | solution.py:286
  62.8 1.7 %collective-permute-start.24 = (bf16[2,32,256]{2,1,0:T(8,128)(2,1)S(1)}, bf16[2,32,256]{2,1,0:T(8,128)(2,1)S(1)}, u32[]{:S(2)}, u32[]{:S(2)}) collective-permute-start(bf16[2,32,256]{2,1,0:T(8,128)(2,1)S(1)} %get-tuple-element.90), channel_id=1, source_target_pairs={{0,20},{1,16},{2,4},{3,0},{4,28},{5,24},{6,12},{7,8},{8,21},{9,17}... | collective-permute-start | bytes 98312 | tf_op jit(solution)/shard_map/ppermute | solution.py:280
  64.5 3.2 %collective-permute-start.25 = (bf16[2,32,256]{2,1,0:T(8,128)(2,1)S(1)}, bf16[2,32,256]{2,1,0:T(8,128)(2,1)S(1)}, u32[]{:S(2)}, u32[]{:S(2)}) collective-permute-start(bf16[2,32,256]{2,1,0:T(8,128)(2,1)S(1)} %get-tuple-element.90), channel_id=1, source_target_pairs={{0,4},{1,0},{2,20},{3,16},{4,12},{5,8},{6,28},{7,24},{8,5},{9,1},{... | collective-permute-start | bytes 98312 | tf_op jit(solution)/shard_map/ppermute | solution.py:280
  67.7 2.1 %collective-permute-done.24 = bf16[2,32,256]{2,1,0:T(8,128)(2,1)S(1)} collective-permute-done((bf16[2,32,256]{2,1,0:T(8,128)(2,1)S(1)}, bf16[2,32,256]{2,1,0:T(8,128)(2,1)S(1)}, u32[]{:S(2)}, u32[]{:S(2)}) %collective-permute-start.24) | collective-permute-done | bytes 32800 | tf_op jit(solution)/shard_map/ppermute | solution.py:280
  71.1 0.8 shard_map.72
  71.9 6.1 %collective-permute-start.30 = (bf16[5,32,256]{2,1,0:T(8,128)(2,1)S(1)}, bf16[5,32,256]{2,1,0:T(8,128)(2,1)S(1)}, u32[]{:S(2)}, u32[]{:S(2)}) collective-permute-start(bf16[5,32,256]{2,1,0:T(8,128)(2,1)S(1)} %get-tuple-element.97), channel_id=1, source_target_pairs={{0,7},{1,15},{2,23},{3,31},{4,3},{5,11},{6,19},{7,27},{8,6},{9,14}... | collective-permute-start | bytes 245768 | tf_op jit(solution)/shard_map/ppermute | solution.py:362
  78.4 3.5 %collective-permute-start.29 = (bf16[32,256]{1,0:T(8,128)(2,1)S(1)}, bf16[32,256]{1,0:T(8,128)(2,1)S(1)}, u32[]{:S(2)}, u32[]{:S(2)}) collective-permute-start(bf16[32,256]{1,0:T(8,128)(2,1)S(1)} %get-tuple-element.96), channel_id=1, source_target_pairs={{0,7},{1,6},{2,5},{3,4},{4,3},{5,2},{6,1},{7,0},{8,15},{9,14},{10,... | collective-permute-start | bytes 49160 | tf_op jit(solution)/shard_map/ppermute | solution.py:365
  82.1 1.4 %collective-permute-done.29.refs_3_ = bf16[32,256]{1,0:T(8,128)(2,1)S(1)} collective-permute-done((bf16[32,256]{1,0:T(8,128)(2,1)S(1)}, bf16[32,256]{1,0:T(8,128)(2,1)S(1)}, u32[]{:S(2)}, u32[]{:S(2)}) %collective-permute-start.29) | collective-permute-done | bytes 16416 | tf_op jit(solution)/shard_map/ppermute | solution.py:365
  (60 shorter events, 9.7 us)
Async XLA Ops:
  0.6 12.5 %copy-start.2 = (bf16[5,1,32,256]{3,2,1,0:T(8,128)(2,1)S(1)}, bf16[5,1,32,256]{3,2,1,0:T(8,128)(2,1)}, u32[]{:S(2)}) copy-start(bf16[5,1,32,256]{3,2,1,0:T(8,128)(2,1)} %param.4) | copy-start | bytes 245764
  3.0 1.6 %collective-permute-start = (f32[4,32,256]{2,1,0:T(8,128)}, f32[4,32,256]{2,1,0:T(8,128)S(1)}, u32[]{:S(2)}, u32[]{:S(2)}) collective-permute-start(f32[4,32,256]{2,1,0:T(8,128)} %get-tuple-element.51), channel_id=1, source_target_pairs={{0,4},{1,5},{2,6},{3,7},{4,0},{5,1},{6,2},{7,3},{8,12},{9,13},{10,... | collective-permute-start | bytes 393224 | tf_op jit(solution)/shard_map/ppermute | solution.py:297
  5.5 8.9 %collective-permute-start.2 = (bf16[10,2,256,256]{3,2,1,0:T(8,128)(2,1)S(1)}, bf16[10,2,256,256]{3,2,1,0:T(8,128)(2,1)S(1)}, u32[]{:S(2)}, u32[]{:S(2)}) collective-permute-start(bf16[10,2,256,256]{3,2,1,0:T(8,128)(2,1)S(1)} %bitcast.5), channel_id=1, source_target_pairs={{0,4},{1,5},{2,6},{3,7},{4,0},{5,1},{6,2},{7,3},{8,12},{9,13},{10,... | collective-permute-start | bytes 7864328 | tf_op jit(solution)/shard_map/ppermute | solution.py:300
  5.9 8.5 %collective-permute-start.1 = (bf16[5,256,256]{2,1,0:T(8,128)(2,1)}, bf16[5,256,256]{2,1,0:T(8,128)(2,1)S(1)}, u32[]{:S(2)}, u32[]{:S(2)}) collective-permute-start(bf16[5,256,256]{2,1,0:T(8,128)(2,1)} %bitcast.21), channel_id=1, source_target_pairs={{0,4},{1,5},{2,6},{3,7},{4,0},{5,1},{6,2},{7,3},{8,12},{9,13},{10,... | collective-permute-start | bytes 1966088 | tf_op jit(solution)/shard_map/ppermute | solution.py:300
  6.1 7.0 %collective-permute-start.3 = (bf16[2,32,256]{2,1,0:T(8,128)(2,1)S(1)}, bf16[2,32,256]{2,1,0:T(8,128)(2,1)S(1)}, u32[]{:S(2)}, u32[]{:S(2)}) collective-permute-start(bf16[2,32,256]{2,1,0:T(8,128)(2,1)S(1)} %fusion), channel_id=1, source_target_pairs={{0,4},{1,12},{2,20},{3,28},{4,5},{5,13},{6,21},{7,29},{8,0},{9,8},... | collective-permute-start | bytes 98312 | tf_op jit(solution)/shard_map/ppermute | solution.py:280
  6.5 7.8 %collective-permute-start.5 = (bf16[2,32,256]{2,1,0:T(8,128)(2,1)S(1)}, bf16[2,32,256]{2,1,0:T(8,128)(2,1)S(1)}, u32[]{:S(2)}, u32[]{:S(2)}) collective-permute-start(bf16[2,32,256]{2,1,0:T(8,128)(2,1)S(1)} %fusion), channel_id=1, source_target_pairs={{0,6},{1,14},{2,22},{3,30},{4,7},{5,15},{6,23},{7,31},{8,2},{9,10}... | collective-permute-start | bytes 98312 | tf_op jit(solution)/shard_map/ppermute | solution.py:280
  10.9 6.5 %collective-permute-start.7 = (bf16[192,256]{1,0:T(8,128)(2,1)}, bf16[192,256]{1,0:T(8,128)(2,1)S(1)}, u32[]{:S(2)}, u32[]{:S(2)}) collective-permute-start(bf16[192,256]{1,0:T(8,128)(2,1)} %get-tuple-element.65), channel_id=1, source_target_pairs={{0,28},{1,20},{2,12},{3,4},{4,24},{5,16},{6,8},{7,0},{8,29},{9,21}... | collective-permute-start | bytes 294920 | tf_op jit(solution)/shard_map/ppermute | solution.py:301
  13.1 3.1 %collective-permute-start.4 = (bf16[5,32,256]{2,1,0:T(8,128)(2,1)S(1)}, bf16[5,32,256]{2,1,0:T(8,128)(2,1)S(1)}, u32[]{:S(2)}, u32[]{:S(2)}) collective-permute-start(bf16[5,32,256]{2,1,0:T(8,128)(2,1)S(1)} %bitcast.30), channel_id=1, source_target_pairs={{0,4},{1,5},{2,6},{3,7},{4,0},{5,1},{6,2},{7,3},{8,12},{9,13},{10,... | collective-permute-start | bytes 245768 | tf_op jit(solution)/shard_map/ppermute | solution.py:300
  14.3 1.9 %collective-permute-start.6 = (bf16[2,32,256]{2,1,0:T(8,128)(2,1)S(1)}, bf16[2,32,256]{2,1,0:T(8,128)(2,1)S(1)}, u32[]{:S(2)}, u32[]{:S(2)}) collective-permute-start(bf16[2,32,256]{2,1,0:T(8,128)(2,1)S(1)} %add_convert_fusion.5.refs_9_), channel_id=1, source_target_pairs={{0,4},{1,5},{2,6},{3,7},{4,0},{5,1},{6,2},{7,3},{8,12},{9,13},{10,... | collective-permute-start | bytes 98312 | tf_op jit(solution)/shard_map/ppermute | solution.py:286
  17.4 6.4 %collective-permute-start.10 = (bf16[2,32,256]{2,1,0:T(8,128)(2,1)S(1)}, bf16[2,32,256]{2,1,0:T(8,128)(2,1)S(1)}, u32[]{:S(2)}, u32[]{:S(2)}) collective-permute-start(bf16[2,32,256]{2,1,0:T(8,128)(2,1)S(1)} %get-tuple-element.66), channel_id=1, source_target_pairs={{0,6},{1,14},{2,22},{3,30},{4,7},{5,15},{6,23},{7,31},{8,2},{9,10}... | collective-permute-start | bytes 98312 | tf_op jit(solution)/shard_map/ppermute | solution.py:280
  19.3 4.5 %collective-permute-start.8 = (bf16[2,32,256]{2,1,0:T(8,128)(2,1)S(1)}, bf16[2,32,256]{2,1,0:T(8,128)(2,1)S(1)}, u32[]{:S(2)}, u32[]{:S(2)}) collective-permute-start(bf16[2,32,256]{2,1,0:T(8,128)(2,1)S(1)} %get-tuple-element.66), channel_id=1, source_target_pairs={{0,4},{1,12},{2,20},{3,28},{4,5},{5,13},{6,21},{7,29},{8,0},{9,8},... | collective-permute-start | bytes 98312 | tf_op jit(solution)/shard_map/ppermute | solution.py:280
  23.8 3.2 %collective-permute-start.11 = (bf16[2,32,256]{2,1,0:T(8,128)(2,1)S(1)}, bf16[2,32,256]{2,1,0:T(8,128)(2,1)S(1)}, u32[]{:S(2)}, u32[]{:S(2)}) collective-permute-start(bf16[2,32,256]{2,1,0:T(8,128)(2,1)S(1)} %add_convert_fusion.4.refs_9_), channel_id=1, source_target_pairs={{0,4},{1,5},{2,6},{3,7},{4,0},{5,1},{6,2},{7,3},{8,12},{9,13},{10,... | collective-permute-start | bytes 98312 | tf_op jit(solution)/shard_map/ppermute | solution.py:286
  27.4 5.3 %collective-permute-start.12 = (bf16[2,32,256]{2,1,0:T(8,128)(2,1)S(1)}, bf16[2,32,256]{2,1,0:T(8,128)(2,1)S(1)}, u32[]{:S(2)}, u32[]{:S(2)}) collective-permute-start(bf16[2,32,256]{2,1,0:T(8,128)(2,1)S(1)} %get-tuple-element.76), channel_id=1, source_target_pairs={{0,4},{1,12},{2,20},{3,28},{4,5},{5,13},{6,21},{7,29},{8,0},{9,8},... | collective-permute-start | bytes 98312 | tf_op jit(solution)/shard_map/ppermute | solution.py:280
  27.5 8.7 %collective-permute-start.13 = (bf16[2,32,256]{2,1,0:T(8,128)(2,1)S(1)}, bf16[2,32,256]{2,1,0:T(8,128)(2,1)S(1)}, u32[]{:S(2)}, u32[]{:S(2)}) collective-permute-start(bf16[2,32,256]{2,1,0:T(8,128)(2,1)S(1)} %get-tuple-element.76), channel_id=1, source_target_pairs={{0,6},{1,14},{2,22},{3,30},{4,7},{5,15},{6,23},{7,31},{8,2},{9,10}... | collective-permute-start | bytes 98312 | tf_op jit(solution)/shard_map/ppermute | solution.py:280
  32.7 9.5 %collective-permute-start.9 = (bf16[192,256]{1,0:T(8,128)(2,1)S(1)}, bf16[192,256]{1,0:T(8,128)(2,1)S(1)}, u32[]{:S(2)}, u32[]{:S(2)}) collective-permute-start(bf16[192,256]{1,0:T(8,128)(2,1)S(1)} %collective-permute-done.7.refs_3_), channel_id=1, source_target_pairs={{0,4},{1,5},{2,6},{3,7},{4,0},{5,1},{6,2},{7,3},{8,12},{9,13},{10,... | collective-permute-start | bytes 294920 | tf_op jit(solution)/shard_map/ppermute | solution.py:341
  36.3 1.3 %collective-permute-start.14 = (bf16[2,32,256]{2,1,0:T(8,128)(2,1)S(1)}, bf16[2,32,256]{2,1,0:T(8,128)(2,1)S(1)}, u32[]{:S(2)}, u32[]{:S(2)}) collective-permute-start(bf16[2,32,256]{2,1,0:T(8,128)(2,1)S(1)} %add_convert_fusion.3.refs_9_), channel_id=1, source_target_pairs={{0,4},{1,5},{2,6},{3,7},{4,0},{5,1},{6,2},{7,3},{8,12},{9,13},{10,... | collective-permute-start | bytes 98312 | tf_op jit(solution)/shard_map/ppermute | solution.py:286
  37.9 4.3 %collective-permute-start.15 = (bf16[2,32,256]{2,1,0:T(8,128)(2,1)S(1)}, bf16[2,32,256]{2,1,0:T(8,128)(2,1)S(1)}, u32[]{:S(2)}, u32[]{:S(2)}) collective-permute-start(bf16[2,32,256]{2,1,0:T(8,128)(2,1)S(1)} %get-tuple-element.81.refs_9_), channel_id=1, source_target_pairs={{0,12},{1,13},{2,14},{3,15},{4,8},{5,9},{6,10},{7,11},{8,4},{9,5},... | collective-permute-start | bytes 98312 | tf_op jit(solution)/shard_map/ppermute | solution.py:280
  39.2 4.5 %collective-permute-start.16 = (bf16[2,32,256]{2,1,0:T(8,128)(2,1)S(1)}, bf16[2,32,256]{2,1,0:T(8,128)(2,1)S(1)}, u32[]{:S(2)}, u32[]{:S(2)}) collective-permute-start(bf16[2,32,256]{2,1,0:T(8,128)(2,1)S(1)} %get-tuple-element.81.refs_9_), channel_id=1, source_target_pairs={{0,20},{1,21},{2,22},{3,23},{4,16},{5,17},{6,18},{7,19},{8,28},{9,... | collective-permute-start | bytes 98312 | tf_op jit(solution)/shard_map/ppermute | solution.py:280
  42.1 4.2 %collective-permute-start.17 = (bf16[2,32,256]{2,1,0:T(8,128)(2,1)S(1)}, bf16[2,32,256]{2,1,0:T(8,128)(2,1)S(1)}, u32[]{:S(2)}, u32[]{:S(2)}) collective-permute-start(bf16[2,32,256]{2,1,0:T(8,128)(2,1)S(1)} %get-tuple-element.81.refs_9_), channel_id=1, source_target_pairs={{0,28},{1,29},{2,30},{3,31},{4,24},{5,25},{6,26},{7,27},{8,20},{9,... | collective-permute-start | bytes 98312 | tf_op jit(solution)/shard_map/ppermute | solution.py:280
  46.9 5.7 %collective-permute-start.18 = (bf16[2,32,256]{2,1,0:T(8,128)(2,1)S(1)}, bf16[2,32,256]{2,1,0:T(8,128)(2,1)S(1)}, u32[]{:S(2)}, u32[]{:S(2)}) collective-permute-start(bf16[2,32,256]{2,1,0:T(8,128)(2,1)S(1)} %get-tuple-element.83), channel_id=1, source_target_pairs={{0,20},{1,16},{2,4},{3,0},{4,28},{5,24},{6,12},{7,8},{8,21},{9,17}... | collective-permute-start | bytes 98312 | tf_op jit(solution)/shard_map/ppermute | solution.py:280
  47.0 5.7 %collective-permute-start.19 = (bf16[2,32,256]{2,1,0:T(8,128)(2,1)S(1)}, bf16[2,32,256]{2,1,0:T(8,128)(2,1)S(1)}, u32[]{:S(2)}, u32[]{:S(2)}) collective-permute-start(bf16[2,32,256]{2,1,0:T(8,128)(2,1)S(1)} %get-tuple-element.83), channel_id=1, source_target_pairs={{0,4},{1,0},{2,20},{3,16},{4,12},{5,8},{6,28},{7,24},{8,5},{9,1},{... | collective-permute-start | bytes 98312 | tf_op jit(solution)/shard_map/ppermute | solution.py:280
  52.7 1.3 %collective-permute-start.20 = (bf16[2,32,256]{2,1,0:T(8,128)(2,1)S(1)}, bf16[2,32,256]{2,1,0:T(8,128)(2,1)S(1)}, u32[]{:S(2)}, u32[]{:S(2)}) collective-permute-start(bf16[2,32,256]{2,1,0:T(8,128)(2,1)S(1)} %add_convert_fusion.2.refs_8_), channel_id=1, source_target_pairs={{0,4},{1,5},{2,6},{3,7},{4,0},{5,1},{6,2},{7,3},{8,12},{9,13},{10,... | collective-permute-start | bytes 98312 | tf_op jit(solution)/shard_map/ppermute | solution.py:286
  54.3 7.0 %collective-permute-start.21 = (bf16[2,32,256]{2,1,0:T(8,128)(2,1)S(1)}, bf16[2,32,256]{2,1,0:T(8,128)(2,1)S(1)}, u32[]{:S(2)}, u32[]{:S(2)}) collective-permute-start(bf16[2,32,256]{2,1,0:T(8,128)(2,1)S(1)} %get-tuple-element.86), channel_id=1, source_target_pairs={{0,20},{1,16},{2,4},{3,0},{4,28},{5,24},{6,12},{7,8},{8,21},{9,17}... | collective-permute-start | bytes 98312 | tf_op jit(solution)/shard_map/ppermute | solution.py:280
  56.2 5.0 %collective-permute-start.22 = (bf16[2,32,256]{2,1,0:T(8,128)(2,1)S(1)}, bf16[2,32,256]{2,1,0:T(8,128)(2,1)S(1)}, u32[]{:S(2)}, u32[]{:S(2)}) collective-permute-start(bf16[2,32,256]{2,1,0:T(8,128)(2,1)S(1)} %get-tuple-element.86), channel_id=1, source_target_pairs={{0,4},{1,0},{2,20},{3,16},{4,12},{5,8},{6,28},{7,24},{8,5},{9,1},{... | collective-permute-start | bytes 98312 | tf_op jit(solution)/shard_map/ppermute | solution.py:280
  61.3 1.3 %collective-permute-start.23 = (bf16[2,32,256]{2,1,0:T(8,128)(2,1)S(1)}, bf16[2,32,256]{2,1,0:T(8,128)(2,1)S(1)}, u32[]{:S(2)}, u32[]{:S(2)}) collective-permute-start(bf16[2,32,256]{2,1,0:T(8,128)(2,1)S(1)} %add_convert_fusion.1.refs_8_), channel_id=1, source_target_pairs={{0,4},{1,5},{2,6},{3,7},{4,0},{5,1},{6,2},{7,3},{8,12},{9,13},{10,... | collective-permute-start | bytes 98312 | tf_op jit(solution)/shard_map/ppermute | solution.py:286
  62.8 7.0 %collective-permute-start.24 = (bf16[2,32,256]{2,1,0:T(8,128)(2,1)S(1)}, bf16[2,32,256]{2,1,0:T(8,128)(2,1)S(1)}, u32[]{:S(2)}, u32[]{:S(2)}) collective-permute-start(bf16[2,32,256]{2,1,0:T(8,128)(2,1)S(1)} %get-tuple-element.90), channel_id=1, source_target_pairs={{0,20},{1,16},{2,4},{3,0},{4,28},{5,24},{6,12},{7,8},{8,21},{9,17}... | collective-permute-start | bytes 98312 | tf_op jit(solution)/shard_map/ppermute | solution.py:280
  64.5 5.3 %collective-permute-start.25 = (bf16[2,32,256]{2,1,0:T(8,128)(2,1)S(1)}, bf16[2,32,256]{2,1,0:T(8,128)(2,1)S(1)}, u32[]{:S(2)}, u32[]{:S(2)}) collective-permute-start(bf16[2,32,256]{2,1,0:T(8,128)(2,1)S(1)} %get-tuple-element.90), channel_id=1, source_target_pairs={{0,4},{1,0},{2,20},{3,16},{4,12},{5,8},{6,28},{7,24},{8,5},{9,1},{... | collective-permute-start | bytes 98312 | tf_op jit(solution)/shard_map/ppermute | solution.py:280
  69.8 1.3 %collective-permute-start.26 = (bf16[2,32,256]{2,1,0:T(8,128)(2,1)S(1)}, bf16[2,32,256]{2,1,0:T(8,128)(2,1)S(1)}, u32[]{:S(2)}, u32[]{:S(2)}) collective-permute-start(bf16[2,32,256]{2,1,0:T(8,128)(2,1)S(1)} %add_convert_fusion.refs_8_), channel_id=1, source_target_pairs={{0,4},{1,5},{2,6},{3,7},{4,0},{5,1},{6,2},{7,3},{8,12},{9,13},{10,... | collective-permute-start | bytes 98312 | tf_op jit(solution)/shard_map/ppermute | solution.py:286
  71.9 11.6 %collective-permute-start.30 = (bf16[5,32,256]{2,1,0:T(8,128)(2,1)S(1)}, bf16[5,32,256]{2,1,0:T(8,128)(2,1)S(1)}, u32[]{:S(2)}, u32[]{:S(2)}) collective-permute-start(bf16[5,32,256]{2,1,0:T(8,128)(2,1)S(1)} %get-tuple-element.97), channel_id=1, source_target_pairs={{0,7},{1,15},{2,23},{3,31},{4,3},{5,11},{6,19},{7,27},{8,6},{9,14}... | collective-permute-start | bytes 245768 | tf_op jit(solution)/shard_map/ppermute | solution.py:362
  78.0 3.9 %collective-permute-start.27 = (bf16[32,256]{1,0:T(8,128)(2,1)S(1)}, bf16[32,256]{1,0:T(8,128)(2,1)S(1)}, u32[]{:S(2)}, u32[]{:S(2)}) collective-permute-start(bf16[32,256]{1,0:T(8,128)(2,1)S(1)} %get-tuple-element.96), channel_id=1, source_target_pairs={{0,5},{1,4},{2,7},{3,6},{4,1},{5,0},{6,3},{7,2},{8,13},{9,12},{10,... | collective-permute-start | bytes 49160 | tf_op jit(solution)/shard_map/ppermute | solution.py:365
  78.1 4.1 %collective-permute-start.28 = (bf16[32,256]{1,0:T(8,128)(2,1)S(1)}, bf16[32,256]{1,0:T(8,128)(2,1)S(1)}, u32[]{:S(2)}, u32[]{:S(2)}) collective-permute-start(bf16[32,256]{1,0:T(8,128)(2,1)S(1)} %get-tuple-element.96), channel_id=1, source_target_pairs={{0,6},{1,7},{2,4},{3,5},{4,2},{5,3},{6,0},{7,1},{8,14},{9,15},{10,... | collective-permute-start | bytes 49160 | tf_op jit(solution)/shard_map/ppermute | solution.py:365
  78.4 5.1 %collective-permute-start.29 = (bf16[32,256]{1,0:T(8,128)(2,1)S(1)}, bf16[32,256]{1,0:T(8,128)(2,1)S(1)}, u32[]{:S(2)}, u32[]{:S(2)}) collective-permute-start(bf16[32,256]{1,0:T(8,128)(2,1)S(1)} %get-tuple-element.96), channel_id=1, source_target_pairs={{0,7},{1,6},{2,5},{3,4},{4,3},{5,2},{6,1},{7,0},{8,15},{9,14},{10,... | collective-permute-start | bytes 49160 | tf_op jit(solution)/shard_map/ppermute | solution.py:365
  (3 other events, 7.8 us)

commit v6 on v5

--- a/solution.py
+++ b/solution.py
@@ -229,19 +229,21 @@
     else:
         for ref, (_, part) in zip(outs[1:], parts, strict=False):
             ref[...] = part
-        for i, v in enumerate((y4, *solved)):
+        for i, v in enumerate((y4, *solved[1:])):
             outs[3][i] = v[1 - k]
 
 
 def out_kernel(n, *refs):
     own, got = refs[0], refs[1:n]
-    y, moved = refs[n : n + 4], refs[n + 4]
-    forward, solved, forward_ref, solved_ref, sems = refs[n + 5 :]
+    y, moved, inv = refs[n : n + 4], refs[n + 4], refs[n + 5]
+    forward, solved, forward_ref, solved_ref, sems = refs[n + 6 :]
     k, _ = place()
     for level in range(4):
         forward_ref[level, 0] = y[level][k]
-        solved_ref[4 - level, 0] = moved[1 + level]
+    for i in range(1, 4):
+        solved_ref[4 - i, 0] = moved[i]
     forward_ref[4, 0] = moved[0]
+    solved_ref[4, 0] = bf16(dot(moved[0], inv[4], NN))
     solved_ref[0, 0] = bf16(-tree([f32(own[...])] + [f32(g[...]) for g in got]))
     copies = [
         pltpu.make_async_copy(forward_ref, forward, sems.at[0]),
@@ -356,7 +358,7 @@
         pairs = [pair_index(level, level - 1)]
         x[level], msg, *more = call(
             functools.partial(up_kernel, level, pairs),
-            [vec, vec] if level > 1 else [vec, vec[1:], vec[1:], (5, *vec[1:])],
+            [vec, vec] if level > 1 else [vec, vec[1:], vec[1:], slots],
             (keep, gotten, inv, inv_o, mine, other, y[level - 1], y[4], some, rest, ahead, *x[4:level:-1]),
         )
     moved = lax.ppermute(more[1], BOTH, turn_perm(n))
@@ -368,11 +370,11 @@
     return pl.pallas_call(
         functools.partial(out_kernel, n),
         out_shape=[out, out],
-        in_specs=[VMEM] * (n + 5),
+        in_specs=[VMEM] * (n + 6),
         out_specs=[ANY] * 2,
         scratch_shapes=[pltpu.VMEM(out.shape, out.dtype)] * 2 + [pltpu.SemaphoreType.DMA((2,))],
         compiler_params=ROOM,
-    )(msg, *got, *y[:4], moved)
+    )(msg, *got, *y[:4], moved, inv)
 
 
 def solution(mesh):

time: 84.4 us -> 84.5 us (level)
  no operation moved by 1% of the time
where the time goes in v6:
time: 84.5 us; the launch traced here: 84.3 us
  starting transfers between devices  43.9 us (52%)
  waiting for transfers between devices  27.4 us (32%)
  Pallas kernels  10.2 us (12%)
  local copies, waits for them, and re-layouts  0.97 us (1%)
  other arithmetic  0.91 us (1%)
  between operations  0.89 us (1%)
    ppermute x15, starting transfers between devices, on_device(): send = lambda x, perms: [lax.ppermute(x, BOTH, p) for p in perms]  28.7 us
    ppermute x15, waiting for transfers between devices, on_device(): send = lambda x, perms: [lax.ppermute(x, BOTH, p) for p in perms]  20.5 us
    ppermute x1, starting transfers between devices, on_device(): moved = lax.ppermute(more[1], BOTH, turn_perm(n))  6.12 us
    pallas_call x11, Pallas kernels, call(): pl.pallas_call(body, out_shape=[jax.ShapeDtypeStruct(s, dtype) for s in o...  4.63 us
    ppermute x3, starting transfers between devices, on_device(): got = {m: lax.ppermute(more[0], BOTH, lines[m - 1]) for m in order}  3.87 us
    ppermute x6, waiting for transfers between devices, share(): return (got, some, swap(some))  3.32 us
    pallas_call x1, Pallas kernels, on_device(): pl.pallas_call(start_kernel, grid=(1,), out_shape=[jax.ShapeDtypeStruct(s...  2.35 us
    ppermute x1, starting transfers between devices, on_device(): inv_to = lax.ppermute(last, BOTH, far_perm(n))  2.22 us
  transfers between devices with their start and end apart: 31, of which 16 were waited for; matrix products, arithmetic and copies ran while one was open for 0% of the time, Pallas kernels for 6%

profile of v6, /device:TPU:0, one launch (start us, length us, event | category | flops | bytes accessed | tf_op | source)
XLA Modules:
  0.0 84.3 jit_solution(3717817044584166957)
XLA Ops:
  0.6 2.4 %shard_map.59 = (f32[4,32,256]{2,1,0:T(8,128)}, f32[4,32,256]{2,1,0:T(8,128)}, bf16[192,256]{1,0:T(8,128)(2,1)}) custom-call(s32[2,1,10]{2,1,0:T(1,128)} %bitcast.35, bf16[5,32,256]{2,1,0:T(8,128)(2,1)} %bitcast.30, bf16[5,256,256]{2,1,0:T(8,128)(2,1)} %bitcast.19, bf16[5,256,256]{2,1,0:T(8,128)(2,1)} %bitcast.20, bf16[10,2,256,256]{3,2,1,0:T(8,128)(2,1)} %bitcast.4), custom_call_target="tpu_custom_call" | custom-call | tf_op jit(solution)/shard_map/pallas_call | solution.py:291
  3.5 1.2 %collective-permute-done.gotten_in = f32[4,32,256]{2,1,0:T(8,128)S(1)} collective-permute-done((f32[4,32,256]{2,1,0:T(8,128)}, f32[4,32,256]{2,1,0:T(8,128)S(1)}, u32[]{:S(2)}, u32[]{:S(2)}) %collective-permute-start) | collective-permute-done | bytes 131104 | tf_op jit(solution)/shard_map/ppermute | solution.py:299
  4.7 0.8 %fusion = bf16[2,32,256]{2,1,0:T(8,128)(2,1)S(1)} fusion(f32[4,32,256]{2,1,0:T(8,128)S(1)} %collective-permute-done.gotten_in, f32[4,32,256]{2,1,0:T(8,128)} %get-tuple-element.50.keep_in), kind=kLoop, calls=%fused_computation.1 | loop fusion | flops 32768 | bytes 163840 | tf_op jit(solution)/shard_map/convert_element_type | solution.py:70
  6.5 4.5 %collective-permute-start.5 = (bf16[2,32,256]{2,1,0:T(8,128)(2,1)S(1)}, bf16[2,32,256]{2,1,0:T(8,128)(2,1)S(1)}, u32[]{:S(2)}, u32[]{:S(2)}) collective-permute-start(bf16[2,32,256]{2,1,0:T(8,128)(2,1)S(1)} %fusion), channel_id=1, source_target_pairs={{0,6},{1,14},{2,22},{3,30},{4,7},{5,15},{6,23},{7,31},{8,2},{9,10}... | collective-permute-start | bytes 98312 | tf_op jit(solution)/shard_map/ppermute | solution.py:282
  10.9 2.2 %collective-permute-start.7 = (bf16[192,256]{1,0:T(8,128)(2,1)}, bf16[192,256]{1,0:T(8,128)(2,1)S(1)}, u32[]{:S(2)}, u32[]{:S(2)}) collective-permute-start(bf16[192,256]{1,0:T(8,128)(2,1)} %get-tuple-element.65), channel_id=1, source_target_pairs={{0,28},{1,20},{2,12},{3,4},{4,24},{5,16},{6,8},{7,0},{8,29},{9,21}... | collective-permute-start | bytes 294920 | tf_op jit(solution)/shard_map/ppermute | solution.py:303
  13.1 1.1 %collective-permute-done.5 = bf16[2,32,256]{2,1,0:T(8,128)(2,1)S(1)} collective-permute-done((bf16[2,32,256]{2,1,0:T(8,128)(2,1)S(1)}, bf16[2,32,256]{2,1,0:T(8,128)(2,1)S(1)}, u32[]{:S(2)}, u32[]{:S(2)}) %collective-permute-start.5) | collective-permute-done | bytes 32800 | tf_op jit(solution)/shard_map/ppermute | solution.py:282
  14.4 1.0 %copy-done.3 = f32[4,32,256]{2,1,0:T(8,128)S(1)} copy-done((f32[4,32,256]{2,1,0:T(8,128)S(1)}, f32[4,32,256]{2,1,0:T(8,128)}, u32[]{:S(2)}) %copy-start.3) | copy-done | bytes 131096
  15.4 0.8 shard_map.60
  17.4 1.9 %collective-permute-start.10 = (bf16[2,32,256]{2,1,0:T(8,128)(2,1)S(1)}, bf16[2,32,256]{2,1,0:T(8,128)(2,1)S(1)}, u32[]{:S(2)}, u32[]{:S(2)}) collective-permute-start(bf16[2,32,256]{2,1,0:T(8,128)(2,1)S(1)} %get-tuple-element.66), channel_id=1, source_target_pairs={{0,6},{1,14},{2,22},{3,30},{4,7},{5,15},{6,23},{7,31},{8,2},{9,10}... | collective-permute-start | bytes 98312 | tf_op jit(solution)/shard_map/ppermute | solution.py:282
  19.3 2.4 %collective-permute-start.8 = (bf16[2,32,256]{2,1,0:T(8,128)(2,1)S(1)}, bf16[2,32,256]{2,1,0:T(8,128)(2,1)S(1)}, u32[]{:S(2)}, u32[]{:S(2)}) collective-permute-start(bf16[2,32,256]{2,1,0:T(8,128)(2,1)S(1)} %get-tuple-element.66), channel_id=1, source_target_pairs={{0,4},{1,12},{2,20},{3,28},{4,5},{5,13},{6,21},{7,29},{8,0},{9,8},... | collective-permute-start | bytes 98312 | tf_op jit(solution)/shard_map/ppermute | solution.py:282
  21.7 2.1 %collective-permute-done.10 = bf16[2,32,256]{2,1,0:T(8,128)(2,1)S(1)} collective-permute-done((bf16[2,32,256]{2,1,0:T(8,128)(2,1)S(1)}, bf16[2,32,256]{2,1,0:T(8,128)(2,1)S(1)}, u32[]{:S(2)}, u32[]{:S(2)}) %collective-permute-start.10) | collective-permute-done | bytes 32800 | tf_op jit(solution)/shard_map/ppermute | solution.py:282
  23.8 1.6 %collective-permute-start.11 = (bf16[2,32,256]{2,1,0:T(8,128)(2,1)S(1)}, bf16[2,32,256]{2,1,0:T(8,128)(2,1)S(1)}, u32[]{:S(2)}, u32[]{:S(2)}) collective-permute-start(bf16[2,32,256]{2,1,0:T(8,128)(2,1)S(1)} %add_convert_fusion.4.refs_9_), channel_id=1, source_target_pairs={{0,4},{1,5},{2,6},{3,7},{4,0},{5,1},{6,2},{7,3},{8,12},{9,13},{10,... | collective-permute-start | bytes 98312 | tf_op jit(solution)/shard_map/ppermute | solution.py:288
  25.4 1.6 %shard_map.62 = (bf16[5,256,256]{2,1,0:T(8,128)(2,1)S(1)}, bf16[10,2,256,256]{3,2,1,0:T(8,128)(2,1)S(1)}, f32[2,32,256]{2,1,0:T(8,128)S(1)}) custom-call(f32[4,32,256]{2,1,0:T(8,128)S(1)} %get-tuple-element.56.refs_0_.keep, f32[4,32,256]{2,1,0:T(8,128)S(1)} %get-tuple-element.57.refs_1_.gotten, bf16[10,2,256,256]{3,2,1,0:T(8,128)(2,1)S(1)} %bitcast.8, ...), custom_call_target="tpu_custom_call" | custom-call | tf_op jit(solution)/shard_map/pallas_call | solution.py:323
  27.5 5.2 %collective-permute-start.13 = (bf16[2,32,256]{2,1,0:T(8,128)(2,1)S(1)}, bf16[2,32,256]{2,1,0:T(8,128)(2,1)S(1)}, u32[]{:S(2)}, u32[]{:S(2)}) collective-permute-start(bf16[2,32,256]{2,1,0:T(8,128)(2,1)S(1)} %get-tuple-element.76), channel_id=1, source_target_pairs={{0,6},{1,14},{2,22},{3,30},{4,7},{5,15},{6,23},{7,31},{8,2},{9,10}... | collective-permute-start | bytes 98312 | tf_op jit(solution)/shard_map/ppermute | solution.py:282
  32.7 3.5 %collective-permute-done.13 = bf16[2,32,256]{2,1,0:T(8,128)(2,1)S(1)} collective-permute-done((bf16[2,32,256]{2,1,0:T(8,128)(2,1)S(1)}, bf16[2,32,256]{2,1,0:T(8,128)(2,1)S(1)}, u32[]{:S(2)}, u32[]{:S(2)}) %collective-permute-start.13) | collective-permute-done | bytes 32800 | tf_op jit(solution)/shard_map/ppermute | solution.py:282
  37.9 1.3 %collective-permute-start.15 = (bf16[2,32,256]{2,1,0:T(8,128)(2,1)S(1)}, bf16[2,32,256]{2,1,0:T(8,128)(2,1)S(1)}, u32[]{:S(2)}, u32[]{:S(2)}) collective-permute-start(bf16[2,32,256]{2,1,0:T(8,128)(2,1)S(1)} %get-tuple-element.81.refs_9_), channel_id=1, source_target_pairs={{0,12},{1,13},{2,14},{3,15},{4,8},{5,9},{6,10},{7,11},{8,4},{9,5},... | collective-permute-start | bytes 98312 | tf_op jit(solution)/shard_map/ppermute | solution.py:282
  39.2 2.9 %collective-permute-start.16 = (bf16[2,32,256]{2,1,0:T(8,128)(2,1)S(1)}, bf16[2,32,256]{2,1,0:T(8,128)(2,1)S(1)}, u32[]{:S(2)}, u32[]{:S(2)}) collective-permute-start(bf16[2,32,256]{2,1,0:T(8,128)(2,1)S(1)} %get-tuple-element.81.refs_9_), channel_id=1, source_target_pairs={{0,20},{1,21},{2,22},{3,23},{4,16},{5,17},{6,18},{7,19},{8,28},{9,... | collective-permute-start | bytes 98312 | tf_op jit(solution)/shard_map/ppermute | solution.py:282
  42.2 1.5 %collective-permute-done.16.refs_11_ = bf16[2,32,256]{2,1,0:T(8,128)(2,1)S(1)} collective-permute-done((bf16[2,32,256]{2,1,0:T(8,128)(2,1)S(1)}, bf16[2,32,256]{2,1,0:T(8,128)(2,1)S(1)}, u32[]{:S(2)}, u32[]{:S(2)}) %collective-permute-start.16) | collective-permute-done | bytes 32800 | tf_op jit(solution)/shard_map/ppermute | solution.py:282
  43.7 2.6 %collective-permute-done.17.refs_12_ = bf16[2,32,256]{2,1,0:T(8,128)(2,1)S(1)} collective-permute-done((bf16[2,32,256]{2,1,0:T(8,128)(2,1)S(1)}, bf16[2,32,256]{2,1,0:T(8,128)(2,1)S(1)}, u32[]{:S(2)}, u32[]{:S(2)}) %collective-permute-start.17) | collective-permute-done | bytes 32800 | tf_op jit(solution)/shard_map/ppermute | solution.py:282
  47.3 5.4 %collective-permute-done.18 = bf16[2,32,256]{2,1,0:T(8,128)(2,1)S(1)} collective-permute-done((bf16[2,32,256]{2,1,0:T(8,128)(2,1)S(1)}, bf16[2,32,256]{2,1,0:T(8,128)(2,1)S(1)}, u32[]{:S(2)}, u32[]{:S(2)}) %collective-permute-start.18) | collective-permute-done | bytes 32800 | tf_op jit(solution)/shard_map/ppermute | solution.py:282
  53.0 1.0 %collective-permute-done.20.refs_9_ = bf16[2,32,256]{2,1,0:T(8,128)(2,1)S(1)} collective-permute-done((bf16[2,32,256]{2,1,0:T(8,128)(2,1)S(1)}, bf16[2,32,256]{2,1,0:T(8,128)(2,1)S(1)}, u32[]{:S(2)}, u32[]{:S(2)}) %collective-permute-start.20) | collective-permute-done | bytes 32800 | tf_op jit(solution)/shard_map/ppermute | solution.py:288
  54.3 1.9 %collective-permute-start.21 = (bf16[2,32,256]{2,1,0:T(8,128)(2,1)S(1)}, bf16[2,32,256]{2,1,0:T(8,128)(2,1)S(1)}, u32[]{:S(2)}, u32[]{:S(2)}) collective-permute-start(bf16[2,32,256]{2,1,0:T(8,128)(2,1)S(1)} %get-tuple-element.86), channel_id=1, source_target_pairs={{0,20},{1,16},{2,4},{3,0},{4,28},{5,24},{6,12},{7,8},{8,21},{9,17}... | collective-permute-start | bytes 98312 | tf_op jit(solution)/shard_map/ppermute | solution.py:282
  56.2 2.9 %collective-permute-start.22 = (bf16[2,32,256]{2,1,0:T(8,128)(2,1)S(1)}, bf16[2,32,256]{2,1,0:T(8,128)(2,1)S(1)}, u32[]{:S(2)}, u32[]{:S(2)}) collective-permute-start(bf16[2,32,256]{2,1,0:T(8,128)(2,1)S(1)} %get-tuple-element.86), channel_id=1, source_target_pairs={{0,4},{1,0},{2,20},{3,16},{4,12},{5,8},{6,28},{7,24},{8,5},{9,1},{... | collective-permute-start | bytes 98312 | tf_op jit(solution)/shard_map/ppermute | solution.py:282
  59.1 2.2 %collective-permute-done.21 = bf16[2,32,256]{2,1,0:T(8,128)(2,1)S(1)} collective-permute-done((bf16[2,32,256]{2,1,0:T(8,128)(2,1)S(1)}, bf16[2,32,256]{2,1,0:T(8,128)(2,1)S(1)}, u32[]{:S(2)}, u32[]{:S(2)}) %collective-permute-start.21) | collective-permute-done | bytes 32800 | tf_op jit(solution)/shard_map/ppermute | solution.py:282
  61.6 0.9 %collective-permute-done.23.refs_9_ = bf16[2,32,256]{2,1,0:T(8,128)(2,1)S(1)} collective-permute-done((bf16[2,32,256]{2,1,0:T(8,128)(2,1)S(1)}, bf16[2,32,256]{2,1,0:T(8,128)(2,1)S(1)}, u32[]{:S(2)}, u32[]{:S(2)}) %collective-permute-start.23) | collective-permute-done | bytes 32800 | tf_op jit(solution)/shard_map/ppermute | solution.py:288
  62.8 1.7 %collective-permute-start.24 = (bf16[2,32,256]{2,1,0:T(8,128)(2,1)S(1)}, bf16[2,32,256]{2,1,0:T(8,128)(2,1)S(1)}, u32[]{:S(2)}, u32[]{:S(2)}) collective-permute-start(bf16[2,32,256]{2,1,0:T(8,128)(2,1)S(1)} %get-tuple-element.90), channel_id=1, source_target_pairs={{0,20},{1,16},{2,4},{3,0},{4,28},{5,24},{6,12},{7,8},{8,21},{9,17}... | collective-permute-start | bytes 98312 | tf_op jit(solution)/shard_map/ppermute | solution.py:282
  64.5 3.2 %collective-permute-start.25 = (bf16[2,32,256]{2,1,0:T(8,128)(2,1)S(1)}, bf16[2,32,256]{2,1,0:T(8,128)(2,1)S(1)}, u32[]{:S(2)}, u32[]{:S(2)}) collective-permute-start(bf16[2,32,256]{2,1,0:T(8,128)(2,1)S(1)} %get-tuple-element.90), channel_id=1, source_target_pairs={{0,4},{1,0},{2,20},{3,16},{4,12},{5,8},{6,28},{7,24},{8,5},{9,1},{... | collective-permute-start | bytes 98312 | tf_op jit(solution)/shard_map/ppermute | solution.py:282
  67.7 2.1 %collective-permute-done.24 = bf16[2,32,256]{2,1,0:T(8,128)(2,1)S(1)} collective-permute-done((bf16[2,32,256]{2,1,0:T(8,128)(2,1)S(1)}, bf16[2,32,256]{2,1,0:T(8,128)(2,1)S(1)}, u32[]{:S(2)}, u32[]{:S(2)}) %collective-permute-start.24) | collective-permute-done | bytes 32800 | tf_op jit(solution)/shard_map/ppermute | solution.py:282
  71.1 0.8 shard_map.72
  71.9 6.1 %collective-permute-start.30 = (bf16[4,32,256]{2,1,0:T(8,128)(2,1)S(1)}, bf16[4,32,256]{2,1,0:T(8,128)(2,1)S(1)}, u32[]{:S(2)}, u32[]{:S(2)}) collective-permute-start(bf16[4,32,256]{2,1,0:T(8,128)(2,1)S(1)} %get-tuple-element.97), channel_id=1, source_target_pairs={{0,7},{1,15},{2,23},{3,31},{4,3},{5,11},{6,19},{7,27},{8,6},{9,14}... | collective-permute-start | bytes 196616 | tf_op jit(solution)/shard_map/ppermute | solution.py:364
  78.4 3.5 %collective-permute-start.29 = (bf16[32,256]{1,0:T(8,128)(2,1)S(1)}, bf16[32,256]{1,0:T(8,128)(2,1)S(1)}, u32[]{:S(2)}, u32[]{:S(2)}) collective-permute-start(bf16[32,256]{1,0:T(8,128)(2,1)S(1)} %get-tuple-element.96), channel_id=1, source_target_pairs={{0,7},{1,6},{2,5},{3,4},{4,3},{5,2},{6,1},{7,0},{8,15},{9,14},{10,... | collective-permute-start | bytes 49160 | tf_op jit(solution)/shard_map/ppermute | solution.py:367
  82.1 1.4 %collective-permute-done.29.refs_3_ = bf16[32,256]{1,0:T(8,128)(2,1)S(1)} collective-permute-done((bf16[32,256]{1,0:T(8,128)(2,1)S(1)}, bf16[32,256]{1,0:T(8,128)(2,1)S(1)}, u32[]{:S(2)}, u32[]{:S(2)}) %collective-permute-start.29) | collective-permute-done | bytes 16416 | tf_op jit(solution)/shard_map/ppermute | solution.py:367
  (60 shorter events, 9.8 us)
Async XLA Ops:
  0.6 12.5 %copy-start.2 = (bf16[5,1,32,256]{3,2,1,0:T(8,128)(2,1)S(1)}, bf16[5,1,32,256]{3,2,1,0:T(8,128)(2,1)}, u32[]{:S(2)}) copy-start(bf16[5,1,32,256]{3,2,1,0:T(8,128)(2,1)} %param.4) | copy-start | bytes 245764
  3.0 1.6 %collective-permute-start = (f32[4,32,256]{2,1,0:T(8,128)}, f32[4,32,256]{2,1,0:T(8,128)S(1)}, u32[]{:S(2)}, u32[]{:S(2)}) collective-permute-start(f32[4,32,256]{2,1,0:T(8,128)} %get-tuple-element.51), channel_id=1, source_target_pairs={{0,4},{1,5},{2,6},{3,7},{4,0},{5,1},{6,2},{7,3},{8,12},{9,13},{10,... | collective-permute-start | bytes 393224 | tf_op jit(solution)/shard_map/ppermute | solution.py:299
  5.5 8.9 %collective-permute-start.2 = (bf16[10,2,256,256]{3,2,1,0:T(8,128)(2,1)S(1)}, bf16[10,2,256,256]{3,2,1,0:T(8,128)(2,1)S(1)}, u32[]{:S(2)}, u32[]{:S(2)}) collective-permute-start(bf16[10,2,256,256]{3,2,1,0:T(8,128)(2,1)S(1)} %bitcast.5), channel_id=1, source_target_pairs={{0,4},{1,5},{2,6},{3,7},{4,0},{5,1},{6,2},{7,3},{8,12},{9,13},{10,... | collective-permute-start | bytes 7864328 | tf_op jit(solution)/shard_map/ppermute | solution.py:302
  5.9 8.5 %collective-permute-start.1 = (bf16[5,256,256]{2,1,0:T(8,128)(2,1)}, bf16[5,256,256]{2,1,0:T(8,128)(2,1)S(1)}, u32[]{:S(2)}, u32[]{:S(2)}) collective-permute-start(bf16[5,256,256]{2,1,0:T(8,128)(2,1)} %bitcast.21), channel_id=1, source_target_pairs={{0,4},{1,5},{2,6},{3,7},{4,0},{5,1},{6,2},{7,3},{8,12},{9,13},{10,... | collective-permute-start | bytes 1966088 | tf_op jit(solution)/shard_map/ppermute | solution.py:302
  6.1 7.0 %collective-permute-start.3 = (bf16[2,32,256]{2,1,0:T(8,128)(2,1)S(1)}, bf16[2,32,256]{2,1,0:T(8,128)(2,1)S(1)}, u32[]{:S(2)}, u32[]{:S(2)}) collective-permute-start(bf16[2,32,256]{2,1,0:T(8,128)(2,1)S(1)} %fusion), channel_id=1, source_target_pairs={{0,4},{1,12},{2,20},{3,28},{4,5},{5,13},{6,21},{7,29},{8,0},{9,8},... | collective-permute-start | bytes 98312 | tf_op jit(solution)/shard_map/ppermute | solution.py:282
  6.5 7.8 %collective-permute-start.5 = (bf16[2,32,256]{2,1,0:T(8,128)(2,1)S(1)}, bf16[2,32,256]{2,1,0:T(8,128)(2,1)S(1)}, u32[]{:S(2)}, u32[]{:S(2)}) collective-permute-start(bf16[2,32,256]{2,1,0:T(8,128)(2,1)S(1)} %fusion), channel_id=1, source_target_pairs={{0,6},{1,14},{2,22},{3,30},{4,7},{5,15},{6,23},{7,31},{8,2},{9,10}... | collective-permute-start | bytes 98312 | tf_op jit(solution)/shard_map/ppermute | solution.py:282
  10.9 6.5 %collective-permute-start.7 = (bf16[192,256]{1,0:T(8,128)(2,1)}, bf16[192,256]{1,0:T(8,128)(2,1)S(1)}, u32[]{:S(2)}, u32[]{:S(2)}) collective-permute-start(bf16[192,256]{1,0:T(8,128)(2,1)} %get-tuple-element.65), channel_id=1, source_target_pairs={{0,28},{1,20},{2,12},{3,4},{4,24},{5,16},{6,8},{7,0},{8,29},{9,21}... | collective-permute-start | bytes 294920 | tf_op jit(solution)/shard_map/ppermute | solution.py:303
  13.1 3.1 %collective-permute-start.4 = (bf16[5,32,256]{2,1,0:T(8,128)(2,1)S(1)}, bf16[5,32,256]{2,1,0:T(8,128)(2,1)S(1)}, u32[]{:S(2)}, u32[]{:S(2)}) collective-permute-start(bf16[5,32,256]{2,1,0:T(8,128)(2,1)S(1)} %bitcast.31), channel_id=1, source_target_pairs={{0,4},{1,5},{2,6},{3,7},{4,0},{5,1},{6,2},{7,3},{8,12},{9,13},{10,... | collective-permute-start | bytes 245768 | tf_op jit(solution)/shard_map/ppermute | solution.py:302
  14.3 1.9 %collective-permute-start.6 = (bf16[2,32,256]{2,1,0:T(8,128)(2,1)S(1)}, bf16[2,32,256]{2,1,0:T(8,128)(2,1)S(1)}, u32[]{:S(2)}, u32[]{:S(2)}) collective-permute-start(bf16[2,32,256]{2,1,0:T(8,128)(2,1)S(1)} %add_convert_fusion.5.refs_9_), channel_id=1, source_target_pairs={{0,4},{1,5},{2,6},{3,7},{4,0},{5,1},{6,2},{7,3},{8,12},{9,13},{10,... | collective-permute-start | bytes 98312 | tf_op jit(solution)/shard_map/ppermute | solution.py:288
  17.4 6.4 %collective-permute-start.10 = (bf16[2,32,256]{2,1,0:T(8,128)(2,1)S(1)}, bf16[2,32,256]{2,1,0:T(8,128)(2,1)S(1)}, u32[]{:S(2)}, u32[]{:S(2)}) collective-permute-start(bf16[2,32,256]{2,1,0:T(8,128)(2,1)S(1)} %get-tuple-element.66), channel_id=1, source_target_pairs={{0,6},{1,14},{2,22},{3,30},{4,7},{5,15},{6,23},{7,31},{8,2},{9,10}... | collective-permute-start | bytes 98312 | tf_op jit(solution)/shard_map/ppermute | solution.py:282
  19.3 4.5 %collective-permute-start.8 = (bf16[2,32,256]{2,1,0:T(8,128)(2,1)S(1)}, bf16[2,32,256]{2,1,0:T(8,128)(2,1)S(1)}, u32[]{:S(2)}, u32[]{:S(2)}) collective-permute-start(bf16[2,32,256]{2,1,0:T(8,128)(2,1)S(1)} %get-tuple-element.66), channel_id=1, source_target_pairs={{0,4},{1,12},{2,20},{3,28},{4,5},{5,13},{6,21},{7,29},{8,0},{9,8},... | collective-permute-start | bytes 98312 | tf_op jit(solution)/shard_map/ppermute | solution.py:282
  23.8 3.2 %collective-permute-start.11 = (bf16[2,32,256]{2,1,0:T(8,128)(2,1)S(1)}, bf16[2,32,256]{2,1,0:T(8,128)(2,1)S(1)}, u32[]{:S(2)}, u32[]{:S(2)}) collective-permute-start(bf16[2,32,256]{2,1,0:T(8,128)(2,1)S(1)} %add_convert_fusion.4.refs_9_), channel_id=1, source_target_pairs={{0,4},{1,5},{2,6},{3,7},{4,0},{5,1},{6,2},{7,3},{8,12},{9,13},{10,... | collective-permute-start | bytes 98312 | tf_op jit(solution)/shard_map/ppermute | solution.py:288
  27.4 5.3 %collective-permute-start.12 = (bf16[2,32,256]{2,1,0:T(8,128)(2,1)S(1)}, bf16[2,32,256]{2,1,0:T(8,128)(2,1)S(1)}, u32[]{:S(2)}, u32[]{:S(2)}) collective-permute-start(bf16[2,32,256]{2,1,0:T(8,128)(2,1)S(1)} %get-tuple-element.76), channel_id=1, source_target_pairs={{0,4},{1,12},{2,20},{3,28},{4,5},{5,13},{6,21},{7,29},{8,0},{9,8},... | collective-permute-start | bytes 98312 | tf_op jit(solution)/shard_map/ppermute | solution.py:282
  27.5 8.7 %collective-permute-start.13 = (bf16[2,32,256]{2,1,0:T(8,128)(2,1)S(1)}, bf16[2,32,256]{2,1,0:T(8,128)(2,1)S(1)}, u32[]{:S(2)}, u32[]{:S(2)}) collective-permute-start(bf16[2,32,256]{2,1,0:T(8,128)(2,1)S(1)} %get-tuple-element.76), channel_id=1, source_target_pairs={{0,6},{1,14},{2,22},{3,30},{4,7},{5,15},{6,23},{7,31},{8,2},{9,10}... | collective-permute-start | bytes 98312 | tf_op jit(solution)/shard_map/ppermute | solution.py:282
  32.7 9.5 %collective-permute-start.9 = (bf16[192,256]{1,0:T(8,128)(2,1)S(1)}, bf16[192,256]{1,0:T(8,128)(2,1)S(1)}, u32[]{:S(2)}, u32[]{:S(2)}) collective-permute-start(bf16[192,256]{1,0:T(8,128)(2,1)S(1)} %collective-permute-done.7.refs_3_), channel_id=1, source_target_pairs={{0,4},{1,5},{2,6},{3,7},{4,0},{5,1},{6,2},{7,3},{8,12},{9,13},{10,... | collective-permute-start | bytes 294920 | tf_op jit(solution)/shard_map/ppermute | solution.py:343
  36.3 1.3 %collective-permute-start.14 = (bf16[2,32,256]{2,1,0:T(8,128)(2,1)S(1)}, bf16[2,32,256]{2,1,0:T(8,128)(2,1)S(1)}, u32[]{:S(2)}, u32[]{:S(2)}) collective-permute-start(bf16[2,32,256]{2,1,0:T(8,128)(2,1)S(1)} %add_convert_fusion.3.refs_9_), channel_id=1, source_target_pairs={{0,4},{1,5},{2,6},{3,7},{4,0},{5,1},{6,2},{7,3},{8,12},{9,13},{10,... | collective-permute-start | bytes 98312 | tf_op jit(solution)/shard_map/ppermute | solution.py:288
  37.9 4.3 %collective-permute-start.15 = (bf16[2,32,256]{2,1,0:T(8,128)(2,1)S(1)}, bf16[2,32,256]{2,1,0:T(8,128)(2,1)S(1)}, u32[]{:S(2)}, u32[]{:S(2)}) collective-permute-start(bf16[2,32,256]{2,1,0:T(8,128)(2,1)S(1)} %get-tuple-element.81.refs_9_), channel_id=1, source_target_pairs={{0,12},{1,13},{2,14},{3,15},{4,8},{5,9},{6,10},{7,11},{8,4},{9,5},... | collective-permute-start | bytes 98312 | tf_op jit(solution)/shard_map/ppermute | solution.py:282
  39.2 4.5 %collective-permute-start.16 = (bf16[2,32,256]{2,1,0:T(8,128)(2,1)S(1)}, bf16[2,32,256]{2,1,0:T(8,128)(2,1)S(1)}, u32[]{:S(2)}, u32[]{:S(2)}) collective-permute-start(bf16[2,32,256]{2,1,0:T(8,128)(2,1)S(1)} %get-tuple-element.81.refs_9_), channel_id=1, source_target_pairs={{0,20},{1,21},{2,22},{3,23},{4,16},{5,17},{6,18},{7,19},{8,28},{9,... | collective-permute-start | bytes 98312 | tf_op jit(solution)/shard_map/ppermute | solution.py:282
  42.1 4.2 %collective-permute-start.17 = (bf16[2,32,256]{2,1,0:T(8,128)(2,1)S(1)}, bf16[2,32,256]{2,1,0:T(8,128)(2,1)S(1)}, u32[]{:S(2)}, u32[]{:S(2)}) collective-permute-start(bf16[2,32,256]{2,1,0:T(8,128)(2,1)S(1)} %get-tuple-element.81.refs_9_), channel_id=1, source_target_pairs={{0,28},{1,29},{2,30},{3,31},{4,24},{5,25},{6,26},{7,27},{8,20},{9,... | collective-permute-start | bytes 98312 | tf_op jit(solution)/shard_map/ppermute | solution.py:282
  46.9 5.7 %collective-permute-start.18 = (bf16[2,32,256]{2,1,0:T(8,128)(2,1)S(1)}, bf16[2,32,256]{2,1,0:T(8,128)(2,1)S(1)}, u32[]{:S(2)}, u32[]{:S(2)}) collective-permute-start(bf16[2,32,256]{2,1,0:T(8,128)(2,1)S(1)} %get-tuple-element.83), channel_id=1, source_target_pairs={{0,20},{1,16},{2,4},{3,0},{4,28},{5,24},{6,12},{7,8},{8,21},{9,17}... | collective-permute-start | bytes 98312 | tf_op jit(solution)/shard_map/ppermute | solution.py:282
  47.0 5.7 %collective-permute-start.19 = (bf16[2,32,256]{2,1,0:T(8,128)(2,1)S(1)}, bf16[2,32,256]{2,1,0:T(8,128)(2,1)S(1)}, u32[]{:S(2)}, u32[]{:S(2)}) collective-permute-start(bf16[2,32,256]{2,1,0:T(8,128)(2,1)S(1)} %get-tuple-element.83), channel_id=1, source_target_pairs={{0,4},{1,0},{2,20},{3,16},{4,12},{5,8},{6,28},{7,24},{8,5},{9,1},{... | collective-permute-start | bytes 98312 | tf_op jit(solution)/shard_map/ppermute | solution.py:282
  52.7 1.3 %collective-permute-start.20 = (bf16[2,32,256]{2,1,0:T(8,128)(2,1)S(1)}, bf16[2,32,256]{2,1,0:T(8,128)(2,1)S(1)}, u32[]{:S(2)}, u32[]{:S(2)}) collective-permute-start(bf16[2,32,256]{2,1,0:T(8,128)(2,1)S(1)} %add_convert_fusion.2.refs_8_), channel_id=1, source_target_pairs={{0,4},{1,5},{2,6},{3,7},{4,0},{5,1},{6,2},{7,3},{8,12},{9,13},{10,... | collective-permute-start | bytes 98312 | tf_op jit(solution)/shard_map/ppermute | solution.py:288
  54.3 7.0 %collective-permute-start.21 = (bf16[2,32,256]{2,1,0:T(8,128)(2,1)S(1)}, bf16[2,32,256]{2,1,0:T(8,128)(2,1)S(1)}, u32[]{:S(2)}, u32[]{:S(2)}) collective-permute-start(bf16[2,32,256]{2,1,0:T(8,128)(2,1)S(1)} %get-tuple-element.86), channel_id=1, source_target_pairs={{0,20},{1,16},{2,4},{3,0},{4,28},{5,24},{6,12},{7,8},{8,21},{9,17}... | collective-permute-start | bytes 98312 | tf_op jit(solution)/shard_map/ppermute | solution.py:282
  56.2 5.0 %collective-permute-start.22 = (bf16[2,32,256]{2,1,0:T(8,128)(2,1)S(1)}, bf16[2,32,256]{2,1,0:T(8,128)(2,1)S(1)}, u32[]{:S(2)}, u32[]{:S(2)}) collective-permute-start(bf16[2,32,256]{2,1,0:T(8,128)(2,1)S(1)} %get-tuple-element.86), channel_id=1, source_target_pairs={{0,4},{1,0},{2,20},{3,16},{4,12},{5,8},{6,28},{7,24},{8,5},{9,1},{... | collective-permute-start | bytes 98312 | tf_op jit(solution)/shard_map/ppermute | solution.py:282
  61.3 1.3 %collective-permute-start.23 = (bf16[2,32,256]{2,1,0:T(8,128)(2,1)S(1)}, bf16[2,32,256]{2,1,0:T(8,128)(2,1)S(1)}, u32[]{:S(2)}, u32[]{:S(2)}) collective-permute-start(bf16[2,32,256]{2,1,0:T(8,128)(2,1)S(1)} %add_convert_fusion.1.refs_8_), channel_id=1, source_target_pairs={{0,4},{1,5},{2,6},{3,7},{4,0},{5,1},{6,2},{7,3},{8,12},{9,13},{10,... | collective-permute-start | bytes 98312 | tf_op jit(solution)/shard_map/ppermute | solution.py:288
  62.8 7.0 %collective-permute-start.24 = (bf16[2,32,256]{2,1,0:T(8,128)(2,1)S(1)}, bf16[2,32,256]{2,1,0:T(8,128)(2,1)S(1)}, u32[]{:S(2)}, u32[]{:S(2)}) collective-permute-start(bf16[2,32,256]{2,1,0:T(8,128)(2,1)S(1)} %get-tuple-element.90), channel_id=1, source_target_pairs={{0,20},{1,16},{2,4},{3,0},{4,28},{5,24},{6,12},{7,8},{8,21},{9,17}... | collective-permute-start | bytes 98312 | tf_op jit(solution)/shard_map/ppermute | solution.py:282
  64.5 5.3 %collective-permute-start.25 = (bf16[2,32,256]{2,1,0:T(8,128)(2,1)S(1)}, bf16[2,32,256]{2,1,0:T(8,128)(2,1)S(1)}, u32[]{:S(2)}, u32[]{:S(2)}) collective-permute-start(bf16[2,32,256]{2,1,0:T(8,128)(2,1)S(1)} %get-tuple-element.90), channel_id=1, source_target_pairs={{0,4},{1,0},{2,20},{3,16},{4,12},{5,8},{6,28},{7,24},{8,5},{9,1},{... | collective-permute-start | bytes 98312 | tf_op jit(solution)/shard_map/ppermute | solution.py:282
  69.8 1.3 %collective-permute-start.26 = (bf16[2,32,256]{2,1,0:T(8,128)(2,1)S(1)}, bf16[2,32,256]{2,1,0:T(8,128)(2,1)S(1)}, u32[]{:S(2)}, u32[]{:S(2)}) collective-permute-start(bf16[2,32,256]{2,1,0:T(8,128)(2,1)S(1)} %add_convert_fusion.refs_8_), channel_id=1, source_target_pairs={{0,4},{1,5},{2,6},{3,7},{4,0},{5,1},{6,2},{7,3},{8,12},{9,13},{10,... | collective-permute-start | bytes 98312 | tf_op jit(solution)/shard_map/ppermute | solution.py:288
  71.9 11.6 %collective-permute-start.30 = (bf16[4,32,256]{2,1,0:T(8,128)(2,1)S(1)}, bf16[4,32,256]{2,1,0:T(8,128)(2,1)S(1)}, u32[]{:S(2)}, u32[]{:S(2)}) collective-permute-start(bf16[4,32,256]{2,1,0:T(8,128)(2,1)S(1)} %get-tuple-element.97), channel_id=1, source_target_pairs={{0,7},{1,15},{2,23},{3,31},{4,3},{5,11},{6,19},{7,27},{8,6},{9,14}... | collective-permute-start | bytes 196616 | tf_op jit(solution)/shard_map/ppermute | solution.py:364
  78.0 3.9 %collective-permute-start.27 = (bf16[32,256]{1,0:T(8,128)(2,1)S(1)}, bf16[32,256]{1,0:T(8,128)(2,1)S(1)}, u32[]{:S(2)}, u32[]{:S(2)}) collective-permute-start(bf16[32,256]{1,0:T(8,128)(2,1)S(1)} %get-tuple-element.96), channel_id=1, source_target_pairs={{0,5},{1,4},{2,7},{3,6},{4,1},{5,0},{6,3},{7,2},{8,13},{9,12},{10,... | collective-permute-start | bytes 49160 | tf_op jit(solution)/shard_map/ppermute | solution.py:367
  78.0 4.1 %collective-permute-start.28 = (bf16[32,256]{1,0:T(8,128)(2,1)S(1)}, bf16[32,256]{1,0:T(8,128)(2,1)S(1)}, u32[]{:S(2)}, u32[]{:S(2)}) collective-permute-start(bf16[32,256]{1,0:T(8,128)(2,1)S(1)} %get-tuple-element.96), channel_id=1, source_target_pairs={{0,6},{1,7},{2,4},{3,5},{4,2},{5,3},{6,0},{7,1},{8,14},{9,15},{10,... | collective-permute-start | bytes 49160 | tf_op jit(solution)/shard_map/ppermute | solution.py:367
  78.4 5.1 %collective-permute-start.29 = (bf16[32,256]{1,0:T(8,128)(2,1)S(1)}, bf16[32,256]{1,0:T(8,128)(2,1)S(1)}, u32[]{:S(2)}, u32[]{:S(2)}) collective-permute-start(bf16[32,256]{1,0:T(8,128)(2,1)S(1)} %get-tuple-element.96), channel_id=1, source_target_pairs={{0,7},{1,6},{2,5},{3,4},{4,3},{5,2},{6,1},{7,0},{8,15},{9,14},{10,... | collective-permute-start | bytes 49160 | tf_op jit(solution)/shard_map/ppermute | solution.py:367
  (3 other events, 7.8 us)
